TPU v7x, 128 devices: a whole 4x4x4 slice. The times are simulated.
128 devices in a mesh: row: 8 (over z_lo, x), col: 16 (over y, z_hi, core).
Axes of the slice: x: 4, y: 4, z: 4 (z_hi: 2, z_lo: 2; z = z_hi * 2 + z_lo), core: 2. Of those that a mesh axis runs over, the one named last changes fastest.
Arguments:
- a_tiles: bfloat16 [2176, 128, 128], P(('row', 'col')), may hold values from -0.375 to 0.375
- a_index: int32 [2176, 2], P(('row', 'col')), may hold values from 0 to 63, as said below
- b_tiles: bfloat16 [1280, 128, 128], P(('row', 'col')), may hold values from -6 to 6
- b_index: int32 [1280, 2], P(('row', 'col')), may hold values from 0 to 95, as said below
- row_dist: int32 [64], replicated, may hold values from 0 to 7, as said below
- col_dist: int32 [96], replicated, may hold values from 0 to 15, as said below
- c_index: int32 [3072, 2], P(('row', 'col')), may hold values from 0 to 95, as said below
Outputs:
- c_grid: bfloat16 [64, 96, 128, 128], P('row', 'col')
Inputs may be any that keep to these rules, and one draw needn't show every extreme that they name: `a_index`: distinct tiles. Every tile stored on a device of grid row p has row_dist = p. Contraction block k belongs to image k mod 16; a tile's destination column is (image - p) mod 16. One device sends at most 2 tiles to any destination column; in every grid row one destination column receives exactly 2 from every device of the row, and every other destination column exactly one from every device. `b_index`: distinct tiles. Every tile stored on a device of grid column q has col_dist = q. A tile of image s has destination row (s - q) mod 8. One device sends at most 3 tiles to any destination row; in every grid column one destination row receives exactly 3 from every device of the column, and every other destination row exactly one from every device. `row_dist`: every grid row holds exactly 8 window block rows. `col_dist`: every grid column holds exactly 6 window block columns. `c_index`: each device holds 24 distinct pairs, all with row_dist equal to its grid row and col_dist equal to its grid column.
All inputs are finite; a program needn't handle non-finite values.
Results may differ from a plain program's by a relative error of at most 0.001.
Values may be sent and summed in bfloat16 or wider, within the bound.
No kernel may reach another device: no remote copies, remote signals or barrier semaphores. Data moves between devices by JAX's collectives and lax.ppermute only.
A program may use at most 128 MiB of HBM per device.

v0:
```python
import jax
import jax.numpy as jnp
from jax import lax
from jax.sharding import PartitionSpec as P

RL = 8
CL = 6
KPI = 4
CAP_A = 2
CAP_B = 3


def passed_along(block, axis, distance):
    devices = range(lax.axis_size(axis))
    route = [((i - distance) % len(devices), i) for i in devices]
    return lax.ppermute(block, axis, route)


def group_rank(labels):
    positions = jnp.arange(labels.shape[0])
    earlier_same = (labels[:, None] == labels[None, :]) & (positions[None, :] < positions[:, None])
    return jnp.sum(earlier_same, axis=1)


def pack_slots(pieces, labels, target, targets, capacity):
    within = group_rank(target)
    slot_of = target * capacity + within
    chosen = jnp.arange(targets * capacity)[:, None] == slot_of[None, :]
    packed = jnp.einsum(
        "sn,nxy->sxy", chosen.astype(jnp.bfloat16), pieces, preferred_element_type=jnp.float32
    )
    marked = jnp.sum(chosen[:, :, None].astype(jnp.int32) * (labels[None, :, :] + 1), axis=1) - 1
    return (packed.astype(jnp.bfloat16), marked)


def densify_left(left_tiles, left_labels, row_place, col_count):
    present = left_labels[:, 0] >= 0
    block_row = jnp.maximum(left_labels[:, 0], 0)
    block_k = jnp.maximum(left_labels[:, 1], 0)
    position = jnp.where(present, row_place[block_row] * KPI + block_k // col_count, -1)
    chosen = (jnp.arange(RL * KPI)[:, None] == position[None, :]).astype(jnp.bfloat16)
    filled = jnp.einsum("ns,sxy->nxy", chosen, left_tiles, preferred_element_type=jnp.float32)
    return filled.astype(jnp.bfloat16).reshape(RL, KPI, left_tiles.shape[1], left_tiles.shape[2])


def densify_right(right_tiles, right_labels, col_place, image_now, col_count):
    block_k = jnp.maximum(right_labels[:, 0], 0)
    block_col = jnp.maximum(right_labels[:, 1], 0)
    wanted = (right_labels[:, 0] >= 0) & (block_k % col_count == image_now)
    position = jnp.where(wanted, block_k // col_count * CL + col_place[block_col], -1)
    chosen = (jnp.arange(KPI * CL)[:, None] == position[None, :]).astype(jnp.bfloat16)
    filled = jnp.einsum("ns,sxy->nxy", chosen, right_tiles, preferred_element_type=jnp.float32)
    return filled.astype(jnp.bfloat16).reshape(KPI, CL, right_tiles.shape[1], right_tiles.shape[2])


def block_product(left_dense, right_dense):
    return jnp.einsum(
        "lkxy,kcyz->lcxz", left_dense, right_dense, preferred_element_type=jnp.float32
    )


def per_device(a_tiles, a_index, b_tiles, b_index, row_dist, col_dist, c_index):
    row_count = lax.axis_size("row")
    col_count = lax.axis_size("col")
    grid_row = lax.axis_index("row")
    grid_col = lax.axis_index("col")
    row_place = group_rank(row_dist)
    col_place = group_rank(col_dist)
    start_image = (grid_row + grid_col) % col_count
    left_target = (a_index[:, 1] % col_count - grid_row) % col_count
    right_target = (b_index[:, 0] % col_count - grid_col) % row_count

    def contribution(some_left, some_left_labels, some_right, some_right_labels, image_now):
        left_dense = densify_left(some_left, some_left_labels, row_place, col_count)
        right_dense = densify_right(some_right, some_right_labels, col_place, image_now, col_count)
        return block_product(left_dense, right_dense)

    left_tiles, left_labels = pack_slots(a_tiles, a_index, left_target, col_count, CAP_A)
    left_tiles, left_labels = (
        lax.all_to_all(left_tiles, "col", split_axis=0, concat_axis=0, tiled=True),
        lax.all_to_all(left_labels, "col", split_axis=0, concat_axis=0, tiled=True),
    )
    right_tiles, right_labels = pack_slots(b_tiles, b_index, right_target, row_count, CAP_B)
    right_tiles, right_labels = (
        lax.all_to_all(right_tiles, "row", split_axis=0, concat_axis=0, tiled=True),
        lax.all_to_all(right_labels, "row", split_axis=0, concat_axis=0, tiled=True),
    )
    accumulated = contribution(left_tiles, left_labels, right_tiles, right_labels, start_image)

    def advance(step_index, carry):
        running, near_tiles, near_labels, moving_tiles, moving_labels = carry
        near_tiles, near_labels = passed_along((near_tiles, near_labels), "col", -1)
        moving_tiles, moving_labels = passed_along((moving_tiles, moving_labels), "row", -1)
        image_now = (start_image + step_index) % col_count
        running = running + contribution(
            near_tiles, near_labels, moving_tiles, moving_labels, image_now
        )
        return (running, near_tiles, near_labels, moving_tiles, moving_labels)

    accumulated = lax.fori_loop(
        1, col_count, advance, (accumulated, left_tiles, left_labels, right_tiles, right_labels)
    )[0]
    pattern_row = row_place[c_index[:, 0]]
    pattern_col = col_place[c_index[:, 1]]
    matches = (jnp.arange(RL)[:, None, None] == pattern_row[None, None, :]) & (
        jnp.arange(CL)[None, :, None] == pattern_col[None, None, :]
    )
    in_pattern = jnp.any(matches, axis=2)
    return jnp.where(in_pattern[:, :, None, None], accumulated, 0.0).astype(jnp.bfloat16)


def solution(mesh):
    in_specs = (
        P(("row", "col"), None, None),
        P(("row", "col"), None),
        P(("row", "col"), None, None),
        P(("row", "col"), None),
        P(),
        P(),
        P(("row", "col"), None),
    )
    out_specs = P("row", "col", None, None)
    return jax.shard_map(
        per_device, mesh=mesh, in_specs=in_specs, out_specs=out_specs, check_vma=False
    )
```

profile of v0, /device:TPU:1, one launch (start us, length us, event | category | flops | bytes accessed | tf_op | source)
XLA Modules:
  0.0 627.1 jit_solution(5659254571438317061)
XLA Ops:
  4.0 6.2 all-to-all-start
  17.9 8.5 %all-to-all-start.2 = ((s32[16,2,2]{1,2,0:T(2,128)}), s32[16,2,2]{1,2,0:T(2,128)S(1)}, u32[]{:S(2)}, u32[]{:S(2)}) async-start(s32[16,2,2]{1,2,0:T(2,128)} %copy.67), calls=%async_computation.2 | async-start | bytes 32768 | tf_op jit(solution)/shard_map/all_to_all | solution.py:81
  27.5 6.2 all-to-all-done.2
  41.9 9.7 %all-to-all-done.1 = bf16[24,128,128]{2,1,0:T(8,128)(2,1)S(1)} async-done(((bf16[24,128,128]{2,1,0:T(8,128)(2,1)}), bf16[24,128,128]{2,1,0:T(8,128)(2,1)S(1)}, u32[]{:S(2)}, u32[]{:S(2)}) %all-to-all-start.1) | async-done | bytes 786464 | tf_op jit(solution)/shard_map/all_to_all | solution.py:85
  58.9 14.2 %all-to-all-done.3 = bf16[32,128,128]{2,1,0:T(8,128)(2,1)S(1)} async-done(((bf16[32,128,128]{2,1,0:T(8,128)(2,1)}), bf16[32,128,128]{2,1,0:T(8,128)(2,1)S(1)}, u32[]{:S(2)}, u32[]{:S(2)}) %all-to-all-start.3) | async-done | bytes 1048608 | tf_op jit(solution)/shard_map/all_to_all | solution.py:80
  77.3 546.0 %while.24 = (s32[]{:T(128)}, f32[8,6,128,128]{2,3,0,1:T(8,128)}, bf16[32,128,128]{2,0,1:T(8,128)(2,1)S(1)}, s32[32,2]{0,1:T(2,128)S(1)}, bf16[24,128,128]{2,0,1:...) while((s32[]{:T(128)}, f32[8,6,128,128]{2,3,0,1:T(8,128)}, ...), condition=%wide.region_8.9_spmd, body=%wide.region_7.8_spmd.sunk | while | flops 859443712 | bytes 49558924 | solution.py:100
  83.9 18.9 %collective-permute-done.2 = bf16[24,128,128]{2,0,1:T(8,128)(2,1)S(1)} collective-permute-done((bf16[24,128,128]{2,0,1:T(8,128)(2,1)}, bf16[24,128,128]{2,0,1:T(8,128)(2,1)S(1)}, u32[]{:S(2)}, u32[]{:S(2)}) %collective-permute-start.2) | collective-permute-done | bytes 786464 | tf_op jit(solution)/shard_map/while/body/eval_jaxpr/ppermute | solution.py:16
  108.3 6.8 %collective-permute-start.3 = (s32[24,2]{0,1:T(2,128)S(1)}, s32[24,2]{0,1:T(2,128)S(1)}, u32[]{:S(2)}, u32[]{:S(2)}) collective-permute-start(s32[24,2]{0,1:T(2,128)S(1)} %get-tuple-element.372), channel_id=1, source_target_pairs={{16,0},{32,16},{48,32},{64,48},{80,64},{96,80},{112,96},{0,112},{1... | collective-permute-start | bytes 584 | tf_op jit(solution)/shard_map/while/body/eval_jaxpr/ppermute | solution.py:16
  120.4 18.0 %collective-permute-done.2 = bf16[24,128,128]{2,0,1:T(8,128)(2,1)S(1)} collective-permute-done((bf16[24,128,128]{2,0,1:T(8,128)(2,1)}, bf16[24,128,128]{2,0,1:T(8,128)(2,1)S(1)}, u32[]{:S(2)}, u32[]{:S(2)}) %collective-permute-start.2) | collective-permute-done | bytes 786464 | tf_op jit(solution)/shard_map/while/body/eval_jaxpr/ppermute | solution.py:16
  144.0 8.4 %collective-permute-start.3 = (s32[24,2]{0,1:T(2,128)S(1)}, s32[24,2]{0,1:T(2,128)S(1)}, u32[]{:S(2)}, u32[]{:S(2)}) collective-permute-start(s32[24,2]{0,1:T(2,128)S(1)} %get-tuple-element.372), channel_id=1, source_target_pairs={{16,0},{32,16},{48,32},{64,48},{80,64},{96,80},{112,96},{0,112},{1... | collective-permute-start | bytes 584 | tf_op jit(solution)/shard_map/while/body/eval_jaxpr/ppermute | solution.py:16
  157.7 19.2 %collective-permute-done.2 = bf16[24,128,128]{2,0,1:T(8,128)(2,1)S(1)} collective-permute-done((bf16[24,128,128]{2,0,1:T(8,128)(2,1)}, bf16[24,128,128]{2,0,1:T(8,128)(2,1)S(1)}, u32[]{:S(2)}, u32[]{:S(2)}) %collective-permute-start.2) | collective-permute-done | bytes 786464 | tf_op jit(solution)/shard_map/while/body/eval_jaxpr/ppermute | solution.py:16
  182.5 6.1 collective-permute-start.3
  193.9 15.8 %collective-permute-done.2 = bf16[24,128,128]{2,0,1:T(8,128)(2,1)S(1)} collective-permute-done((bf16[24,128,128]{2,0,1:T(8,128)(2,1)}, bf16[24,128,128]{2,0,1:T(8,128)(2,1)S(1)}, u32[]{:S(2)}, u32[]{:S(2)}) %collective-permute-start.2) | collective-permute-done | bytes 786464 | tf_op jit(solution)/shard_map/while/body/eval_jaxpr/ppermute | solution.py:16
  215.3 10.6 %collective-permute-start.3 = (s32[24,2]{0,1:T(2,128)S(1)}, s32[24,2]{0,1:T(2,128)S(1)}, u32[]{:S(2)}, u32[]{:S(2)}) collective-permute-start(s32[24,2]{0,1:T(2,128)S(1)} %get-tuple-element.372), channel_id=1, source_target_pairs={{16,0},{32,16},{48,32},{64,48},{80,64},{96,80},{112,96},{0,112},{1... | collective-permute-start | bytes 584 | tf_op jit(solution)/shard_map/while/body/eval_jaxpr/ppermute | solution.py:16
  231.2 19.5 %collective-permute-done.2 = bf16[24,128,128]{2,0,1:T(8,128)(2,1)S(1)} collective-permute-done((bf16[24,128,128]{2,0,1:T(8,128)(2,1)}, bf16[24,128,128]{2,0,1:T(8,128)(2,1)S(1)}, u32[]{:S(2)}, u32[]{:S(2)}) %collective-permute-start.2) | collective-permute-done | bytes 786464 | tf_op jit(solution)/shard_map/while/body/eval_jaxpr/ppermute | solution.py:16
  267.4 15.9 %collective-permute-done.2 = bf16[24,128,128]{2,0,1:T(8,128)(2,1)S(1)} collective-permute-done((bf16[24,128,128]{2,0,1:T(8,128)(2,1)}, bf16[24,128,128]{2,0,1:T(8,128)(2,1)S(1)}, u32[]{:S(2)}, u32[]{:S(2)}) %collective-permute-start.2) | collective-permute-done | bytes 786464 | tf_op jit(solution)/shard_map/while/body/eval_jaxpr/ppermute | solution.py:16
  288.9 10.5 %collective-permute-start.3 = (s32[24,2]{0,1:T(2,128)S(1)}, s32[24,2]{0,1:T(2,128)S(1)}, u32[]{:S(2)}, u32[]{:S(2)}) collective-permute-start(s32[24,2]{0,1:T(2,128)S(1)} %get-tuple-element.372), channel_id=1, source_target_pairs={{16,0},{32,16},{48,32},{64,48},{80,64},{96,80},{112,96},{0,112},{1... | collective-permute-start | bytes 584 | tf_op jit(solution)/shard_map/while/body/eval_jaxpr/ppermute | solution.py:16
  304.7 19.4 %collective-permute-done.2 = bf16[24,128,128]{2,0,1:T(8,128)(2,1)S(1)} collective-permute-done((bf16[24,128,128]{2,0,1:T(8,128)(2,1)}, bf16[24,128,128]{2,0,1:T(8,128)(2,1)S(1)}, u32[]{:S(2)}, u32[]{:S(2)}) %collective-permute-start.2) | collective-permute-done | bytes 786464 | tf_op jit(solution)/shard_map/while/body/eval_jaxpr/ppermute | solution.py:16
  341.0 15.9 %collective-permute-done.2 = bf16[24,128,128]{2,0,1:T(8,128)(2,1)S(1)} collective-permute-done((bf16[24,128,128]{2,0,1:T(8,128)(2,1)}, bf16[24,128,128]{2,0,1:T(8,128)(2,1)S(1)}, u32[]{:S(2)}, u32[]{:S(2)}) %collective-permute-start.2) | collective-permute-done | bytes 786464 | tf_op jit(solution)/shard_map/while/body/eval_jaxpr/ppermute | solution.py:16
  362.5 10.4 %collective-permute-start.3 = (s32[24,2]{0,1:T(2,128)S(1)}, s32[24,2]{0,1:T(2,128)S(1)}, u32[]{:S(2)}, u32[]{:S(2)}) collective-permute-start(s32[24,2]{0,1:T(2,128)S(1)} %get-tuple-element.372), channel_id=1, source_target_pairs={{16,0},{32,16},{48,32},{64,48},{80,64},{96,80},{112,96},{0,112},{1... | collective-permute-start | bytes 584 | tf_op jit(solution)/shard_map/while/body/eval_jaxpr/ppermute | solution.py:16
  378.2 19.3 %collective-permute-done.2 = bf16[24,128,128]{2,0,1:T(8,128)(2,1)S(1)} collective-permute-done((bf16[24,128,128]{2,0,1:T(8,128)(2,1)}, bf16[24,128,128]{2,0,1:T(8,128)(2,1)S(1)}, u32[]{:S(2)}, u32[]{:S(2)}) %collective-permute-start.2) | collective-permute-done | bytes 786464 | tf_op jit(solution)/shard_map/while/body/eval_jaxpr/ppermute | solution.py:16
  414.5 16.0 %collective-permute-done.2 = bf16[24,128,128]{2,0,1:T(8,128)(2,1)S(1)} collective-permute-done((bf16[24,128,128]{2,0,1:T(8,128)(2,1)}, bf16[24,128,128]{2,0,1:T(8,128)(2,1)S(1)}, u32[]{:S(2)}, u32[]{:S(2)}) %collective-permute-start.2) | collective-permute-done | bytes 786464 | tf_op jit(solution)/shard_map/while/body/eval_jaxpr/ppermute | solution.py:16
  436.1 10.3 %collective-permute-start.3 = (s32[24,2]{0,1:T(2,128)S(1)}, s32[24,2]{0,1:T(2,128)S(1)}, u32[]{:S(2)}, u32[]{:S(2)}) collective-permute-start(s32[24,2]{0,1:T(2,128)S(1)} %get-tuple-element.372), channel_id=1, source_target_pairs={{16,0},{32,16},{48,32},{64,48},{80,64},{96,80},{112,96},{0,112},{1... | collective-permute-start | bytes 584 | tf_op jit(solution)/shard_map/while/body/eval_jaxpr/ppermute | solution.py:16
  451.7 19.2 %collective-permute-done.2 = bf16[24,128,128]{2,0,1:T(8,128)(2,1)S(1)} collective-permute-done((bf16[24,128,128]{2,0,1:T(8,128)(2,1)}, bf16[24,128,128]{2,0,1:T(8,128)(2,1)S(1)}, u32[]{:S(2)}, u32[]{:S(2)}) %collective-permute-start.2) | collective-permute-done | bytes 786464 | tf_op jit(solution)/shard_map/while/body/eval_jaxpr/ppermute | solution.py:16
  476.5 6.2 collective-permute-start.3
  488.0 16.1 %collective-permute-done.2 = bf16[24,128,128]{2,0,1:T(8,128)(2,1)S(1)} collective-permute-done((bf16[24,128,128]{2,0,1:T(8,128)(2,1)}, bf16[24,128,128]{2,0,1:T(8,128)(2,1)S(1)}, u32[]{:S(2)}, u32[]{:S(2)}) %collective-permute-start.2) | collective-permute-done | bytes 786464 | tf_op jit(solution)/shard_map/while/body/eval_jaxpr/ppermute | solution.py:16
  509.7 10.2 %collective-permute-start.3 = (s32[24,2]{0,1:T(2,128)S(1)}, s32[24,2]{0,1:T(2,128)S(1)}, u32[]{:S(2)}, u32[]{:S(2)}) collective-permute-start(s32[24,2]{0,1:T(2,128)S(1)} %get-tuple-element.372), channel_id=1, source_target_pairs={{16,0},{32,16},{48,32},{64,48},{80,64},{96,80},{112,96},{0,112},{1... | collective-permute-start | bytes 584 | tf_op jit(solution)/shard_map/while/body/eval_jaxpr/ppermute | solution.py:16
  525.2 19.1 %collective-permute-done.2 = bf16[24,128,128]{2,0,1:T(8,128)(2,1)S(1)} collective-permute-done((bf16[24,128,128]{2,0,1:T(8,128)(2,1)}, bf16[24,128,128]{2,0,1:T(8,128)(2,1)S(1)}, u32[]{:S(2)}, u32[]{:S(2)}) %collective-permute-start.2) | collective-permute-done | bytes 786464 | tf_op jit(solution)/shard_map/while/body/eval_jaxpr/ppermute | solution.py:16
  549.9 6.4 %collective-permute-start.3 = (s32[24,2]{0,1:T(2,128)S(1)}, s32[24,2]{0,1:T(2,128)S(1)}, u32[]{:S(2)}, u32[]{:S(2)}) collective-permute-start(s32[24,2]{0,1:T(2,128)S(1)} %get-tuple-element.372), channel_id=1, source_target_pairs={{16,0},{32,16},{48,32},{64,48},{80,64},{96,80},{112,96},{0,112},{1... | collective-permute-start | bytes 584 | tf_op jit(solution)/shard_map/while/body/eval_jaxpr/ppermute | solution.py:16
  561.5 16.2 %collective-permute-done.2 = bf16[24,128,128]{2,0,1:T(8,128)(2,1)S(1)} collective-permute-done((bf16[24,128,128]{2,0,1:T(8,128)(2,1)}, bf16[24,128,128]{2,0,1:T(8,128)(2,1)S(1)}, u32[]{:S(2)}, u32[]{:S(2)}) %collective-permute-start.2) | collective-permute-done | bytes 786464 | tf_op jit(solution)/shard_map/while/body/eval_jaxpr/ppermute | solution.py:16
  583.3 10.1 %collective-permute-start.3 = (s32[24,2]{0,1:T(2,128)S(1)}, s32[24,2]{0,1:T(2,128)S(1)}, u32[]{:S(2)}, u32[]{:S(2)}) collective-permute-start(s32[24,2]{0,1:T(2,128)S(1)} %get-tuple-element.372), channel_id=1, source_target_pairs={{16,0},{32,16},{48,32},{64,48},{80,64},{96,80},{112,96},{0,112},{1... | collective-permute-start | bytes 584 | tf_op jit(solution)/shard_map/while/body/eval_jaxpr/ppermute | solution.py:16
  598.7 19.0 %collective-permute-done.2 = bf16[24,128,128]{2,0,1:T(8,128)(2,1)S(1)} collective-permute-done((bf16[24,128,128]{2,0,1:T(8,128)(2,1)}, bf16[24,128,128]{2,0,1:T(8,128)(2,1)S(1)}, u32[]{:S(2)}, u32[]{:S(2)}) %collective-permute-start.2) | collective-permute-done | bytes 786464 | tf_op jit(solution)/shard_map/while/body/eval_jaxpr/ppermute | solution.py:16
  (459 shorter events, 217.2 us)
Async XLA Ops:
  33.7 17.9 %all-to-all-start.1 = ((bf16[24,128,128]{2,1,0:T(8,128)(2,1)}), bf16[24,128,128]{2,1,0:T(8,128)(2,1)S(1)}, u32[]{:S(2)}, u32[]{:S(2)}) async-start(bf16[24,128,128]{2,1,0:T(8,128)(2,1)} %copy.63), calls=%async_computation.1 | async-start | bytes 1572864 | tf_op jit(solution)/shard_map/all_to_all | solution.py:85
  51.6 21.5 %all-to-all-start.3 = ((bf16[32,128,128]{2,1,0:T(8,128)(2,1)}), bf16[32,128,128]{2,1,0:T(8,128)(2,1)S(1)}, u32[]{:S(2)}, u32[]{:S(2)}) async-start(bf16[32,128,128]{2,1,0:T(8,128)(2,1)} %copy.70), calls=%async_computation.3 | async-start | bytes 2097152 | tf_op jit(solution)/shard_map/all_to_all | solution.py:80
  78.5 24.2 %collective-permute-start.2 = (bf16[24,128,128]{2,0,1:T(8,128)(2,1)}, bf16[24,128,128]{2,0,1:T(8,128)(2,1)S(1)}, u32[]{:S(2)}, u32[]{:S(2)}) collective-permute-start(bf16[24,128,128]{2,0,1:T(8,128)(2,1)} %get-tuple-element.371), channel_id=1, source_target_pairs={{16,0},{32,16},{48,32},{64,48},{80,64},{96,80},{112,96},{0,112},{1... | collective-permute-start | bytes 2359304 | tf_op jit(solution)/shard_map/while/body/eval_jaxpr/ppermute | solution.py:16
  79.8 24.4 %collective-permute-start = (bf16[32,128,128]{2,0,1:T(8,128)(2,1)S(1)}, bf16[32,128,128]{2,0,1:T(8,128)(2,1)S(1)}, u32[]{:S(2)}, u32[]{:S(2)}) collective-permute-start(bf16[32,128,128]{2,0,1:T(8,128)(2,1)S(1)} %get-tuple-element.369), channel_id=1, source_target_pairs={{1,0},{2,1},{3,2},{4,3},{5,4},{6,5},{7,6},{8,7},{9,8},{10,9},{11,1... | collective-permute-start | bytes 3145736 | tf_op jit(solution)/shard_map/while/body/eval_jaxpr/ppermute | solution.py:16
  115.1 23.3 %collective-permute-start.2 = (bf16[24,128,128]{2,0,1:T(8,128)(2,1)}, bf16[24,128,128]{2,0,1:T(8,128)(2,1)S(1)}, u32[]{:S(2)}, u32[]{:S(2)}) collective-permute-start(bf16[24,128,128]{2,0,1:T(8,128)(2,1)} %get-tuple-element.371), channel_id=1, source_target_pairs={{16,0},{32,16},{48,32},{64,48},{80,64},{96,80},{112,96},{0,112},{1... | collective-permute-start | bytes 2359304 | tf_op jit(solution)/shard_map/while/body/eval_jaxpr/ppermute | solution.py:16
  117.0 22.8 %collective-permute-start = (bf16[32,128,128]{2,0,1:T(8,128)(2,1)S(1)}, bf16[32,128,128]{2,0,1:T(8,128)(2,1)S(1)}, u32[]{:S(2)}, u32[]{:S(2)}) collective-permute-start(bf16[32,128,128]{2,0,1:T(8,128)(2,1)S(1)} %get-tuple-element.369), channel_id=1, source_target_pairs={{1,0},{2,1},{3,2},{4,3},{5,4},{6,5},{7,6},{8,7},{9,8},{10,9},{11,1... | collective-permute-start | bytes 3145736 | tf_op jit(solution)/shard_map/while/body/eval_jaxpr/ppermute | solution.py:16
  152.4 24.5 %collective-permute-start.2 = (bf16[24,128,128]{2,0,1:T(8,128)(2,1)}, bf16[24,128,128]{2,0,1:T(8,128)(2,1)S(1)}, u32[]{:S(2)}, u32[]{:S(2)}) collective-permute-start(bf16[24,128,128]{2,0,1:T(8,128)(2,1)} %get-tuple-element.371), channel_id=1, source_target_pairs={{16,0},{32,16},{48,32},{64,48},{80,64},{96,80},{112,96},{0,112},{1... | collective-permute-start | bytes 2359304 | tf_op jit(solution)/shard_map/while/body/eval_jaxpr/ppermute | solution.py:16
  154.0 24.3 %collective-permute-start = (bf16[32,128,128]{2,0,1:T(8,128)(2,1)S(1)}, bf16[32,128,128]{2,0,1:T(8,128)(2,1)S(1)}, u32[]{:S(2)}, u32[]{:S(2)}) collective-permute-start(bf16[32,128,128]{2,0,1:T(8,128)(2,1)S(1)} %get-tuple-element.369), channel_id=1, source_target_pairs={{1,0},{2,1},{3,2},{4,3},{5,4},{6,5},{7,6},{8,7},{9,8},{10,9},{11,1... | collective-permute-start | bytes 3145736 | tf_op jit(solution)/shard_map/while/body/eval_jaxpr/ppermute | solution.py:16
  188.6 21.0 %collective-permute-start.2 = (bf16[24,128,128]{2,0,1:T(8,128)(2,1)}, bf16[24,128,128]{2,0,1:T(8,128)(2,1)S(1)}, u32[]{:S(2)}, u32[]{:S(2)}) collective-permute-start(bf16[24,128,128]{2,0,1:T(8,128)(2,1)} %get-tuple-element.371), channel_id=1, source_target_pairs={{16,0},{32,16},{48,32},{64,48},{80,64},{96,80},{112,96},{0,112},{1... | collective-permute-start | bytes 2359304 | tf_op jit(solution)/shard_map/while/body/eval_jaxpr/ppermute | solution.py:16
  191.8 19.3 %collective-permute-start = (bf16[32,128,128]{2,0,1:T(8,128)(2,1)S(1)}, bf16[32,128,128]{2,0,1:T(8,128)(2,1)S(1)}, u32[]{:S(2)}, u32[]{:S(2)}) collective-permute-start(bf16[32,128,128]{2,0,1:T(8,128)(2,1)S(1)} %get-tuple-element.369), channel_id=1, source_target_pairs={{1,0},{2,1},{3,2},{4,3},{5,4},{6,5},{7,6},{8,7},{9,8},{10,9},{11,1... | collective-permute-start | bytes 3145736 | tf_op jit(solution)/shard_map/while/body/eval_jaxpr/ppermute | solution.py:16
  225.9 24.8 %collective-permute-start.2 = (bf16[24,128,128]{2,0,1:T(8,128)(2,1)}, bf16[24,128,128]{2,0,1:T(8,128)(2,1)S(1)}, u32[]{:S(2)}, u32[]{:S(2)}) collective-permute-start(bf16[24,128,128]{2,0,1:T(8,128)(2,1)} %get-tuple-element.371), channel_id=1, source_target_pairs={{16,0},{32,16},{48,32},{64,48},{80,64},{96,80},{112,96},{0,112},{1... | collective-permute-start | bytes 2359304 | tf_op jit(solution)/shard_map/while/body/eval_jaxpr/ppermute | solution.py:16
  227.3 24.8 %collective-permute-start = (bf16[32,128,128]{2,0,1:T(8,128)(2,1)S(1)}, bf16[32,128,128]{2,0,1:T(8,128)(2,1)S(1)}, u32[]{:S(2)}, u32[]{:S(2)}) collective-permute-start(bf16[32,128,128]{2,0,1:T(8,128)(2,1)S(1)} %get-tuple-element.369), channel_id=1, source_target_pairs={{1,0},{2,1},{3,2},{4,3},{5,4},{6,5},{7,6},{8,7},{9,8},{10,9},{11,1... | collective-permute-start | bytes 3145736 | tf_op jit(solution)/shard_map/while/body/eval_jaxpr/ppermute | solution.py:16
  262.2 21.1 %collective-permute-start.2 = (bf16[24,128,128]{2,0,1:T(8,128)(2,1)}, bf16[24,128,128]{2,0,1:T(8,128)(2,1)S(1)}, u32[]{:S(2)}, u32[]{:S(2)}) collective-permute-start(bf16[24,128,128]{2,0,1:T(8,128)(2,1)} %get-tuple-element.371), channel_id=1, source_target_pairs={{16,0},{32,16},{48,32},{64,48},{80,64},{96,80},{112,96},{0,112},{1... | collective-permute-start | bytes 2359304 | tf_op jit(solution)/shard_map/while/body/eval_jaxpr/ppermute | solution.py:16
  265.3 19.4 %collective-permute-start = (bf16[32,128,128]{2,0,1:T(8,128)(2,1)S(1)}, bf16[32,128,128]{2,0,1:T(8,128)(2,1)S(1)}, u32[]{:S(2)}, u32[]{:S(2)}) collective-permute-start(bf16[32,128,128]{2,0,1:T(8,128)(2,1)S(1)} %get-tuple-element.369), channel_id=1, source_target_pairs={{1,0},{2,1},{3,2},{4,3},{5,4},{6,5},{7,6},{8,7},{9,8},{10,9},{11,1... | collective-permute-start | bytes 3145736 | tf_op jit(solution)/shard_map/while/body/eval_jaxpr/ppermute | solution.py:16
  299.4 24.6 %collective-permute-start.2 = (bf16[24,128,128]{2,0,1:T(8,128)(2,1)}, bf16[24,128,128]{2,0,1:T(8,128)(2,1)S(1)}, u32[]{:S(2)}, u32[]{:S(2)}) collective-permute-start(bf16[24,128,128]{2,0,1:T(8,128)(2,1)} %get-tuple-element.371), channel_id=1, source_target_pairs={{16,0},{32,16},{48,32},{64,48},{80,64},{96,80},{112,96},{0,112},{1... | collective-permute-start | bytes 2359304 | tf_op jit(solution)/shard_map/while/body/eval_jaxpr/ppermute | solution.py:16
  300.8 24.7 %collective-permute-start = (bf16[32,128,128]{2,0,1:T(8,128)(2,1)S(1)}, bf16[32,128,128]{2,0,1:T(8,128)(2,1)S(1)}, u32[]{:S(2)}, u32[]{:S(2)}) collective-permute-start(bf16[32,128,128]{2,0,1:T(8,128)(2,1)S(1)} %get-tuple-element.369), channel_id=1, source_target_pairs={{1,0},{2,1},{3,2},{4,3},{5,4},{6,5},{7,6},{8,7},{9,8},{10,9},{11,1... | collective-permute-start | bytes 3145736 | tf_op jit(solution)/shard_map/while/body/eval_jaxpr/ppermute | solution.py:16
  335.7 21.2 %collective-permute-start.2 = (bf16[24,128,128]{2,0,1:T(8,128)(2,1)}, bf16[24,128,128]{2,0,1:T(8,128)(2,1)S(1)}, u32[]{:S(2)}, u32[]{:S(2)}) collective-permute-start(bf16[24,128,128]{2,0,1:T(8,128)(2,1)} %get-tuple-element.371), channel_id=1, source_target_pairs={{16,0},{32,16},{48,32},{64,48},{80,64},{96,80},{112,96},{0,112},{1... | collective-permute-start | bytes 2359304 | tf_op jit(solution)/shard_map/while/body/eval_jaxpr/ppermute | solution.py:16
  338.8 19.5 %collective-permute-start = (bf16[32,128,128]{2,0,1:T(8,128)(2,1)S(1)}, bf16[32,128,128]{2,0,1:T(8,128)(2,1)S(1)}, u32[]{:S(2)}, u32[]{:S(2)}) collective-permute-start(bf16[32,128,128]{2,0,1:T(8,128)(2,1)S(1)} %get-tuple-element.369), channel_id=1, source_target_pairs={{1,0},{2,1},{3,2},{4,3},{5,4},{6,5},{7,6},{8,7},{9,8},{10,9},{11,1... | collective-permute-start | bytes 3145736 | tf_op jit(solution)/shard_map/while/body/eval_jaxpr/ppermute | solution.py:16
  372.9 24.5 %collective-permute-start.2 = (bf16[24,128,128]{2,0,1:T(8,128)(2,1)}, bf16[24,128,128]{2,0,1:T(8,128)(2,1)S(1)}, u32[]{:S(2)}, u32[]{:S(2)}) collective-permute-start(bf16[24,128,128]{2,0,1:T(8,128)(2,1)} %get-tuple-element.371), channel_id=1, source_target_pairs={{16,0},{32,16},{48,32},{64,48},{80,64},{96,80},{112,96},{0,112},{1... | collective-permute-start | bytes 2359304 | tf_op jit(solution)/shard_map/while/body/eval_jaxpr/ppermute | solution.py:16
  374.4 24.5 %collective-permute-start = (bf16[32,128,128]{2,0,1:T(8,128)(2,1)S(1)}, bf16[32,128,128]{2,0,1:T(8,128)(2,1)S(1)}, u32[]{:S(2)}, u32[]{:S(2)}) collective-permute-start(bf16[32,128,128]{2,0,1:T(8,128)(2,1)S(1)} %get-tuple-element.369), channel_id=1, source_target_pairs={{1,0},{2,1},{3,2},{4,3},{5,4},{6,5},{7,6},{8,7},{9,8},{10,9},{11,1... | collective-permute-start | bytes 3145736 | tf_op jit(solution)/shard_map/while/body/eval_jaxpr/ppermute | solution.py:16
  409.2 21.3 %collective-permute-start.2 = (bf16[24,128,128]{2,0,1:T(8,128)(2,1)}, bf16[24,128,128]{2,0,1:T(8,128)(2,1)S(1)}, u32[]{:S(2)}, u32[]{:S(2)}) collective-permute-start(bf16[24,128,128]{2,0,1:T(8,128)(2,1)} %get-tuple-element.371), channel_id=1, source_target_pairs={{16,0},{32,16},{48,32},{64,48},{80,64},{96,80},{112,96},{0,112},{1... | collective-permute-start | bytes 2359304 | tf_op jit(solution)/shard_map/while/body/eval_jaxpr/ppermute | solution.py:16
  412.2 19.6 %collective-permute-start = (bf16[32,128,128]{2,0,1:T(8,128)(2,1)S(1)}, bf16[32,128,128]{2,0,1:T(8,128)(2,1)S(1)}, u32[]{:S(2)}, u32[]{:S(2)}) collective-permute-start(bf16[32,128,128]{2,0,1:T(8,128)(2,1)S(1)} %get-tuple-element.369), channel_id=1, source_target_pairs={{1,0},{2,1},{3,2},{4,3},{5,4},{6,5},{7,6},{8,7},{9,8},{10,9},{11,1... | collective-permute-start | bytes 3145736 | tf_op jit(solution)/shard_map/while/body/eval_jaxpr/ppermute | solution.py:16
  446.4 24.5 %collective-permute-start.2 = (bf16[24,128,128]{2,0,1:T(8,128)(2,1)}, bf16[24,128,128]{2,0,1:T(8,128)(2,1)S(1)}, u32[]{:S(2)}, u32[]{:S(2)}) collective-permute-start(bf16[24,128,128]{2,0,1:T(8,128)(2,1)} %get-tuple-element.371), channel_id=1, source_target_pairs={{16,0},{32,16},{48,32},{64,48},{80,64},{96,80},{112,96},{0,112},{1... | collective-permute-start | bytes 2359304 | tf_op jit(solution)/shard_map/while/body/eval_jaxpr/ppermute | solution.py:16
  447.9 24.4 %collective-permute-start = (bf16[32,128,128]{2,0,1:T(8,128)(2,1)S(1)}, bf16[32,128,128]{2,0,1:T(8,128)(2,1)S(1)}, u32[]{:S(2)}, u32[]{:S(2)}) collective-permute-start(bf16[32,128,128]{2,0,1:T(8,128)(2,1)S(1)} %get-tuple-element.369), channel_id=1, source_target_pairs={{1,0},{2,1},{3,2},{4,3},{5,4},{6,5},{7,6},{8,7},{9,8},{10,9},{11,1... | collective-permute-start | bytes 3145736 | tf_op jit(solution)/shard_map/while/body/eval_jaxpr/ppermute | solution.py:16
  482.7 21.3 %collective-permute-start.2 = (bf16[24,128,128]{2,0,1:T(8,128)(2,1)}, bf16[24,128,128]{2,0,1:T(8,128)(2,1)S(1)}, u32[]{:S(2)}, u32[]{:S(2)}) collective-permute-start(bf16[24,128,128]{2,0,1:T(8,128)(2,1)} %get-tuple-element.371), channel_id=1, source_target_pairs={{16,0},{32,16},{48,32},{64,48},{80,64},{96,80},{112,96},{0,112},{1... | collective-permute-start | bytes 2359304 | tf_op jit(solution)/shard_map/while/body/eval_jaxpr/ppermute | solution.py:16
  485.7 19.8 %collective-permute-start = (bf16[32,128,128]{2,0,1:T(8,128)(2,1)S(1)}, bf16[32,128,128]{2,0,1:T(8,128)(2,1)S(1)}, u32[]{:S(2)}, u32[]{:S(2)}) collective-permute-start(bf16[32,128,128]{2,0,1:T(8,128)(2,1)S(1)} %get-tuple-element.369), channel_id=1, source_target_pairs={{1,0},{2,1},{3,2},{4,3},{5,4},{6,5},{7,6},{8,7},{9,8},{10,9},{11,1... | collective-permute-start | bytes 3145736 | tf_op jit(solution)/shard_map/while/body/eval_jaxpr/ppermute | solution.py:16
  519.9 24.4 %collective-permute-start.2 = (bf16[24,128,128]{2,0,1:T(8,128)(2,1)}, bf16[24,128,128]{2,0,1:T(8,128)(2,1)S(1)}, u32[]{:S(2)}, u32[]{:S(2)}) collective-permute-start(bf16[24,128,128]{2,0,1:T(8,128)(2,1)} %get-tuple-element.371), channel_id=1, source_target_pairs={{16,0},{32,16},{48,32},{64,48},{80,64},{96,80},{112,96},{0,112},{1... | collective-permute-start | bytes 2359304 | tf_op jit(solution)/shard_map/while/body/eval_jaxpr/ppermute | solution.py:16
  521.4 24.2 %collective-permute-start = (bf16[32,128,128]{2,0,1:T(8,128)(2,1)S(1)}, bf16[32,128,128]{2,0,1:T(8,128)(2,1)S(1)}, u32[]{:S(2)}, u32[]{:S(2)}) collective-permute-start(bf16[32,128,128]{2,0,1:T(8,128)(2,1)S(1)} %get-tuple-element.369), channel_id=1, source_target_pairs={{1,0},{2,1},{3,2},{4,3},{5,4},{6,5},{7,6},{8,7},{9,8},{10,9},{11,1... | collective-permute-start | bytes 3145736 | tf_op jit(solution)/shard_map/while/body/eval_jaxpr/ppermute | solution.py:16
  556.2 21.4 %collective-permute-start.2 = (bf16[24,128,128]{2,0,1:T(8,128)(2,1)}, bf16[24,128,128]{2,0,1:T(8,128)(2,1)S(1)}, u32[]{:S(2)}, u32[]{:S(2)}) collective-permute-start(bf16[24,128,128]{2,0,1:T(8,128)(2,1)} %get-tuple-element.371), channel_id=1, source_target_pairs={{16,0},{32,16},{48,32},{64,48},{80,64},{96,80},{112,96},{0,112},{1... | collective-permute-start | bytes 2359304 | tf_op jit(solution)/shard_map/while/body/eval_jaxpr/ppermute | solution.py:16
  559.2 19.9 %collective-permute-start = (bf16[32,128,128]{2,0,1:T(8,128)(2,1)S(1)}, bf16[32,128,128]{2,0,1:T(8,128)(2,1)S(1)}, u32[]{:S(2)}, u32[]{:S(2)}) collective-permute-start(bf16[32,128,128]{2,0,1:T(8,128)(2,1)S(1)} %get-tuple-element.369), channel_id=1, source_target_pairs={{1,0},{2,1},{3,2},{4,3},{5,4},{6,5},{7,6},{8,7},{9,8},{10,9},{11,1... | collective-permute-start | bytes 3145736 | tf_op jit(solution)/shard_map/while/body/eval_jaxpr/ppermute | solution.py:16
  593.4 24.3 %collective-permute-start.2 = (bf16[24,128,128]{2,0,1:T(8,128)(2,1)}, bf16[24,128,128]{2,0,1:T(8,128)(2,1)S(1)}, u32[]{:S(2)}, u32[]{:S(2)}) collective-permute-start(bf16[24,128,128]{2,0,1:T(8,128)(2,1)} %get-tuple-element.371), channel_id=1, source_target_pairs={{16,0},{32,16},{48,32},{64,48},{80,64},{96,80},{112,96},{0,112},{1... | collective-permute-start | bytes 2359304 | tf_op jit(solution)/shard_map/while/body/eval_jaxpr/ppermute | solution.py:16
  594.9 24.1 %collective-permute-start = (bf16[32,128,128]{2,0,1:T(8,128)(2,1)S(1)}, bf16[32,128,128]{2,0,1:T(8,128)(2,1)S(1)}, u32[]{:S(2)}, u32[]{:S(2)}) collective-permute-start(bf16[32,128,128]{2,0,1:T(8,128)(2,1)S(1)} %get-tuple-element.369), channel_id=1, source_target_pairs={{1,0},{2,1},{3,2},{4,3},{5,4},{6,5},{7,6},{8,7},{9,8},{10,9},{11,1... | collective-permute-start | bytes 3145736 | tf_op jit(solution)/shard_map/while/body/eval_jaxpr/ppermute | solution.py:16
  (65 other events, 621.0 us)
where the time goes:
time: 632 us; the launch traced here: 627 us
  waiting for transfers between devices  322 us (51%)
  starting transfers between devices  171 us (27%)
  local copies, waits for them, and re-layouts  73.1 us (12%)
  matrix products  49.1 us (8%)
  other arithmetic  9.9 us (2%)
    ppermute x60, waiting for transfers between devices, passed_along(): return lax.ppermute(block, axis, route)  292 us
    ppermute x60, starting transfers between devices, passed_along(): return lax.ppermute(block, axis, route)  148 us
    while x120, local copies, waits for them, and re-layouts  38.2 us
    dot_general x16, matrix products, block_product(): jnp.einsum('lkxy,kcyz->lcxz', left_dense, right_dense, preferred_element_...  34.2 us
    all_to_all x1, waiting for transfers between devices, per_device(): lax.all_to_all(left_tiles, 'col', split_axis=0, concat_axis=0, tiled=True)  14.2 us
  transfers between devices with their start and end apart: 64, of which 33 were waited for; matrix products, arithmetic and copies ran while one was open for 9% of the time, Pallas kernels for 0%

commit v1 on v0

v1 whole, which is shorter than its diff:
```python
import functools

import jax
import jax.numpy as jnp
from jax import lax
from jax.experimental import pallas as pl
from jax.experimental.pallas import tpu as pltpu
from jax.sharding import PartitionSpec as P

TILE = 128
RL = 8
CL = 6
KW = 64
MR = 64
MC = 96
ATD = 17
BTD = 10
CT = 24
N_ROW = 8
N_COL = 16
LIST = 656

A_PLACES = [
    (y, z, c) for z in (0, 1) for y in (0, 3, 1, 2) for c in (0, 1)
]
B_PLACES = [(x, z) for z in (0, 1) for x in (0, 3, 1, 2)]


def col_move(x, dy=0, dz=0, dc=0, by_core=False):
    pairs = []
    for i in range(N_COL):
        y, z, c = i // 4, i // 2 % 2, i % 2
        step = -dy if by_core and c else dy
        pairs.append((i, (y + step) % 4 * 4 + (z + dz) % 2 * 2 + (c + dc) % 2))
    return lax.ppermute(x, "col", pairs)


def row_move(x, dx=0, dz=0):
    pairs = []
    for i in range(N_ROW):
        z, xx = i // 4, i % 4
        pairs.append((i, (z + dz) % 2 * 4 + (xx + dx) % 4))
    return lax.ppermute(x, "row", pairs)


def row_move_by_core(x):
    pairs = []
    for p in range(N_ROW):
        for q in range(N_COL):
            step = -1 if q % 2 else 1
            pairs.append((p * N_COL + q, (p // 4 * 4 + (p % 4 + step) % 4) * N_COL + q))
    return lax.ppermute(x, ("row", "col"), pairs)


def list_kernel(
    where_ref, aidx_ref, bidx_ref, rdist_ref, cdist_ref, cidx_ref,
    list_ref, start_ref, place_ref,
    row_place, col_place, slot_at, head, follow, b_col,
):
    p = where_ref[0]
    q = where_ref[1]

    def rank(n, dist_ref, mine, out):
        def body(r, count):
            hit = dist_ref[r] == mine
            out[r] = jnp.where(hit, count, 0)
            return count + hit.astype(jnp.int32)
        lax.fori_loop(0, n, body, jnp.int32(0))

    rank(MR, rdist_ref, p, row_place)
    rank(MC, cdist_ref, q, col_place)

    def clear(n, out):
        def body(r, _):
            out[r] = jnp.int32(-1)
            return 0
        lax.fori_loop(0, n, body, 0)

    clear(RL * CL, slot_at)
    clear(KW, head)

    def pattern(n, _):
        at = row_place[cidx_ref[2 * n]] * CL + col_place[cidx_ref[2 * n + 1]]
        slot_at[at] = n
        place_ref[n] = at
        return 0

    lax.fori_loop(0, CT, pattern, 0)

    for m, (sx, sz) in enumerate(B_PLACES):
        src = (p // 4 + sz) % 2 * 4 + (p % 4 + sx) % 4

        def link(t, _, src=src, m=m):
            at = (src * BTD + t) * 2
            k = bidx_ref[at]
            b = m * BTD + t
            b_col[b] = col_place[bidx_ref[at + 1]]
            follow[b] = head[k]
            head[k] = b
            return 0

        lax.fori_loop(0, BTD, link, 0)

    count = jnp.int32(0)
    for m, (sy, sz, sc) in enumerate(A_PLACES):
        src = (q // 4 + sy) % 4 * 4 + (q // 2 + sz) % 2 * 2 + (q + sc) % 2
        start_ref[m] = count

        def tile(t, count, src=src):
            at = (src * ATD + t) * 2
            i = row_place[aidx_ref[at]] * CL
            k = aidx_ref[at + 1]

            def more(state):
                return state[0] >= 0

            def step(state):
                b, count = state
                slot = slot_at[i + b_col[b]]
                list_ref[count] = t + b * 32 + slot * 4096
                return follow[b], count + (slot >= 0).astype(jnp.int32)

            return lax.while_loop(more, step, (head[k], count))[1]

        count = lax.fori_loop(0, ATD, tile, count)
    start_ref[len(A_PLACES)] = count


def build_lists(where, aidx, bidx, rdist, cdist, cidx):
    smem = pl.BlockSpec(memory_space=pltpu.SMEM)
    i32 = jnp.int32
    return pl.pallas_call(
        list_kernel,
        out_shape=(
            jax.ShapeDtypeStruct((LIST,), i32),
            jax.ShapeDtypeStruct((len(A_PLACES) + 1,), i32),
            jax.ShapeDtypeStruct((CT,), i32),
        ),
        in_specs=[smem] * 6,
        out_specs=(smem,) * 3,
        scratch_shapes=[
            pltpu.SMEM((MR,), i32),
            pltpu.SMEM((MC,), i32),
            pltpu.SMEM((RL * CL,), i32),
            pltpu.SMEM((KW,), i32),
            pltpu.SMEM((N_ROW * BTD,), i32),
            pltpu.SMEM((N_ROW * BTD,), i32),
        ],
    )(where, aidx, bidx, rdist, cdist, cidx)


def add_products(list_ref, start_ref, m, a_ref, b_ref, acc_ref):
    def body(n, _):
        entry = list_ref[n]
        t = entry & 31
        b = (entry >> 5) & 127
        slot = entry >> 12
        acc_ref[slot] += jnp.dot(a_ref[t], b_ref[b], preferred_element_type=jnp.float32)
        return 0

    lax.fori_loop(start_ref[m], start_ref[m + 1], body, 0)


def first_kernel(n_a, list_ref, start_ref, *refs):
    a_refs, b_refs = refs[:n_a], refs[n_a:n_a + len(B_PLACES)]
    acc_ref, b_ref = refs[n_a + len(B_PLACES):]
    acc_ref[...] = jnp.zeros_like(acc_ref)
    for m, ref in enumerate(b_refs):
        b_ref[m * BTD:(m + 1) * BTD] = ref[...]
    for m, ref in enumerate(a_refs):
        add_products(list_ref, start_ref, m, ref, b_ref, acc_ref)


def last_kernel(first, list_ref, start_ref, place_ref, acc_in, b_ref, *refs):
    a_refs, (out_ref, acc_ref) = refs[:-2], refs[-2:]
    out_ref[...] = jnp.zeros_like(out_ref)
    acc_ref[...] = acc_in[...]
    for m, ref in enumerate(a_refs):
        add_products(list_ref, start_ref, first + m, ref, b_ref, acc_ref)

    def body(n, _):
        out_ref[place_ref[n]] = acc_ref[n].astype(jnp.bfloat16)
        return 0

    lax.fori_loop(0, CT, body, 0)


def per_device(a_tiles, a_index, b_tiles, b_index, row_dist, col_dist, c_index):
    core = lax.axis_index("col") % 2
    where = jnp.stack([lax.axis_index("row"), lax.axis_index("col")]).astype(jnp.int32)
    aidx = lax.all_gather(a_index.reshape(2 * ATD), "col", tiled=True)
    bidx = lax.all_gather(b_index.reshape(2 * BTD), "row", tiled=True)
    entries, starts, places = build_lists(
        where, aidx, bidx, row_dist, col_dist, c_index.reshape(2 * CT)
    )

    a_blocks = []
    b_blocks = []
    a_far = col_move(a_tiles, dz=1)
    b_far = row_move(b_tiles, dz=1)
    for tiles in (a_tiles, a_far):
        up, down = col_move(tiles, dy=1), col_move(tiles, dy=-1)
        across = col_move(jnp.where(core == 0, up, down), dy=1, by_core=True)
        for block in (tiles, up, down, across):
            a_blocks += [block, col_move(block, dc=1)]
    for tiles in (b_tiles, b_far):
        up, down = row_move(tiles, dx=1), row_move(tiles, dx=-1)
        across = row_move_by_core(jnp.where(core == 0, up, down))
        b_blocks += [tiles, up, down, across]

    vmem = pl.BlockSpec(memory_space=pltpu.VMEM)
    smem = pl.BlockSpec(memory_space=pltpu.SMEM)
    early = len(A_PLACES) - 2
    acc, b_all = pl.pallas_call(
        functools.partial(first_kernel, early),
        out_shape=(
            jax.ShapeDtypeStruct((CT, TILE, TILE), jnp.float32),
            jax.ShapeDtypeStruct((N_ROW * BTD, TILE, TILE), jnp.bfloat16),
        ),
        in_specs=[smem] * 2 + [vmem] * (early + len(B_PLACES)),
        out_specs=(vmem,) * 2,
        compiler_params=pltpu.CompilerParams(vmem_limit_bytes=24 << 20),
        cost_estimate=pl.CostEstimate(flops=3_000_000_000, bytes_accessed=14_000_000, transcendentals=0),
    )(entries, starts, *a_blocks[:early], *b_blocks)
    out = pl.pallas_call(
        functools.partial(last_kernel, early),
        out_shape=jax.ShapeDtypeStruct((RL * CL, TILE, TILE), jnp.bfloat16),
        in_specs=[smem] * 3 + [vmem] * (2 + len(A_PLACES) - early),
        out_specs=vmem,
        scratch_shapes=[pltpu.VMEM((CT, TILE, TILE), jnp.float32)],
        compiler_params=pltpu.CompilerParams(vmem_limit_bytes=16 << 20),
        cost_estimate=pl.CostEstimate(flops=500_000_000, bytes_accessed=8_000_000, transcendentals=0),
    )(entries, starts, places, acc, b_all, *a_blocks[early:])
    return out.reshape(RL, CL, TILE, TILE)


def solution(mesh):
    in_specs = (
        P(("row", "col"), None, None),
        P(("row", "col"), None),
        P(("row", "col"), None, None),
        P(("row", "col"), None),
        P(),
        P(),
        P(("row", "col"), None),
    )
    out_specs = P("row", "col", None, None)
    return jax.shard_map(
        per_device, mesh=mesh, in_specs=in_specs, out_specs=out_specs, check_vma=False
    )
```

time: 632 us -> 141 us (0.22)
  the two profiles are of different devices: /device:TPU:1 before, /device:TPU:0 now
where the time goes in v1:
time: 141 us
  Pallas kernels  42.6 us (30%)
  waiting for transfers between devices  29.2 us (21%)
  starting transfers between devices  25 us (18%)
  blocking collectives  24.4 us (17%)
  local copies, waits for them, and re-layouts  17.2 us (12%)
  between operations  1.56 us (1%)
    unnamed x2, blocking collectives  24.4 us
    pallas_call x1, Pallas kernels, per_device(): pl.pallas_call(functools.partial(first_kernel, early), out_shape=(jax.Sha...  24.2 us
    unnamed x61, local copies, waits for them, and re-layouts  16.4 us
    ppermute x15, starting transfers between devices, col_move(): return lax.ppermute(x, 'col', pairs)  15.7 us
    ppermute x5, waiting for transfers between devices, row_move(): return lax.ppermute(x, 'row', pairs)  13.8 us
    pallas_call x1, Pallas kernels, build_lists(): pl.pallas_call(list_kernel, out_shape=(jax.ShapeDtypeStruct((LIST,), i32)...  13.2 us
    ppermute x15, waiting for transfers between devices, col_move(): return lax.ppermute(x, 'col', pairs)  9.21 us
    ppermute x5, starting transfers between devices, row_move(): return lax.ppermute(x, 'row', pairs)  8.67 us
  transfers between devices with their start and end apart: 22, of which 9 were waited for; matrix products, arithmetic and copies ran while one was open for 3% of the time, Pallas kernels for 27%

profile of v1, /device:TPU:0, one launch (start us, length us, event | category | flops | bytes accessed | tf_op | source)
XLA Modules:
  0.0 140.9 jit_solution(760263868072688388)
XLA Ops:
  0.0 1.6 %collective-permute-start.13 = (bf16[10,128,128]{2,1,0:T(8,128)(2,1)}, bf16[10,128,128]{2,1,0:T(8,128)(2,1)S(1)}, u32[]{:S(2)}, u32[]{:S(2)}) collective-permute-start(bf16[10,128,128]{2,1,0:T(8,128)(2,1)} %refs_14_.1), channel_id=1, source_target_pairs={{0,16},{16,32},{32,48},{48,0},{64,80},{80,96},{96,112},{112,64},{1... | collective-permute-start | bytes 983048 | tf_op jit(solution)/shard_map/ppermute | solution.py:43
  1.6 3.9 %collective-permute-start.7 = (bf16[17,128,128]{2,1,0:T(8,128)(2,1)}, bf16[17,128,128]{2,1,0:T(8,128)(2,1)}, u32[]{:S(2)}, u32[]{:S(2)}) collective-permute-start(bf16[17,128,128]{2,1,0:T(8,128)(2,1)} %refs_0_.1), channel_id=1, source_target_pairs={{0,2},{1,3},{2,0},{3,1},{4,6},{5,7},{6,4},{7,5},{8,10},{9,11},{10,... | collective-permute-start | bytes 1671176 | tf_op jit(solution)/shard_map/ppermute | solution.py:35
  5.5 1.6 %collective-permute-start.1 = (bf16[17,128,128]{2,1,0:T(8,128)(2,1)}, bf16[17,128,128]{2,1,0:T(8,128)(2,1)S(1)}, u32[]{:S(2)}, u32[]{:S(2)}) collective-permute-start(bf16[17,128,128]{2,1,0:T(8,128)(2,1)} %refs_0_.1), channel_id=1, source_target_pairs={{0,4},{1,5},{2,6},{3,7},{4,8},{5,9},{6,10},{7,11},{8,12},{9,13},{1... | collective-permute-start | bytes 1671176 | tf_op jit(solution)/shard_map/ppermute | solution.py:35
  7.0 1.7 %collective-permute-start.3 = (bf16[17,128,128]{2,1,0:T(8,128)(2,1)}, bf16[17,128,128]{2,1,0:T(8,128)(2,1)S(1)}, u32[]{:S(2)}, u32[]{:S(2)}) collective-permute-start(bf16[17,128,128]{2,1,0:T(8,128)(2,1)} %refs_0_.1), channel_id=1, source_target_pairs={{0,12},{1,13},{2,14},{3,15},{4,0},{5,1},{6,2},{7,3},{8,4},{9,5},{1... | collective-permute-start | bytes 1671176 | tf_op jit(solution)/shard_map/ppermute | solution.py:35
  8.7 1.7 %collective-permute-start.14 = (bf16[10,128,128]{2,1,0:T(8,128)(2,1)}, bf16[10,128,128]{2,1,0:T(8,128)(2,1)S(1)}, u32[]{:S(2)}, u32[]{:S(2)}) collective-permute-start(bf16[10,128,128]{2,1,0:T(8,128)(2,1)} %refs_14_.1), channel_id=1, source_target_pairs={{0,48},{16,0},{32,16},{48,32},{64,112},{80,64},{96,80},{112,96},{1... | collective-permute-start | bytes 983048 | tf_op jit(solution)/shard_map/ppermute | solution.py:43
  10.8 2.1 %collective-permute-start.16 = (bf16[10,128,128]{2,1,0:T(8,128)(2,1)}, bf16[10,128,128]{2,1,0:T(8,128)(2,1)}, u32[]{:S(2)}, u32[]{:S(2)}) collective-permute-start(bf16[10,128,128]{2,1,0:T(8,128)(2,1)} %refs_14_.1), channel_id=1, source_target_pairs={{0,64},{16,80},{32,96},{48,112},{64,0},{80,16},{96,32},{112,48},{1... | collective-permute-start | bytes 983048 | tf_op jit(solution)/shard_map/ppermute | solution.py:43
  12.9 4.4 %collective-permute-done.14.refs_16_ = bf16[10,128,128]{2,1,0:T(8,128)(2,1)S(1)} collective-permute-done((bf16[10,128,128]{2,1,0:T(8,128)(2,1)}, bf16[10,128,128]{2,1,0:T(8,128)(2,1)S(1)}, u32[]{:S(2)}, u32[]{:S(2)}) %collective-permute-start.14) | collective-permute-done | bytes 327712 | tf_op jit(solution)/shard_map/ppermute | solution.py:43
  17.3 2.0 %collective-permute-done.7.refs_8_ = bf16[17,128,128]{2,1,0:T(8,128)(2,1)} collective-permute-done((bf16[17,128,128]{2,1,0:T(8,128)(2,1)}, bf16[17,128,128]{2,1,0:T(8,128)(2,1)}, u32[]{:S(2)}, u32[]{:S(2)}) %collective-permute-start.7) | collective-permute-done | bytes 557088 | tf_op jit(solution)/shard_map/ppermute | solution.py:35
  19.3 1.6 %collective-permute-start.9 = (bf16[17,128,128]{2,1,0:T(8,128)(2,1)}, bf16[17,128,128]{2,1,0:T(8,128)(2,1)S(1)}, u32[]{:S(2)}, u32[]{:S(2)}) collective-permute-start(bf16[17,128,128]{2,1,0:T(8,128)(2,1)} %collective-permute-done.7.refs_8_), channel_id=1, source_target_pairs={{0,4},{1,5},{2,6},{3,7},{4,8},{5,9},{6,10},{7,11},{8,12},{9,13},{1... | collective-permute-start | bytes 1671176 | tf_op jit(solution)/shard_map/ppermute | solution.py:35
  20.8 5.0 %collective-permute-done.16.refs_18_ = bf16[10,128,128]{2,1,0:T(8,128)(2,1)} collective-permute-done((bf16[10,128,128]{2,1,0:T(8,128)(2,1)}, bf16[10,128,128]{2,1,0:T(8,128)(2,1)}, u32[]{:S(2)}, u32[]{:S(2)}) %collective-permute-start.16) | collective-permute-done | bytes 327712 | tf_op jit(solution)/shard_map/ppermute | solution.py:43
  25.9 1.5 %collective-permute-start.17 = (bf16[10,128,128]{2,1,0:T(8,128)(2,1)}, bf16[10,128,128]{2,1,0:T(8,128)(2,1)S(1)}, u32[]{:S(2)}, u32[]{:S(2)}) collective-permute-start(bf16[10,128,128]{2,1,0:T(8,128)(2,1)} %collective-permute-done.16.refs_18_), channel_id=1, source_target_pairs={{0,16},{16,32},{32,48},{48,0},{64,80},{80,96},{96,112},{112,64},{1... | collective-permute-start | bytes 983048 | tf_op jit(solution)/shard_map/ppermute | solution.py:43
  27.4 1.7 %collective-permute-start.18 = (bf16[10,128,128]{2,1,0:T(8,128)(2,1)}, bf16[10,128,128]{2,1,0:T(8,128)(2,1)S(1)}, u32[]{:S(2)}, u32[]{:S(2)}) collective-permute-start(bf16[10,128,128]{2,1,0:T(8,128)(2,1)} %collective-permute-done.16.refs_18_), channel_id=1, source_target_pairs={{0,48},{16,0},{32,16},{48,32},{64,112},{80,64},{96,80},{112,96},{1... | collective-permute-start | bytes 983048 | tf_op jit(solution)/shard_map/ppermute | solution.py:43
  29.1 3.0 %collective-permute-start.11 = (bf16[17,128,128]{2,1,0:T(8,128)(2,1)}, bf16[17,128,128]{2,1,0:T(8,128)(2,1)S(1)}, u32[]{:S(2)}, u32[]{:S(2)}) collective-permute-start(bf16[17,128,128]{2,1,0:T(8,128)(2,1)} %collective-permute-done.7.refs_8_), channel_id=1, source_target_pairs={{0,12},{1,13},{2,14},{3,15},{4,0},{5,1},{6,2},{7,3},{8,4},{9,5},{1... | collective-permute-start | bytes 1671176 | tf_op jit(solution)/shard_map/ppermute | solution.py:35
  32.7 2.9 %collective-permute-done.17.refs_19_ = bf16[10,128,128]{2,1,0:T(8,128)(2,1)S(1)} collective-permute-done((bf16[10,128,128]{2,1,0:T(8,128)(2,1)}, bf16[10,128,128]{2,1,0:T(8,128)(2,1)S(1)}, u32[]{:S(2)}, u32[]{:S(2)}) %collective-permute-start.17) | collective-permute-done | bytes 327712 | tf_op jit(solution)/shard_map/ppermute | solution.py:43
  35.6 1.6 %collective-permute-start.5 = (bf16[17,128,128]{2,1,0:T(8,128)(2,1)S(1)}, bf16[17,128,128]{2,1,0:T(8,128)(2,1)}, u32[]{:S(2)}, u32[]{:S(2)}) collective-permute-start(bf16[17,128,128]{2,1,0:T(8,128)(2,1)S(1)} %broadcast_select_fusion.1), channel_id=1, source_target_pairs={{0,4},{1,13},{2,6},{3,15},{4,8},{5,1},{6,10},{7,3},{8,12},{9,5},{1... | collective-permute-start | bytes 1671176 | tf_op jit(solution)/shard_map/ppermute | solution.py:35
  37.1 1.1 collective-permute-done.18.refs_20_
  38.8 6.7 %collective-permute-done.11.refs_12_ = bf16[17,128,128]{2,1,0:T(8,128)(2,1)S(1)} collective-permute-done((bf16[17,128,128]{2,1,0:T(8,128)(2,1)}, bf16[17,128,128]{2,1,0:T(8,128)(2,1)S(1)}, u32[]{:S(2)}, u32[]{:S(2)}) %collective-permute-start.11) | collective-permute-done | bytes 557088 | tf_op jit(solution)/shard_map/ppermute | solution.py:35
  47.5 6.3 %collective-permute-done.19.refs_21_ = bf16[10,128,128]{2,1,0:T(8,128)(2,1)S(1)} collective-permute-done((bf16[10,128,128]{2,1,0:T(8,128)(2,1)S(1)}, bf16[10,128,128]{2,1,0:T(8,128)(2,1)S(1)}, u32[]{:S(2)}, u32[]{:S(2)}) %collective-permute-start.19) | collective-permute-done | bytes 327712 | tf_op jit(solution)/shard_map/ppermute | solution.py:52
  61.9 11.4 %all-reduce.1.bidx_ref = s32[160]{0:T(256)} all-reduce(s32[160]{0:T(256)S(1)} %dynamic-update-slice.1), channel_id=1, replica_groups=mesh['row'=8,'col'=16] {'row'}, use_global_device_ids=true, to_apply=%add.1 | all-reduce | flops 160 | bytes 1280
  73.3 13.0 %all-reduce.aidx_ref = s32[544]{0:T(1024)} all-reduce(s32[544]{0:T(1024)S(1)} %dynamic-update-slice), channel_id=1, replica_groups=mesh['row'=8,'col'=16] {'col'}, use_global_device_ids=true, to_apply=%add | all-reduce | flops 544 | bytes 4352
  86.9 13.2 %shard_map.73 = (s32[656]{0:T(1024)}, s32[17]{0:T(128)}, s32[24]{0:T(128)}) custom-call(s32[2]{0:T(128)} %pad_add_fusion.where_ref, s32[544]{0:T(1024)} %all-reduce.aidx_ref, s32[160]{0:T(256)} %all-reduce.1.bidx_ref, s32[64]{0:T(128)} %rdist_ref.1, s32[96]{0:T(128)} %cdist_ref.1, s32[48]{0:T(128)} %reshape.14.cidx_ref), custom_call_target="tpu_custom_call" | custom-call | tf_op jit(solution)/shard_map/pallas_call | solution.py:132
  101.1 1.0 copy-done.3
  102.1 1.0 copy-done.5
  103.0 1.0 copy-done.7
  105.3 1.1 copy-done.11
  106.4 1.1 copy-done.13
  107.4 1.1 copy-done.15
  108.5 1.0 copy-done.16
  109.5 1.0 copy-done.18
  110.4 1.0 copy-done.20
  111.4 24.2 %shard_map.74 = (f32[24,128,128]{2,1,0:T(8,128)S(1)}, bf16[80,128,128]{2,1,0:T(8,128)(2,1)S(1)}) custom-call(s32[656]{0:T(1024)S(1)} %copy-done.8, s32[17]{0:T(128)S(1)} %copy-done.9, bf16[17,128,128]{2,1,0:T(8,128)(2,1)S(1)} %copy-done.11, bf16[17,128,128]{2,1,0:T(8,128)(2,1)} %collective-permute-done.refs_1_, ...), custom_call_target="tpu_custom_call" | custom-call | flops 3000000000 | bytes 14000000 | tf_op jit(solution)/shard_map/pallas_call | solution.py:214
  135.6 5.3 %shard_map.75 = bf16[48,128,128]{2,1,0:T(8,128)(2,1)} custom-call(s32[656]{0:T(1024)S(1)} %copy-done.8, s32[17]{0:T(128)S(1)} %copy-done.9, s32[24]{0:T(128)S(1)} %copy-done.10, f32[24,128,128]{2,1,0:T(8,128)S(1)} %get-tuple-element.13.acc_in, bf16[80,128,128]{2,1,0:T(8,128)(2,1)S(1)} %get-tuple-element.14.b_ref, ...), custom_call_target="tpu_custom_call" | custom-call | flops 500000000 | bytes 8000000 | tf_op jit(solution)/shard_map/pallas_call | solution.py:225
  (86 shorter events, 13.0 us)
Async XLA Ops:
  0.0 10.8 %collective-permute-start.13 = (bf16[10,128,128]{2,1,0:T(8,128)(2,1)}, bf16[10,128,128]{2,1,0:T(8,128)(2,1)S(1)}, u32[]{:S(2)}, u32[]{:S(2)}) collective-permute-start(bf16[10,128,128]{2,1,0:T(8,128)(2,1)} %refs_14_.1), channel_id=1, source_target_pairs={{0,16},{16,32},{32,48},{48,0},{64,80},{80,96},{96,112},{112,64},{1... | collective-permute-start | bytes 983048 | tf_op jit(solution)/shard_map/ppermute | solution.py:43
  1.6 17.7 %collective-permute-start.7 = (bf16[17,128,128]{2,1,0:T(8,128)(2,1)}, bf16[17,128,128]{2,1,0:T(8,128)(2,1)}, u32[]{:S(2)}, u32[]{:S(2)}) collective-permute-start(bf16[17,128,128]{2,1,0:T(8,128)(2,1)} %refs_0_.1), channel_id=1, source_target_pairs={{0,2},{1,3},{2,0},{3,1},{4,6},{5,7},{6,4},{7,5},{8,10},{9,11},{10,... | collective-permute-start | bytes 1671176 | tf_op jit(solution)/shard_map/ppermute | solution.py:35
  5.5 21.9 %collective-permute-start.1 = (bf16[17,128,128]{2,1,0:T(8,128)(2,1)}, bf16[17,128,128]{2,1,0:T(8,128)(2,1)S(1)}, u32[]{:S(2)}, u32[]{:S(2)}) collective-permute-start(bf16[17,128,128]{2,1,0:T(8,128)(2,1)} %refs_0_.1), channel_id=1, source_target_pairs={{0,4},{1,5},{2,6},{3,7},{4,8},{5,9},{6,10},{7,11},{8,12},{9,13},{1... | collective-permute-start | bytes 1671176 | tf_op jit(solution)/shard_map/ppermute | solution.py:35
  7.0 22.1 %collective-permute-start.3 = (bf16[17,128,128]{2,1,0:T(8,128)(2,1)}, bf16[17,128,128]{2,1,0:T(8,128)(2,1)S(1)}, u32[]{:S(2)}, u32[]{:S(2)}) collective-permute-start(bf16[17,128,128]{2,1,0:T(8,128)(2,1)} %refs_0_.1), channel_id=1, source_target_pairs={{0,12},{1,13},{2,14},{3,15},{4,0},{5,1},{6,2},{7,3},{8,4},{9,5},{1... | collective-permute-start | bytes 1671176 | tf_op jit(solution)/shard_map/ppermute | solution.py:35
  8.7 8.6 %collective-permute-start.14 = (bf16[10,128,128]{2,1,0:T(8,128)(2,1)}, bf16[10,128,128]{2,1,0:T(8,128)(2,1)S(1)}, u32[]{:S(2)}, u32[]{:S(2)}) collective-permute-start(bf16[10,128,128]{2,1,0:T(8,128)(2,1)} %refs_14_.1), channel_id=1, source_target_pairs={{0,48},{16,0},{32,16},{48,32},{64,112},{80,64},{96,80},{112,96},{1... | collective-permute-start | bytes 983048 | tf_op jit(solution)/shard_map/ppermute | solution.py:43
  10.8 28.0 %copy-start = (bf16[10,128,128]{2,1,0:T(8,128)(2,1)}, bf16[10,128,128]{2,1,0:T(8,128)(2,1)S(1)}, u32[]{:S(2)}) copy-start(bf16[10,128,128]{2,1,0:T(8,128)(2,1)S(1)} %collective-permute-done.13.refs_15_) | copy-start | bytes 983044
  10.8 15.1 %collective-permute-start.16 = (bf16[10,128,128]{2,1,0:T(8,128)(2,1)}, bf16[10,128,128]{2,1,0:T(8,128)(2,1)}, u32[]{:S(2)}, u32[]{:S(2)}) collective-permute-start(bf16[10,128,128]{2,1,0:T(8,128)(2,1)} %refs_14_.1), channel_id=1, source_target_pairs={{0,64},{16,80},{32,96},{48,112},{64,0},{80,16},{96,32},{112,48},{1... | collective-permute-start | bytes 983048 | tf_op jit(solution)/shard_map/ppermute | solution.py:43
  17.3 21.5 %copy-start.2 = (bf16[10,128,128]{2,1,0:T(8,128)(2,1)}, bf16[10,128,128]{2,1,0:T(8,128)(2,1)S(1)}, u32[]{:S(2)}) copy-start(bf16[10,128,128]{2,1,0:T(8,128)(2,1)S(1)} %collective-permute-done.14.refs_16_) | copy-start | bytes 983044
  17.3 15.0 %collective-permute-start = (bf16[17,128,128]{2,1,0:T(8,128)(2,1)}, bf16[17,128,128]{2,1,0:T(8,128)(2,1)}, u32[]{:S(2)}, u32[]{:S(2)}) collective-permute-start(bf16[17,128,128]{2,1,0:T(8,128)(2,1)} %refs_0_.1), channel_id=1, source_target_pairs={{0,1},{1,0},{2,3},{3,2},{4,5},{5,4},{6,7},{7,6},{8,9},{9,8},{10,11... | collective-permute-start | bytes 1671176 | tf_op jit(solution)/shard_map/ppermute | solution.py:35
  19.3 19.0 %collective-permute-start.9 = (bf16[17,128,128]{2,1,0:T(8,128)(2,1)}, bf16[17,128,128]{2,1,0:T(8,128)(2,1)S(1)}, u32[]{:S(2)}, u32[]{:S(2)}) collective-permute-start(bf16[17,128,128]{2,1,0:T(8,128)(2,1)} %collective-permute-done.7.refs_8_), channel_id=1, source_target_pairs={{0,4},{1,5},{2,6},{3,7},{4,8},{5,9},{6,10},{7,11},{8,12},{9,13},{1... | collective-permute-start | bytes 1671176 | tf_op jit(solution)/shard_map/ppermute | solution.py:35
  25.9 9.7 %collective-permute-start.17 = (bf16[10,128,128]{2,1,0:T(8,128)(2,1)}, bf16[10,128,128]{2,1,0:T(8,128)(2,1)S(1)}, u32[]{:S(2)}, u32[]{:S(2)}) collective-permute-start(bf16[10,128,128]{2,1,0:T(8,128)(2,1)} %collective-permute-done.16.refs_18_), channel_id=1, source_target_pairs={{0,16},{16,32},{32,48},{48,0},{64,80},{80,96},{96,112},{112,64},{1... | collective-permute-start | bytes 983048 | tf_op jit(solution)/shard_map/ppermute | solution.py:43
  27.4 10.9 %collective-permute-start.18 = (bf16[10,128,128]{2,1,0:T(8,128)(2,1)}, bf16[10,128,128]{2,1,0:T(8,128)(2,1)S(1)}, u32[]{:S(2)}, u32[]{:S(2)}) collective-permute-start(bf16[10,128,128]{2,1,0:T(8,128)(2,1)} %collective-permute-done.16.refs_18_), channel_id=1, source_target_pairs={{0,48},{16,0},{32,16},{48,32},{64,112},{80,64},{96,80},{112,96},{1... | collective-permute-start | bytes 983048 | tf_op jit(solution)/shard_map/ppermute | solution.py:43
  29.1 16.4 %collective-permute-start.11 = (bf16[17,128,128]{2,1,0:T(8,128)(2,1)}, bf16[17,128,128]{2,1,0:T(8,128)(2,1)S(1)}, u32[]{:S(2)}, u32[]{:S(2)}) collective-permute-start(bf16[17,128,128]{2,1,0:T(8,128)(2,1)} %collective-permute-done.7.refs_8_), channel_id=1, source_target_pairs={{0,12},{1,13},{2,14},{3,15},{4,0},{5,1},{6,2},{7,3},{8,4},{9,5},{1... | collective-permute-start | bytes 1671176 | tf_op jit(solution)/shard_map/ppermute | solution.py:35
  32.2 25.5 %copy-start.22 = (s32[17,2]{0,1:T(2,128)S(1)}, s32[17,2]{0,1:T(2,128)}, u32[]{:S(2)}) copy-start(s32[17,2]{0,1:T(2,128)} %param.8) | copy-start | bytes 412
  32.2 25.7 %copy-start.21 = (s32[10,2]{0,1:T(2,128)S(1)}, s32[10,2]{0,1:T(2,128)}, u32[]{:S(2)}) copy-start(s32[10,2]{0,1:T(2,128)} %param.10) | copy-start | bytes 244
  32.3 25.8 %copy-start.25 = (u32[128]{0:T(128)S(1)}, u32[128]{0:T(128)}, u32[]{:S(2)}) copy-start(u32[128]{0:T(128)} %constant.30) | copy-start | bytes 1540
  32.3 26.4 %copy-start.24 = (u32[128]{0:T(128)S(1)}, u32[128]{0:T(128)}, u32[]{:S(2)}) copy-start(u32[128]{0:T(128)} %constant.35) | copy-start | bytes 1540
  32.3 27.1 %copy-start.23 = (s32[24,2]{0,1:T(2,128)S(1)}, s32[24,2]{0,1:T(2,128)}, u32[]{:S(2)}) copy-start(s32[24,2]{0,1:T(2,128)} %param.13) | copy-start | bytes 580
  32.3 13.6 %collective-permute-start.15 = (bf16[10,128,128]{2,1,0:T(8,128)(2,1)S(1)}, bf16[10,128,128]{2,1,0:T(8,128)(2,1)S(1)}, u32[]{:S(2)}, u32[]{:S(2)}) collective-permute-start(bf16[10,128,128]{2,1,0:T(8,128)(2,1)S(1)} %broadcast_select_fusion.3), channel_id=1, source_target_pairs={{0,16},{1,49},{2,18},{3,51},{4,20},{5,53},{6,22},{7,55},{8,24},{9,... | collective-permute-start | bytes 983048 | tf_op jit(solution)/shard_map/ppermute | solution.py:52
  35.6 21.6 %copy-start.4 = (bf16[10,128,128]{2,1,0:T(8,128)(2,1)}, bf16[10,128,128]{2,1,0:T(8,128)(2,1)S(1)}, u32[]{:S(2)}) copy-start(bf16[10,128,128]{2,1,0:T(8,128)(2,1)S(1)} %collective-permute-done.17.refs_19_) | copy-start | bytes 983044
  35.6 20.3 %collective-permute-start.5 = (bf16[17,128,128]{2,1,0:T(8,128)(2,1)S(1)}, bf16[17,128,128]{2,1,0:T(8,128)(2,1)}, u32[]{:S(2)}, u32[]{:S(2)}) collective-permute-start(bf16[17,128,128]{2,1,0:T(8,128)(2,1)S(1)} %broadcast_select_fusion.1), channel_id=1, source_target_pairs={{0,4},{1,13},{2,6},{3,15},{4,8},{5,1},{6,10},{7,3},{8,12},{9,5},{1... | collective-permute-start | bytes 1671176 | tf_op jit(solution)/shard_map/ppermute | solution.py:35
  38.2 19.5 %copy-start.6 = (bf16[10,128,128]{2,1,0:T(8,128)(2,1)}, bf16[10,128,128]{2,1,0:T(8,128)(2,1)S(1)}, u32[]{:S(2)}) copy-start(bf16[10,128,128]{2,1,0:T(8,128)(2,1)S(1)} %collective-permute-done.18.refs_20_) | copy-start | bytes 983044
  38.2 16.3 %collective-permute-start.2 = (bf16[17,128,128]{2,1,0:T(8,128)(2,1)S(1)}, bf16[17,128,128]{2,1,0:T(8,128)(2,1)S(1)}, u32[]{:S(2)}, u32[]{:S(2)}) collective-permute-start(bf16[17,128,128]{2,1,0:T(8,128)(2,1)S(1)} %collective-permute-done.1.refs_2_), channel_id=1, source_target_pairs={{0,1},{1,0},{2,3},{3,2},{4,5},{5,4},{6,7},{7,6},{8,9},{9,8},{10,11... | collective-permute-start | bytes 1671176 | tf_op jit(solution)/shard_map/ppermute | solution.py:35
  38.2 17.6 %collective-permute-start.4 = (bf16[17,128,128]{2,1,0:T(8,128)(2,1)S(1)}, bf16[17,128,128]{2,1,0:T(8,128)(2,1)S(1)}, u32[]{:S(2)}, u32[]{:S(2)}) collective-permute-start(bf16[17,128,128]{2,1,0:T(8,128)(2,1)S(1)} %collective-permute-done.3.refs_4_), channel_id=1, source_target_pairs={{0,1},{1,0},{2,3},{3,2},{4,5},{5,4},{6,7},{7,6},{8,9},{9,8},{10,11... | collective-permute-start | bytes 1671176 | tf_op jit(solution)/shard_map/ppermute | solution.py:35
  45.5 8.3 %collective-permute-start.19 = (bf16[10,128,128]{2,1,0:T(8,128)(2,1)S(1)}, bf16[10,128,128]{2,1,0:T(8,128)(2,1)S(1)}, u32[]{:S(2)}, u32[]{:S(2)}) collective-permute-start(bf16[10,128,128]{2,1,0:T(8,128)(2,1)S(1)} %broadcast_select_fusion.2), channel_id=1, source_target_pairs={{0,16},{1,49},{2,18},{3,51},{4,20},{5,53},{6,22},{7,55},{8,24},{9,... | collective-permute-start | bytes 983048 | tf_op jit(solution)/shard_map/ppermute | solution.py:52
  46.6 11.1 %collective-permute-start.20 = (bf16[17,128,128]{2,1,0:T(8,128)(2,1)S(1)}, bf16[17,128,128]{2,1,0:T(8,128)(2,1)S(1)}, u32[]{:S(2)}, u32[]{:S(2)}) collective-permute-start(bf16[17,128,128]{2,1,0:T(8,128)(2,1)S(1)} %broadcast_select_fusion), channel_id=1, source_target_pairs={{0,4},{1,13},{2,6},{3,15},{4,8},{5,1},{6,10},{7,3},{8,12},{9,5},{1... | collective-permute-start | bytes 1671176 | tf_op jit(solution)/shard_map/ppermute | solution.py:35
  54.5 45.5 %collective-permute-start.8 = (bf16[17,128,128]{2,1,0:T(8,128)(2,1)}, bf16[17,128,128]{2,1,0:T(8,128)(2,1)}, u32[]{:S(2)}, u32[]{:S(2)}) collective-permute-start(bf16[17,128,128]{2,1,0:T(8,128)(2,1)} %collective-permute-done.7.refs_8_), channel_id=1, source_target_pairs={{0,1},{1,0},{2,3},{3,2},{4,5},{5,4},{6,7},{7,6},{8,9},{9,8},{10,11... | collective-permute-start | bytes 1671176 | tf_op jit(solution)/shard_map/ppermute | solution.py:35
  55.3 44.7 %collective-permute-start.10 = (bf16[17,128,128]{2,1,0:T(8,128)(2,1)S(1)}, bf16[17,128,128]{2,1,0:T(8,128)(2,1)}, u32[]{:S(2)}, u32[]{:S(2)}) collective-permute-start(bf16[17,128,128]{2,1,0:T(8,128)(2,1)S(1)} %collective-permute-done.9.refs_10_), channel_id=1, source_target_pairs={{0,1},{1,0},{2,3},{3,2},{4,5},{5,4},{6,7},{7,6},{8,9},{9,8},{10,11... | collective-permute-start | bytes 1671176 | tf_op jit(solution)/shard_map/ppermute | solution.py:35
  55.9 44.2 %collective-permute-start.6 = (bf16[17,128,128]{2,1,0:T(8,128)(2,1)}, bf16[17,128,128]{2,1,0:T(8,128)(2,1)}, u32[]{:S(2)}, u32[]{:S(2)}) collective-permute-start(bf16[17,128,128]{2,1,0:T(8,128)(2,1)} %collective-permute-done.5.refs_6_), channel_id=1, source_target_pairs={{0,1},{1,0},{2,3},{3,2},{4,5},{5,4},{6,7},{7,6},{8,9},{9,8},{10,11... | collective-permute-start | bytes 1671176 | tf_op jit(solution)/shard_map/ppermute | solution.py:35
  56.7 43.4 %collective-permute-start.12 = (bf16[17,128,128]{2,1,0:T(8,128)(2,1)S(1)}, bf16[17,128,128]{2,1,0:T(8,128)(2,1)}, u32[]{:S(2)}, u32[]{:S(2)}) collective-permute-start(bf16[17,128,128]{2,1,0:T(8,128)(2,1)S(1)} %collective-permute-done.11.refs_12_), channel_id=1, source_target_pairs={{0,1},{1,0},{2,3},{3,2},{4,5},{5,4},{6,7},{7,6},{8,9},{9,8},{10,11... | collective-permute-start | bytes 1671176 | tf_op jit(solution)/shard_map/ppermute | solution.py:35
  57.7 77.9 %collective-permute-start.21 = (bf16[17,128,128]{2,1,0:T(8,128)(2,1)S(1)}, bf16[17,128,128]{2,1,0:T(8,128)(2,1)S(1)}, u32[]{:S(2)}, u32[]{:S(2)}) collective-permute-start(bf16[17,128,128]{2,1,0:T(8,128)(2,1)S(1)} %collective-permute-done.20.refs_0_), channel_id=1, source_target_pairs={{0,1},{1,0},{2,3},{3,2},{4,5},{5,4},{6,7},{7,6},{8,9},{9,8},{10,11... | collective-permute-start | bytes 1671176 | tf_op jit(solution)/shard_map/ppermute | solution.py:35
  111.4 24.2 %copy-start.10 = (s32[24]{0:T(128)S(1)}, s32[24]{0:T(128)}, u32[]{:S(2)}) copy-start(s32[24]{0:T(128)} %get-tuple-element.12.place_ref) | copy-start | bytes 292
  (16 other events, 14.4 us)

commit v2 on v1

v2 whole, which is shorter than its diff:
```python
import functools

import jax
import jax.numpy as jnp
from jax import lax
from jax.experimental import pallas as pl
from jax.experimental.pallas import tpu as pltpu
from jax.sharding import PartitionSpec as P

TILE = 128
RL = 8
CL = 6
KW = 64
MR = 64
MC = 96
ATD = 17
BTD = 10
CT = 24
N_ROW = 8
N_COL = 16
LABEL = 16
A_ROWS = ATD * TILE
B_ROWS = BTD * TILE
A_BLOCK = A_ROWS + LABEL
B_BLOCK = B_ROWS + LABEL
LIST = 640
GROUP = 4


def col_move(x, dy=0, dz=0, dc=0, by_core=False):
    pairs = []
    for i in range(N_COL):
        y, z, c = i // 4, i // 2 % 2, i % 2
        step = -dy if by_core and c else dy
        pairs.append((i, (y + step) % 4 * 4 + (z + dz) % 2 * 2 + (c + dc) % 2))
    return lax.ppermute(x, "col", pairs)


def row_move(x, dx=0, dz=0):
    pairs = []
    for i in range(N_ROW):
        z, xx = i // 4, i % 4
        pairs.append((i, (z + dz) % 2 * 4 + (xx + dx) % 4))
    return lax.ppermute(x, "row", pairs)


def row_move_by_core(x):
    pairs = []
    for p in range(N_ROW):
        for q in range(N_COL):
            step = -1 if q % 2 else 1
            pairs.append((p * N_COL + q, (p // 4 * 4 + (p % 4 + step) % 4) * N_COL + q))
    return lax.ppermute(x, ("row", "col"), pairs)


def with_labels(tiles, index):
    n = tiles.shape[0]
    labels = jnp.pad(index.T.astype(jnp.bfloat16), ((0, LABEL - 2), (0, TILE - n)))
    return jnp.concatenate([tiles.reshape(n * TILE, TILE), labels])


def copy_blocks(pieces, sems):
    copies = []
    for n, (src, dst) in enumerate(pieces):
        copy = pltpu.make_async_copy(src, dst, sems.at[n])
        copy.start()
        copies.append(copy)
    return copies


def read_labels(raw_ref):
    return raw_ref[:, :8, :].astype(jnp.float32)


def lanes_of(shape):
    return lax.broadcasted_iota(jnp.int32, shape, len(shape) - 1)


def rows_of(shape):
    return lax.broadcasted_iota(jnp.int32, shape, len(shape) - 2)


def small_dot(a, b, contract):
    return lax.dot_general(
        a.astype(jnp.bfloat16), b.astype(jnp.bfloat16), ((contract[:1], contract[1:]), ((), ())),
        preferred_element_type=jnp.float32,
    )


def make_list(n_blocks, labels, row_col, hot_k, slot_b, list_v):
    lane = lanes_of((8, TILE))
    sub = rows_of((8, TILE))
    one_up = jnp.where(lane < ATD, lane + 1, 0).astype(jnp.float32)
    k_rows = rows_of((KW, TILE)).astype(jnp.float32)
    held = jnp.zeros((16, KW), jnp.float32)
    for m in range(n_blocks):
        here = labels[m, 0:1, :] == row_col
        there = (labels[m, 1:2, :] == k_rows).astype(jnp.float32)
        tile = jnp.where(here, one_up, 0.0)
        block = jnp.where(here & (one_up > 0), float(m + 1), 0.0)
        held += small_dot(jnp.concatenate([tile, block]), there, (1, 1))
    found = small_dot(held, hot_k, (1, 0))
    tile, block = found[:8], found[8:]
    hit = (tile > 0) & (slot_b > 0)
    hits = hit.astype(jnp.float32)
    square = (TILE, TILE)
    before = (rows_of(square) < lanes_of(square)).astype(jnp.float32)
    place = small_dot(hits, before, (1, 0))
    in_row = small_dot(hits, jnp.ones(square, jnp.float32), (1, 0))
    for i in range(7):
        place += jnp.where(sub > i, in_row[i:i + 1], 0.0)
    place = jnp.where(hit, place, -1.0)
    total = jnp.sum(hits).astype(jnp.int32)
    b_tile = (lane - 6 * (lane >> 4)).astype(jnp.float32)
    fields = []
    for i in range(8):
        rows = (tile[i:i + 1] - 1, block[i:i + 1] - 1, b_tile[:1], CT + 1 - slot_b[i:i + 1])
        field = jnp.zeros((8, TILE), jnp.float32)
        for n, row in enumerate(rows):
            field = jnp.where(sub == n, row, field)
        fields.append(field)
    fields = jnp.concatenate(fields, axis=1).astype(jnp.bfloat16)

    for c in range(LIST // TILE):
        @pl.when(c * TILE < total)
        def _(c=c):
            spots = (rows_of(square) + c * TILE).astype(jnp.float32)
            chosen = jnp.concatenate(
                [(place[i:i + 1] == spots).astype(jnp.bfloat16) for i in range(8)], axis=1)
            got = small_dot(fields, chosen, (1, 1)).astype(jnp.int32)
            entry = got[0:1] + got[1:2] * ATD + got[2:3] * 512 + (CT - got[3:4]) * 65536
            list_v[c:c + 1, :] = entry
    return total


def store_list(list_v, list_ref, sem):
    copy = pltpu.make_async_copy(list_v, list_ref, sem)
    copy.start()
    copy.wait()


def add_products(total, list_ref, a_ref, b_ref, acc_ref):
    def body(g, _):
        found = []
        for u in range(GROUP):
            n = g * GROUP + u
            entry = list_ref[n >> 7, n & 127]
            a = pl.multiple_of((entry & 511) * TILE, TILE)
            b = pl.multiple_of(((entry >> 9) & 127) * TILE, TILE)
            product = jnp.dot(
                a_ref[pl.ds(a, TILE), :], b_ref[pl.ds(b, TILE), :],
                preferred_element_type=jnp.float32,
            )
            found.append((entry >> 16, product))
        for slot, product in found:
            acc_ref[slot] += product
        return 0

    lax.fori_loop(0, (total + GROUP - 1) // GROUP, body, 0)


def first_kernel(
    n_a, n_b, where_ref, rdist_ref, cdist_ref, cidx_ref, *refs,
):
    a_in, b_in = refs[:n_a], refs[n_a:n_a + n_b]
    (acc_ref, b_ref, row_col_ref, hot_k_ref, slot_b_ref, place_ref,
     a_ref, a_raw, b_raw, list_v, row_at, col_at, row_place, col_place, slot_ref, list_ref,
     a_sems, b_sems, raw_sems, list_sem) = refs[n_a + n_b:]
    raw = [(ref.at[pl.ds(A_ROWS, LABEL)], a_raw.at[m]) for m, ref in enumerate(a_in)]
    for m, ref in enumerate(b_in):
        for h in range(2):
            raw.append((ref.at[pl.ds(h * B_BLOCK + B_ROWS, LABEL)], b_raw.at[2 * m + h]))
    raw_copies = copy_blocks(raw, raw_sems)
    b_copies = copy_blocks(
        [(ref.at[pl.ds(h * B_BLOCK, B_ROWS)], b_ref.at[pl.ds((2 * m + h) * B_ROWS, B_ROWS)])
         for m, ref in enumerate(b_in) for h in range(2)], b_sems)
    a_copies = copy_blocks(
        [(ref.at[pl.ds(0, A_ROWS)], a_ref.at[pl.ds(m * A_ROWS, A_ROWS)])
         for m, ref in enumerate(a_in)], a_sems)
    acc_ref[...] = jnp.zeros_like(acc_ref)

    def rank(n, dist_ref, mine, at_ref, out):
        def body(r, count):
            out[r] = count
            at_ref[count] = r
            return count + jnp.where(dist_ref[r] == mine, 1, 0)
        lax.fori_loop(0, n, body, jnp.int32(0), unroll=8)

    rank(MR, rdist_ref, where_ref[0], row_at, row_place)
    rank(MC, cdist_ref, where_ref[1], col_at, col_place)

    def clear(n, _):
        slot_ref[n] = jnp.int32(0)
        return 0

    lax.fori_loop(0, RL * CL, clear, 0, unroll=8)

    def pattern(n, _):
        at = row_place[cidx_ref[n, 0]] * CL + col_place[cidx_ref[n, 1]]
        slot_ref[at] = n + 1
        place_ref[n] = at
        return 0

    lax.fori_loop(0, CT, pattern, 0, unroll=4)
    for copy in raw_copies:
        copy.wait()
    lane = lanes_of((8, TILE))
    sub = rows_of((8, TILE))
    b_labels = read_labels(b_raw)
    packed = jnp.zeros((8, TILE), jnp.float32)
    for m in range(2 * n_b):
        packed += pltpu.roll(jnp.where(lane < BTD, b_labels[m] + 1, 0.0), 16 * m, 1)
    hot_k_ref[...] = (packed[0:1] - 1 == rows_of((KW, TILE)).astype(jnp.float32)).astype(jnp.float32)
    row_col = jnp.zeros((8, TILE), jnp.float32)
    for i in range(RL):
        row_col = jnp.where(sub == i, row_at[i].astype(jnp.float32), row_col)
    row_col_ref[...] = row_col
    slot_b = jnp.zeros((8, TILE), jnp.float32)
    for j in range(CL):
        column = jnp.zeros((8, TILE), jnp.float32)
        for i in range(RL):
            column = jnp.where(sub == i, slot_ref[i * CL + j].astype(jnp.float32), column)
        slot_b = jnp.where(packed[1:2] - 1 == col_at[j].astype(jnp.float32), column, slot_b)
    slot_b_ref[...] = slot_b

    total = make_list(n_a, read_labels(a_raw), row_col, hot_k_ref[...], slot_b, list_v)
    store_list(list_v, list_ref, list_sem)
    for copy in b_copies + a_copies:
        copy.wait()
    add_products(total, list_ref, a_ref, b_ref, acc_ref)


def last_kernel(
    n_a, place_ref, acc_in, b_ref, row_col_ref, hot_k_ref, slot_b_ref, *refs,
):
    a_in = refs[:n_a]
    (out_ref, acc_ref, a_ref, a_raw, list_v, list_ref, a_sems, raw_sems, list_sem) = refs[n_a:]
    raw_copies = copy_blocks(
        [(ref.at[pl.ds(A_ROWS, LABEL)], a_raw.at[m]) for m, ref in enumerate(a_in)], raw_sems)
    a_copies = copy_blocks(
        [(ref.at[pl.ds(0, A_ROWS)], a_ref.at[pl.ds(m * A_ROWS, A_ROWS)])
         for m, ref in enumerate(a_in)], a_sems)
    for copy in raw_copies:
        copy.wait()
    total = make_list(
        n_a, read_labels(a_raw), row_col_ref[...], hot_k_ref[...], slot_b_ref[...], list_v)
    store_list(list_v, list_ref, list_sem)
    out_ref[...] = jnp.zeros_like(out_ref)
    acc_ref[...] = acc_in[...]
    for copy in a_copies:
        copy.wait()
    add_products(total, list_ref, a_ref, b_ref, acc_ref)

    def body(n, _):
        out_ref[place_ref[n]] = acc_ref[n].astype(jnp.bfloat16)
        return 0

    lax.fori_loop(0, CT, body, 0)


def per_device(a_tiles, a_index, b_tiles, b_index, row_dist, col_dist, c_index):
    core = lax.axis_index("col") % 2
    where = jnp.stack([lax.axis_index("row"), lax.axis_index("col")]).astype(jnp.int32)
    a_own = with_labels(a_tiles, a_index)
    b_own = with_labels(b_tiles, b_index)

    def by_core(first, second):
        return jnp.where(core == 0, first, second)

    def tie(x, *others):
        return lax.optimization_barrier((x, *others))[0]

    up0, down0 = col_move(a_own, dy=1), col_move(a_own, dy=-1)
    far = col_move(a_own, dz=1)
    b_near = jnp.concatenate([b_own, row_move(b_own, dz=1)])
    b_up, b_down = row_move(b_near, dx=1), row_move(b_near, dx=-1)
    pick0 = by_core(up0, down0)
    across0 = col_move(pick0, dy=1, by_core=True)
    far_sent = tie(far, pick0)
    up1, down1 = col_move(far_sent, dy=1), col_move(far_sent, dy=-1)
    b_across = row_move_by_core(by_core(b_up, b_down))
    pick1 = tie(by_core(up1, down1), across0)
    across1 = col_move(pick1, dy=1, by_core=True)

    early = [a_own, far, up0, down0, across0, up1, down1]
    early += [col_move(block, dc=1) for block in early]
    late = [across1, col_move(across1, dc=1)]
    b_blocks = [b_near, b_up, b_down, b_across]

    vmem = pl.BlockSpec(memory_space=pltpu.VMEM)
    smem = pl.BlockSpec(memory_space=pltpu.SMEM)
    anywhere = pl.BlockSpec(memory_space=pl.ANY)
    i32 = jnp.int32
    n_a, n_b = len(early), len(b_blocks)
    acc, b_all, row_col, hot_k, slot_b, places = pl.pallas_call(
        functools.partial(first_kernel, n_a, n_b),
        out_shape=(
            jax.ShapeDtypeStruct((CT + 1, TILE, TILE), jnp.float32),
            jax.ShapeDtypeStruct((2 * n_b * B_ROWS, TILE), jnp.bfloat16),
            jax.ShapeDtypeStruct((8, TILE), jnp.float32),
            jax.ShapeDtypeStruct((KW, TILE), jnp.float32),
            jax.ShapeDtypeStruct((8, TILE), jnp.float32),
            jax.ShapeDtypeStruct((CT,), i32),
        ),
        in_specs=[smem] * 4 + [anywhere] * (n_a + n_b),
        out_specs=(vmem,) * 5 + (smem,),
        scratch_shapes=[
            pltpu.VMEM((n_a * A_ROWS, TILE), jnp.bfloat16),
            pltpu.VMEM((n_a, LABEL, TILE), jnp.bfloat16),
            pltpu.VMEM((2 * n_b, LABEL, TILE), jnp.bfloat16),
            pltpu.VMEM((8, TILE), i32),
            pltpu.SMEM((MR,), i32),
            pltpu.SMEM((MC,), i32),
            pltpu.SMEM((MR,), i32),
            pltpu.SMEM((MC,), i32),
            pltpu.SMEM((RL * CL,), i32),
            pltpu.SMEM((8, TILE), i32),
            pltpu.SemaphoreType.DMA((n_a,)),
            pltpu.SemaphoreType.DMA((2 * n_b,)),
            pltpu.SemaphoreType.DMA((n_a + 2 * n_b,)),
            pltpu.SemaphoreType.DMA,
        ],
        compiler_params=pltpu.CompilerParams(vmem_limit_bytes=16 << 20),
        cost_estimate=pl.CostEstimate(flops=3_000_000_000, bytes_accessed=14_000_000, transcendentals=0),
    )(where, row_dist, col_dist, c_index, *early, *b_blocks)
    n_late = len(late)
    out = pl.pallas_call(
        functools.partial(last_kernel, n_late),
        out_shape=jax.ShapeDtypeStruct((RL * CL, TILE, TILE), jnp.bfloat16),
        in_specs=[smem] + [vmem] * 5 + [anywhere] * n_late,
        out_specs=vmem,
        scratch_shapes=[
            pltpu.VMEM((CT + 1, TILE, TILE), jnp.float32),
            pltpu.VMEM((n_late * A_ROWS, TILE), jnp.bfloat16),
            pltpu.VMEM((n_late, LABEL, TILE), jnp.bfloat16),
            pltpu.VMEM((8, TILE), i32),
            pltpu.SMEM((8, TILE), i32),
            pltpu.SemaphoreType.DMA((n_late,)),
            pltpu.SemaphoreType.DMA((n_late,)),
            pltpu.SemaphoreType.DMA,
        ],
        compiler_params=pltpu.CompilerParams(vmem_limit_bytes=12 << 20),
        cost_estimate=pl.CostEstimate(flops=500_000_000, bytes_accessed=8_000_000, transcendentals=0),
    )(places, acc, b_all, row_col, hot_k, slot_b, *late)
    return out.reshape(RL, CL, TILE, TILE)


def solution(mesh):
    in_specs = (
        P(("row", "col"), None, None),
        P(("row", "col"), None),
        P(("row", "col"), None, None),
        P(("row", "col"), None),
        P(),
        P(),
        P(("row", "col"), None),
    )
    out_specs = P("row", "col", None, None)
    return jax.shard_map(
        per_device, mesh=mesh, in_specs=in_specs, out_specs=out_specs, check_vma=False
    )
```

time: 141 us -> 85.3 us (0.60)
  the two profiles are of different devices: /device:TPU:0 before, /device:TPU:1 now
where the time goes in v2:
time: 85.3 us; the launch traced here: 84.3 us
  starting transfers between devices  34.5 us (40%)
  waiting for transfers between devices  18.3 us (21%)
  Pallas kernels  18.2 us (21%)
  local copies, waits for them, and re-layouts  7.64 us (9%)
  other arithmetic  5.57 us (7%)
    ppermute x15, starting transfers between devices, col_move(): return lax.ppermute(x, 'col', pairs)  28.4 us
    ppermute x15, waiting for transfers between devices, col_move(): return lax.ppermute(x, 'col', pairs)  16.5 us
    pallas_call x1, Pallas kernels, per_device(): pl.pallas_call(functools.partial(first_kernel, n_a, n_b), out_shape=(jax....  12.5 us
    unnamed x25, local copies, waits for them, and re-layouts  7.64 us
    pallas_call x1, Pallas kernels, per_device(): pl.pallas_call(functools.partial(last_kernel, n_late), out_shape=jax.Shap...  5.64 us
    ppermute x3, starting transfers between devices, row_move(): return lax.ppermute(x, 'row', pairs)  3.56 us
    ppermute x1, starting transfers between devices, row_move_by_core(): return lax.ppermute(x, ('row', 'col'), pairs)  2.48 us
    select_n x3, other arithmetic, by_core(): return jnp.where(core == 0, first, second)  2.12 us
  transfers between devices with their start and end apart: 19, of which 7 were waited for; matrix products, arithmetic and copies ran while one was open for 4% of the time, Pallas kernels for 15%

profile of v2, /device:TPU:1, one launch (start us, length us, event | category | flops | bytes accessed | tf_op | source)
XLA Modules:
  0.0 84.3 jit_solution(543422104803089259)
XLA Ops:
  0.0 0.7 convert_bitcast_fusion.1
  0.7 1.9 %fusion.1.refs_0_ = bf16[2192,128]{1,0:T(8,128)(2,1)} fusion(bf16[2,17]{1,0:T(2,128)(2,1)S(1)} %convert_bitcast_fusion.1, bf16[2176,128]{1,0:T(8,128)(2,1)} %bitcast.11), kind=kLoop, calls=%fused_computation.4 | loop fusion | flops 1683456 | bytes 1118276 | tf_op jit(solution)/shard_map/concatenate | solution.py:59
  2.6 2.1 %collective-permute-start.1 = (bf16[2192,128]{1,0:T(8,128)(2,1)}, bf16[2192,128]{1,0:T(8,128)(2,1)S(1)}, u32[]{:S(2)}, u32[]{:S(2)}) collective-permute-start(bf16[2192,128]{1,0:T(8,128)(2,1)} %fusion.1.refs_0_), channel_id=1, source_target_pairs={{0,4},{1,5},{2,6},{3,7},{4,8},{5,9},{6,10},{7,11},{8,12},{9,13},{1... | collective-permute-start | bytes 1683464 | tf_op jit(solution)/shard_map/ppermute | solution.py:36
  4.8 1.4 %collective-permute-start.2 = (bf16[2192,128]{1,0:T(8,128)(2,1)}, bf16[2192,128]{1,0:T(8,128)(2,1)S(1)}, u32[]{:S(2)}, u32[]{:S(2)}) collective-permute-start(bf16[2192,128]{1,0:T(8,128)(2,1)} %fusion.1.refs_0_), channel_id=1, source_target_pairs={{0,12},{1,13},{2,14},{3,15},{4,0},{5,1},{6,2},{7,3},{8,4},{9,5},{1... | collective-permute-start | bytes 1683464 | tf_op jit(solution)/shard_map/ppermute | solution.py:36
  6.2 3.6 %collective-permute-start = (bf16[2192,128]{1,0:T(8,128)(2,1)}, bf16[2192,128]{1,0:T(8,128)(2,1)}, u32[]{:S(2)}, u32[]{:S(2)}) collective-permute-start(bf16[2192,128]{1,0:T(8,128)(2,1)} %fusion.1.refs_0_), channel_id=1, source_target_pairs={{0,2},{1,3},{2,0},{3,1},{4,6},{5,7},{6,4},{7,5},{8,10},{9,11},{10,... | collective-permute-start | bytes 1683464 | tf_op jit(solution)/shard_map/ppermute | solution.py:36
  10.5 0.8 collective-permute-start.13
  11.3 7.5 %collective-permute-done.1.refs_2_ = bf16[2192,128]{1,0:T(8,128)(2,1)S(1)} collective-permute-done((bf16[2192,128]{1,0:T(8,128)(2,1)}, bf16[2192,128]{1,0:T(8,128)(2,1)S(1)}, u32[]{:S(2)}, u32[]{:S(2)}) %collective-permute-start.1) | collective-permute-done | bytes 561184 | tf_op jit(solution)/shard_map/ppermute | solution.py:36
  18.9 3.1 %collective-permute-done.refs_1_ = bf16[2192,128]{1,0:T(8,128)(2,1)} collective-permute-done((bf16[2192,128]{1,0:T(8,128)(2,1)}, bf16[2192,128]{1,0:T(8,128)(2,1)}, u32[]{:S(2)}, u32[]{:S(2)}) %collective-permute-start) | collective-permute-done | bytes 561184 | tf_op jit(solution)/shard_map/ppermute | solution.py:36
  22.0 2.7 %collective-permute-start.5 = (bf16[2192,128]{1,0:T(8,128)(2,1)}, bf16[2192,128]{1,0:T(8,128)(2,1)}, u32[]{:S(2)}, u32[]{:S(2)}) collective-permute-start(bf16[2192,128]{1,0:T(8,128)(2,1)} %collective-permute-done.refs_1_), channel_id=1, source_target_pairs={{0,12},{1,13},{2,14},{3,15},{4,0},{5,1},{6,2},{7,3},{8,4},{9,5},{1... | collective-permute-start | bytes 1683464 | tf_op jit(solution)/shard_map/ppermute | solution.py:36
  24.7 3.8 %collective-permute-start.6 = (bf16[2192,128]{1,0:T(8,128)(2,1)}, bf16[2192,128]{1,0:T(8,128)(2,1)S(1)}, u32[]{:S(2)}, u32[]{:S(2)}) collective-permute-start(bf16[2192,128]{1,0:T(8,128)(2,1)} %fusion.1.refs_0_), channel_id=1, source_target_pairs={{0,1},{1,0},{2,3},{3,2},{4,5},{5,4},{6,7},{7,6},{8,9},{9,8},{10,11... | collective-permute-start | bytes 1683464 | tf_op jit(solution)/shard_map/ppermute | solution.py:36
  28.4 1.1 %collective-permute-done.13 = bf16[1296,128]{1,0:T(8,128)(2,1)S(1)} collective-permute-done((bf16[1296,128]{1,0:T(8,128)(2,1)S(1)}, bf16[1296,128]{1,0:T(8,128)(2,1)S(1)}, u32[]{:S(2)}, u32[]{:S(2)}) %collective-permute-start.13) | collective-permute-done | bytes 331808 | tf_op jit(solution)/shard_map/ppermute | solution.py:44
  29.6 1.3 %collective-permute-start.14 = (bf16[2592,128]{1,0:T(8,128)(2,1)S(1)}, bf16[2592,128]{1,0:T(8,128)(2,1)S(1)}, u32[]{:S(2)}, u32[]{:S(2)}) collective-permute-start(bf16[2592,128]{1,0:T(8,128)(2,1)S(1)} %pad_maximum_fusion.refs_14_), channel_id=1, source_target_pairs={{0,16},{16,32},{32,48},{48,0},{64,80},{80,96},{96,112},{112,64},{1... | collective-permute-start | bytes 1990664 | tf_op jit(solution)/shard_map/ppermute | solution.py:44
  30.9 1.5 %collective-permute-start.15 = (bf16[2592,128]{1,0:T(8,128)(2,1)S(1)}, bf16[2592,128]{1,0:T(8,128)(2,1)S(1)}, u32[]{:S(2)}, u32[]{:S(2)}) collective-permute-start(bf16[2592,128]{1,0:T(8,128)(2,1)S(1)} %pad_maximum_fusion.refs_14_), channel_id=1, source_target_pairs={{0,48},{16,0},{32,16},{48,32},{64,112},{80,64},{96,80},{112,96},{1... | collective-permute-start | bytes 1990664 | tf_op jit(solution)/shard_map/ppermute | solution.py:44
  32.3 2.2 %collective-permute-done.4.refs_5_ = bf16[2192,128]{1,0:T(8,128)(2,1)} collective-permute-done((bf16[2192,128]{1,0:T(8,128)(2,1)}, bf16[2192,128]{1,0:T(8,128)(2,1)}, u32[]{:S(2)}, u32[]{:S(2)}) %collective-permute-start.4) | collective-permute-done | bytes 561184 | tf_op jit(solution)/shard_map/ppermute | solution.py:36
  34.6 5.6 %collective-permute-start.7 = (bf16[2192,128]{1,0:T(8,128)(2,1)}, bf16[2192,128]{1,0:T(8,128)(2,1)S(1)}, u32[]{:S(2)}, u32[]{:S(2)}) collective-permute-start(bf16[2192,128]{1,0:T(8,128)(2,1)} %collective-permute-done.refs_1_), channel_id=1, source_target_pairs={{0,1},{1,0},{2,3},{3,2},{4,5},{5,4},{6,7},{7,6},{8,9},{9,8},{10,11... | collective-permute-start | bytes 1683464 | tf_op jit(solution)/shard_map/ppermute | solution.py:36
  40.2 1.1 %broadcast_select_fusion.1 = bf16[2192,128]{1,0:T(8,128)(2,1)S(1)} fusion(bf16[2192,128]{1,0:T(8,128)(2,1)} %collective-permute-done.4.refs_5_, bf16[2192,128]{1,0:T(8,128)(2,1)} %collective-permute-done.5.refs_6_, pred[]{:T(512)S(6)} %eq.4), kind=kLoop, calls=%fused_computation.5 | loop fusion | flops 280576 | bytes 1683457 | tf_op jit(solution)/shard_map/jit(_where)/select_n | solution.py:268
  41.3 2.1 %collective-permute-done.3.refs_4_ = bf16[2192,128]{1,0:T(8,128)(2,1)} collective-permute-done((bf16[2192,128]{1,0:T(8,128)(2,1)S(1)}, bf16[2192,128]{1,0:T(8,128)(2,1)}, u32[]{:S(2)}, u32[]{:S(2)}) %collective-permute-start.3) | collective-permute-done | bytes 561184 | tf_op jit(solution)/shard_map/ppermute | solution.py:36
  43.4 6.1 %collective-permute-start.8 = (bf16[2192,128]{1,0:T(8,128)(2,1)S(1)}, bf16[2192,128]{1,0:T(8,128)(2,1)S(1)}, u32[]{:S(2)}, u32[]{:S(2)}) collective-permute-start(bf16[2192,128]{1,0:T(8,128)(2,1)S(1)} %collective-permute-done.1.refs_2_), channel_id=1, source_target_pairs={{0,1},{1,0},{2,3},{3,2},{4,5},{5,4},{6,7},{7,6},{8,9},{9,8},{10,11... | collective-permute-start | bytes 1683464 | tf_op jit(solution)/shard_map/ppermute | solution.py:36
  49.7 0.9 %broadcast_select_fusion = bf16[2592,128]{1,0:T(8,128)(2,1)} fusion(bf16[2592,128]{1,0:T(8,128)(2,1)S(1)} %collective-permute-done.14.refs_15_, bf16[2592,128]{1,0:T(8,128)(2,1)S(1)} %collective-permute-done.15.refs_16_, pred[]{:T(512)S(6)} %eq.4), kind=kLoop, calls=%fused_computation.3 | loop fusion | flops 331776 | bytes 1990657 | tf_op jit(solution)/shard_map/jit(_where)/select_n | solution.py:268
  50.6 0.8 copy-done
  51.4 2.5 %collective-permute-start.16 = (bf16[2592,128]{1,0:T(8,128)(2,1)}, bf16[2592,128]{1,0:T(8,128)(2,1)}, u32[]{:S(2)}, u32[]{:S(2)}) collective-permute-start(bf16[2592,128]{1,0:T(8,128)(2,1)} %broadcast_select_fusion), channel_id=1, source_target_pairs={{0,16},{1,49},{2,18},{3,51},{4,20},{5,53},{6,22},{7,55},{8,24},{9,... | collective-permute-start | bytes 1990664 | tf_op jit(solution)/shard_map/ppermute | solution.py:53
  53.9 0.8 copy-done.2
  54.7 0.8 %copy-done.4 = bf16[2192,128]{1,0:T(8,128)(2,1)} copy-done((bf16[2192,128]{1,0:T(8,128)(2,1)}, bf16[2192,128]{1,0:T(8,128)(2,1)S(1)}, u32[]{:S(2)}) %copy-start.4) | copy-done | bytes 561176
  56.1 0.9 %copy-done.6 = bf16[2192,128]{1,0:T(8,128)(2,1)} copy-done((bf16[2192,128]{1,0:T(8,128)(2,1)}, bf16[2192,128]{1,0:T(8,128)(2,1)S(1)}, u32[]{:S(2)}) %copy-start.6) | copy-done | bytes 561176
  56.9 1.5 %collective-permute-done.17.refs_0_ = bf16[2192,128]{1,0:T(8,128)(2,1)} collective-permute-done((bf16[2192,128]{1,0:T(8,128)(2,1)S(1)}, bf16[2192,128]{1,0:T(8,128)(2,1)}, u32[]{:S(2)}, u32[]{:S(2)}) %collective-permute-start.17) | collective-permute-done | bytes 561184 | tf_op jit(solution)/shard_map/ppermute | solution.py:36
  58.5 2.5 %collective-permute-start.18 = (bf16[2192,128]{1,0:T(8,128)(2,1)}, bf16[2192,128]{1,0:T(8,128)(2,1)}, u32[]{:S(2)}, u32[]{:S(2)}) collective-permute-start(bf16[2192,128]{1,0:T(8,128)(2,1)} %collective-permute-done.17.refs_0_), channel_id=1, source_target_pairs={{0,1},{1,0},{2,3},{3,2},{4,5},{5,4},{6,7},{7,6},{8,9},{9,8},{10,11... | collective-permute-start | bytes 1683464 | tf_op jit(solution)/shard_map/ppermute | solution.py:36
  61.9 1.0 %copy-done.1 = bf16[2192,128]{1,0:T(8,128)(2,1)S(1)} copy-done((bf16[2192,128]{1,0:T(8,128)(2,1)S(1)}, bf16[2192,128]{1,0:T(8,128)(2,1)}, u32[]{:S(2)}) %copy-start.1) | copy-done | bytes 561176
  62.9 1.1 %copy-done.3 = bf16[2192,128]{1,0:T(8,128)(2,1)S(1)} copy-done((bf16[2192,128]{1,0:T(8,128)(2,1)S(1)}, bf16[2192,128]{1,0:T(8,128)(2,1)}, u32[]{:S(2)}) %copy-start.3) | copy-done | bytes 561176
  64.0 1.1 %copy-done.5 = bf16[2192,128]{1,0:T(8,128)(2,1)S(1)} copy-done((bf16[2192,128]{1,0:T(8,128)(2,1)S(1)}, bf16[2192,128]{1,0:T(8,128)(2,1)}, u32[]{:S(2)}) %copy-start.5) | copy-done | bytes 561176
  65.0 1.1 %copy-done.7 = bf16[2192,128]{1,0:T(8,128)(2,1)S(1)} copy-done((bf16[2192,128]{1,0:T(8,128)(2,1)S(1)}, bf16[2192,128]{1,0:T(8,128)(2,1)}, u32[]{:S(2)}) %copy-start.7) | copy-done | bytes 561176
  66.1 12.5 %shard_map.73 = (f32[25,128,128]{2,1,0:T(8,128)S(1)}, bf16[10240,128]{1,0:T(8,128)(2,1)S(1)}, f32[8,128]{1,0:T(8,128)S(1)}, f32[64,128]{1,0:T(8,128)S(1)}, f32[8,128]{1,0:T(8,128)S(1)}, /*index=5*/s32[24]{0:T(128)S(1)}) custom-call(s32[2]{0:T(128)S(1)} %pad_add_fusion.where_ref, s32[64]{0:T(128)S(1)} %copy-done.8, s32[96]{0:T(128)S(1)} %copy-done.9, ...), custom_call_target="tpu_custom_call" | custom-call | flops 3000000000 | bytes 14000000 | tf_op jit(solution)/shard_map/pallas_call | solution.py:295
  78.6 5.6 %shard_map.74 = bf16[48,128,128]{2,1,0:T(8,128)(2,1)} custom-call(s32[24]{0:T(128)S(1)} %get-tuple-element.14.place_ref, f32[25,128,128]{2,1,0:T(8,128)S(1)} %get-tuple-element.15.acc_in, bf16[10240,128]{1,0:T(8,128)(2,1)S(1)} %get-tuple-element.16.b_ref, f32[8,128]{1,0:T(8,128)S(1)} %get-tuple-element.17.row_col_ref, ...), custom_call_target="tpu_custom_call" | custom-call | flops 500000000 | bytes 8000000 | tf_op jit(solution)/shard_map/pallas_call | solution.py:327
  (43 shorter events, 2.4 us)
Async XLA Ops:
  0.0 10.5 %copy-start.10 = (bf16[10,128,128]{2,1,0:T(8,128)(2,1)S(1)}, bf16[10,128,128]{2,1,0:T(8,128)(2,1)}, u32[]{:S(2)}) copy-start(bf16[10,128,128]{2,1,0:T(8,128)(2,1)} %param.9) | copy-start | bytes 983044
  2.6 16.2 %collective-permute-start.1 = (bf16[2192,128]{1,0:T(8,128)(2,1)}, bf16[2192,128]{1,0:T(8,128)(2,1)S(1)}, u32[]{:S(2)}, u32[]{:S(2)}) collective-permute-start(bf16[2192,128]{1,0:T(8,128)(2,1)} %fusion.1.refs_0_), channel_id=1, source_target_pairs={{0,4},{1,5},{2,6},{3,7},{4,8},{5,9},{6,10},{7,11},{8,12},{9,13},{1... | collective-permute-start | bytes 1683464 | tf_op jit(solution)/shard_map/ppermute | solution.py:36
  4.8 14.0 %collective-permute-start.2 = (bf16[2192,128]{1,0:T(8,128)(2,1)}, bf16[2192,128]{1,0:T(8,128)(2,1)S(1)}, u32[]{:S(2)}, u32[]{:S(2)}) collective-permute-start(bf16[2192,128]{1,0:T(8,128)(2,1)} %fusion.1.refs_0_), channel_id=1, source_target_pairs={{0,12},{1,13},{2,14},{3,15},{4,0},{5,1},{6,2},{7,3},{8,4},{9,5},{1... | collective-permute-start | bytes 1683464 | tf_op jit(solution)/shard_map/ppermute | solution.py:36
  6.2 15.8 %collective-permute-start = (bf16[2192,128]{1,0:T(8,128)(2,1)}, bf16[2192,128]{1,0:T(8,128)(2,1)}, u32[]{:S(2)}, u32[]{:S(2)}) collective-permute-start(bf16[2192,128]{1,0:T(8,128)(2,1)} %fusion.1.refs_0_), channel_id=1, source_target_pairs={{0,2},{1,3},{2,0},{3,1},{4,6},{5,7},{6,4},{7,5},{8,10},{9,11},{10,... | collective-permute-start | bytes 1683464 | tf_op jit(solution)/shard_map/ppermute | solution.py:36
  10.5 19.0 %collective-permute-start.13 = (bf16[1296,128]{1,0:T(8,128)(2,1)S(1)}, bf16[1296,128]{1,0:T(8,128)(2,1)S(1)}, u32[]{:S(2)}, u32[]{:S(2)}) collective-permute-start(bf16[1296,128]{1,0:T(8,128)(2,1)S(1)} %pad_maximum_fusion.1), channel_id=1, source_target_pairs={{0,64},{16,80},{32,96},{48,112},{64,0},{80,16},{96,32},{112,48},{1... | collective-permute-start | bytes 995336 | tf_op jit(solution)/shard_map/ppermute | solution.py:44
  22.0 12.5 %collective-permute-start.4 = (bf16[2192,128]{1,0:T(8,128)(2,1)}, bf16[2192,128]{1,0:T(8,128)(2,1)}, u32[]{:S(2)}, u32[]{:S(2)}) collective-permute-start(bf16[2192,128]{1,0:T(8,128)(2,1)} %collective-permute-done.refs_1_), channel_id=1, source_target_pairs={{0,4},{1,5},{2,6},{3,7},{4,8},{5,9},{6,10},{7,11},{8,12},{9,13},{1... | collective-permute-start | bytes 1683464 | tf_op jit(solution)/shard_map/ppermute | solution.py:36
  22.0 12.6 %collective-permute-start.5 = (bf16[2192,128]{1,0:T(8,128)(2,1)}, bf16[2192,128]{1,0:T(8,128)(2,1)}, u32[]{:S(2)}, u32[]{:S(2)}) collective-permute-start(bf16[2192,128]{1,0:T(8,128)(2,1)} %collective-permute-done.refs_1_), channel_id=1, source_target_pairs={{0,12},{1,13},{2,14},{3,15},{4,0},{5,1},{6,2},{7,3},{8,4},{9,5},{1... | collective-permute-start | bytes 1683464 | tf_op jit(solution)/shard_map/ppermute | solution.py:36
  24.7 25.9 %collective-permute-start.6 = (bf16[2192,128]{1,0:T(8,128)(2,1)}, bf16[2192,128]{1,0:T(8,128)(2,1)S(1)}, u32[]{:S(2)}, u32[]{:S(2)}) collective-permute-start(bf16[2192,128]{1,0:T(8,128)(2,1)} %fusion.1.refs_0_), channel_id=1, source_target_pairs={{0,1},{1,0},{2,3},{3,2},{4,5},{5,4},{6,7},{7,6},{8,9},{9,8},{10,11... | collective-permute-start | bytes 1683464 | tf_op jit(solution)/shard_map/ppermute | solution.py:36
  29.6 20.0 %collective-permute-start.14 = (bf16[2592,128]{1,0:T(8,128)(2,1)S(1)}, bf16[2592,128]{1,0:T(8,128)(2,1)S(1)}, u32[]{:S(2)}, u32[]{:S(2)}) collective-permute-start(bf16[2592,128]{1,0:T(8,128)(2,1)S(1)} %pad_maximum_fusion.refs_14_), channel_id=1, source_target_pairs={{0,16},{16,32},{32,48},{48,0},{64,80},{80,96},{96,112},{112,64},{1... | collective-permute-start | bytes 1990664 | tf_op jit(solution)/shard_map/ppermute | solution.py:44
  30.9 18.7 %collective-permute-start.15 = (bf16[2592,128]{1,0:T(8,128)(2,1)S(1)}, bf16[2592,128]{1,0:T(8,128)(2,1)S(1)}, u32[]{:S(2)}, u32[]{:S(2)}) collective-permute-start(bf16[2592,128]{1,0:T(8,128)(2,1)S(1)} %pad_maximum_fusion.refs_14_), channel_id=1, source_target_pairs={{0,48},{16,0},{32,16},{48,32},{64,112},{80,64},{96,80},{112,96},{1... | collective-permute-start | bytes 1990664 | tf_op jit(solution)/shard_map/ppermute | solution.py:44
  34.5 8.9 %collective-permute-start.3 = (bf16[2192,128]{1,0:T(8,128)(2,1)S(1)}, bf16[2192,128]{1,0:T(8,128)(2,1)}, u32[]{:S(2)}, u32[]{:S(2)}) collective-permute-start(bf16[2192,128]{1,0:T(8,128)(2,1)S(1)} %broadcast_select_fusion.2), channel_id=1, source_target_pairs={{0,4},{1,13},{2,6},{3,15},{4,8},{5,1},{6,10},{7,3},{8,12},{9,5},{1... | collective-permute-start | bytes 1683464 | tf_op jit(solution)/shard_map/ppermute | solution.py:36
  34.6 19.3 %collective-permute-start.7 = (bf16[2192,128]{1,0:T(8,128)(2,1)}, bf16[2192,128]{1,0:T(8,128)(2,1)S(1)}, u32[]{:S(2)}, u32[]{:S(2)}) collective-permute-start(bf16[2192,128]{1,0:T(8,128)(2,1)} %collective-permute-done.refs_1_), channel_id=1, source_target_pairs={{0,1},{1,0},{2,3},{3,2},{4,5},{5,4},{6,7},{7,6},{8,9},{9,8},{10,11... | collective-permute-start | bytes 1683464 | tf_op jit(solution)/shard_map/ppermute | solution.py:36
  41.3 19.7 %copy-start.11 = (s32[24,2]{0,1:T(2,128)S(1)}, s32[24,2]{0,1:T(2,128)}, u32[]{:S(2)}) copy-start(s32[24,2]{0,1:T(2,128)} %param.13) | copy-start | bytes 580
  41.3 20.5 %copy-start.8 = (s32[64]{0:T(128)S(1)}, s32[64]{0:T(128)}, u32[]{:S(2)}) copy-start(s32[64]{0:T(128)} %rdist_ref.1) | copy-start | bytes 772
  41.3 20.5 %copy-start.9 = (s32[96]{0:T(128)S(1)}, s32[96]{0:T(128)}, u32[]{:S(2)}) copy-start(s32[96]{0:T(128)} %cdist_ref.1) | copy-start | bytes 1156
  43.4 11.3 %collective-permute-start.8 = (bf16[2192,128]{1,0:T(8,128)(2,1)S(1)}, bf16[2192,128]{1,0:T(8,128)(2,1)S(1)}, u32[]{:S(2)}, u32[]{:S(2)}) collective-permute-start(bf16[2192,128]{1,0:T(8,128)(2,1)S(1)} %collective-permute-done.1.refs_2_), channel_id=1, source_target_pairs={{0,1},{1,0},{2,3},{3,2},{4,5},{5,4},{6,7},{7,6},{8,9},{9,8},{10,11... | collective-permute-start | bytes 1683464 | tf_op jit(solution)/shard_map/ppermute | solution.py:36
  49.6 6.5 %collective-permute-start.9 = (bf16[2192,128]{1,0:T(8,128)(2,1)S(1)}, bf16[2192,128]{1,0:T(8,128)(2,1)S(1)}, u32[]{:S(2)}, u32[]{:S(2)}) collective-permute-start(bf16[2192,128]{1,0:T(8,128)(2,1)S(1)} %collective-permute-done.2.refs_3_), channel_id=1, source_target_pairs={{0,1},{1,0},{2,3},{3,2},{4,5},{5,4},{6,7},{7,6},{8,9},{9,8},{10,11... | collective-permute-start | bytes 1683464 | tf_op jit(solution)/shard_map/ppermute | solution.py:36
  49.6 8.9 %collective-permute-start.17 = (bf16[2192,128]{1,0:T(8,128)(2,1)S(1)}, bf16[2192,128]{1,0:T(8,128)(2,1)}, u32[]{:S(2)}, u32[]{:S(2)}) collective-permute-start(bf16[2192,128]{1,0:T(8,128)(2,1)S(1)} %broadcast_select_fusion.1), channel_id=1, source_target_pairs={{0,4},{1,13},{2,6},{3,15},{4,8},{5,1},{6,10},{7,3},{8,12},{9,5},{1... | collective-permute-start | bytes 1683464 | tf_op jit(solution)/shard_map/ppermute | solution.py:36
  50.6 0.8 copy-start
  51.4 10.4 %collective-permute-start.16 = (bf16[2592,128]{1,0:T(8,128)(2,1)}, bf16[2592,128]{1,0:T(8,128)(2,1)}, u32[]{:S(2)}, u32[]{:S(2)}) collective-permute-start(bf16[2592,128]{1,0:T(8,128)(2,1)} %broadcast_select_fusion), channel_id=1, source_target_pairs={{0,16},{1,49},{2,18},{3,51},{4,20},{5,53},{6,22},{7,55},{8,24},{9,... | collective-permute-start | bytes 1990664 | tf_op jit(solution)/shard_map/ppermute | solution.py:53
  53.9 0.8 copy-start.2
  54.7 7.1 %collective-permute-start.11 = (bf16[2192,128]{1,0:T(8,128)(2,1)}, bf16[2192,128]{1,0:T(8,128)(2,1)}, u32[]{:S(2)}, u32[]{:S(2)}) collective-permute-start(bf16[2192,128]{1,0:T(8,128)(2,1)} %collective-permute-done.4.refs_5_), channel_id=1, source_target_pairs={{0,1},{1,0},{2,3},{3,2},{4,5},{5,4},{6,7},{7,6},{8,9},{9,8},{10,11... | collective-permute-start | bytes 1683464 | tf_op jit(solution)/shard_map/ppermute | solution.py:36
  54.7 0.8 %copy-start.4 = (bf16[2192,128]{1,0:T(8,128)(2,1)}, bf16[2192,128]{1,0:T(8,128)(2,1)S(1)}, u32[]{:S(2)}) copy-start(bf16[2192,128]{1,0:T(8,128)(2,1)S(1)} %collective-permute-done.8.refs_9_) | copy-start | bytes 1683460
  55.6 6.3 %collective-permute-start.12 = (bf16[2192,128]{1,0:T(8,128)(2,1)}, bf16[2192,128]{1,0:T(8,128)(2,1)}, u32[]{:S(2)}, u32[]{:S(2)}) collective-permute-start(bf16[2192,128]{1,0:T(8,128)(2,1)} %collective-permute-done.5.refs_6_), channel_id=1, source_target_pairs={{0,1},{1,0},{2,3},{3,2},{4,5},{5,4},{6,7},{7,6},{8,9},{9,8},{10,11... | collective-permute-start | bytes 1683464 | tf_op jit(solution)/shard_map/ppermute | solution.py:36
  56.1 0.9 %copy-start.6 = (bf16[2192,128]{1,0:T(8,128)(2,1)}, bf16[2192,128]{1,0:T(8,128)(2,1)S(1)}, u32[]{:S(2)}) copy-start(bf16[2192,128]{1,0:T(8,128)(2,1)S(1)} %collective-permute-done.9.refs_10_) | copy-start | bytes 1683460
  56.9 4.9 %collective-permute-start.10 = (bf16[2192,128]{1,0:T(8,128)(2,1)}, bf16[2192,128]{1,0:T(8,128)(2,1)}, u32[]{:S(2)}, u32[]{:S(2)}) collective-permute-start(bf16[2192,128]{1,0:T(8,128)(2,1)} %collective-permute-done.3.refs_4_), channel_id=1, source_target_pairs={{0,1},{1,0},{2,3},{3,2},{4,5},{5,4},{6,7},{7,6},{8,9},{9,8},{10,11... | collective-permute-start | bytes 1683464 | tf_op jit(solution)/shard_map/ppermute | solution.py:36
  58.5 20.2 %collective-permute-start.18 = (bf16[2192,128]{1,0:T(8,128)(2,1)}, bf16[2192,128]{1,0:T(8,128)(2,1)}, u32[]{:S(2)}, u32[]{:S(2)}) collective-permute-start(bf16[2192,128]{1,0:T(8,128)(2,1)} %collective-permute-done.17.refs_0_), channel_id=1, source_target_pairs={{0,1},{1,0},{2,3},{3,2},{4,5},{5,4},{6,7},{7,6},{8,9},{9,8},{10,11... | collective-permute-start | bytes 1683464 | tf_op jit(solution)/shard_map/ppermute | solution.py:36
  61.9 1.1 %copy-start.1 = (bf16[2192,128]{1,0:T(8,128)(2,1)S(1)}, bf16[2192,128]{1,0:T(8,128)(2,1)}, u32[]{:S(2)}) copy-start(bf16[2192,128]{1,0:T(8,128)(2,1)} %copy-done) | copy-start | bytes 1683460
  62.9 1.1 %copy-start.3 = (bf16[2192,128]{1,0:T(8,128)(2,1)S(1)}, bf16[2192,128]{1,0:T(8,128)(2,1)}, u32[]{:S(2)}) copy-start(bf16[2192,128]{1,0:T(8,128)(2,1)} %copy-done.2) | copy-start | bytes 1683460
  64.0 1.1 %copy-start.5 = (bf16[2192,128]{1,0:T(8,128)(2,1)S(1)}, bf16[2192,128]{1,0:T(8,128)(2,1)}, u32[]{:S(2)}) copy-start(bf16[2192,128]{1,0:T(8,128)(2,1)} %copy-done.4) | copy-start | bytes 1683460
  65.0 1.1 %copy-start.7 = (bf16[2192,128]{1,0:T(8,128)(2,1)S(1)}, bf16[2192,128]{1,0:T(8,128)(2,1)}, u32[]{:S(2)}) copy-start(bf16[2192,128]{1,0:T(8,128)(2,1)} %copy-done.6) | copy-start | bytes 1683460

commit v3 on v2

--- a/solution.py
+++ b/solution.py
@@ -24,7 +24,7 @@
 A_BLOCK = A_ROWS + LABEL
 B_BLOCK = B_ROWS + LABEL
 LIST = 640
-GROUP = 4
+GROUP = 8
 
 
 def col_move(x, dy=0, dz=0, dc=0, by_core=False):
@@ -54,9 +54,20 @@
 
 
 def with_labels(tiles, index):
-    n = tiles.shape[0]
-    labels = jnp.pad(index.T.astype(jnp.bfloat16), ((0, LABEL - 2), (0, TILE - n)))
-    return jnp.concatenate([tiles.reshape(n * TILE, TILE), labels])
+    n = tiles.shape[0] * TILE
+    inputs = [pltpu.with_memory_space_constraint(x, pltpu.HBM) for x in (tiles.reshape(n, TILE), index.T)]
+    return pl.pallas_call(
+        label_kernel,
+        out_shape=jax.ShapeDtypeStruct((n + LABEL, TILE), jnp.bfloat16),
+        in_specs=[pl.BlockSpec(memory_space=pl.ANY)] * 2,
+        out_specs=pl.BlockSpec(memory_space=pltpu.VMEM),
+        scratch_shapes=[
+            pltpu.VMEM((2, tiles.shape[0]), jnp.int32),
+            pltpu.VMEM((LABEL, TILE), jnp.float32),
+            pltpu.SemaphoreType.DMA((2,)),
+        ],
+        compiler_params=pltpu.CompilerParams(vmem_limit_bytes=2 << 20),
+    )(*inputs)
 
 
 def copy_blocks(pieces, sems):
@@ -159,25 +170,22 @@
     lax.fori_loop(0, (total + GROUP - 1) // GROUP, body, 0)
 
 
-def first_kernel(
+def product_kernel(
     n_a, n_b, where_ref, rdist_ref, cdist_ref, cidx_ref, *refs,
 ):
     a_in, b_in = refs[:n_a], refs[n_a:n_a + n_b]
-    (acc_ref, b_ref, row_col_ref, hot_k_ref, slot_b_ref, place_ref,
-     a_ref, a_raw, b_raw, list_v, row_at, col_at, row_place, col_place, slot_ref, list_ref,
+    (out_ref, acc_ref, a_ref, b_ref, a_raw, b_raw, list_v,
+     row_at, col_at, row_place, col_place, slot_ref, place_ref, list_ref,
      a_sems, b_sems, raw_sems, list_sem) = refs[n_a + n_b:]
-    raw = [(ref.at[pl.ds(A_ROWS, LABEL)], a_raw.at[m]) for m, ref in enumerate(a_in)]
-    for m, ref in enumerate(b_in):
-        for h in range(2):
-            raw.append((ref.at[pl.ds(h * B_BLOCK + B_ROWS, LABEL)], b_raw.at[2 * m + h]))
-    raw_copies = copy_blocks(raw, raw_sems)
+    raw_copies = copy_blocks(
+        [(ref.at[pl.ds(A_ROWS, LABEL)], a_raw.at[m]) for m, ref in enumerate(a_in)]
+        + [(ref.at[pl.ds(B_ROWS, LABEL)], b_raw.at[m]) for m, ref in enumerate(b_in)], raw_sems)
     b_copies = copy_blocks(
-        [(ref.at[pl.ds(h * B_BLOCK, B_ROWS)], b_ref.at[pl.ds((2 * m + h) * B_ROWS, B_ROWS)])
-         for m, ref in enumerate(b_in) for h in range(2)], b_sems)
+        [(ref.at[pl.ds(0, B_ROWS)], b_ref.at[pl.ds(m * B_ROWS, B_ROWS)])
+         for m, ref in enumerate(b_in)], b_sems)
     a_copies = copy_blocks(
         [(ref.at[pl.ds(0, A_ROWS)], a_ref.at[pl.ds(m * A_ROWS, A_ROWS)])
          for m, ref in enumerate(a_in)], a_sems)
-    acc_ref[...] = jnp.zeros_like(acc_ref)
 
     def rank(n, dist_ref, mine, at_ref, out):
         def body(r, count):
@@ -202,146 +210,121 @@
         return 0
 
     lax.fori_loop(0, CT, pattern, 0, unroll=4)
+    acc_ref[...] = jnp.zeros_like(acc_ref)
+    out_ref[...] = jnp.zeros_like(out_ref)
     for copy in raw_copies:
         copy.wait()
     lane = lanes_of((8, TILE))
     sub = rows_of((8, TILE))
     b_labels = read_labels(b_raw)
     packed = jnp.zeros((8, TILE), jnp.float32)
-    for m in range(2 * n_b):
+    for m in range(n_b):
         packed += pltpu.roll(jnp.where(lane < BTD, b_labels[m] + 1, 0.0), 16 * m, 1)
-    hot_k_ref[...] = (packed[0:1] - 1 == rows_of((KW, TILE)).astype(jnp.float32)).astype(jnp.float32)
+    hot_k = (packed[0:1] - 1 == rows_of((KW, TILE)).astype(jnp.float32)).astype(jnp.float32)
     row_col = jnp.zeros((8, TILE), jnp.float32)
     for i in range(RL):
         row_col = jnp.where(sub == i, row_at[i].astype(jnp.float32), row_col)
-    row_col_ref[...] = row_col
     slot_b = jnp.zeros((8, TILE), jnp.float32)
     for j in range(CL):
         column = jnp.zeros((8, TILE), jnp.float32)
         for i in range(RL):
             column = jnp.where(sub == i, slot_ref[i * CL + j].astype(jnp.float32), column)
         slot_b = jnp.where(packed[1:2] - 1 == col_at[j].astype(jnp.float32), column, slot_b)
-    slot_b_ref[...] = slot_b
-
-    total = make_list(n_a, read_labels(a_raw), row_col, hot_k_ref[...], slot_b, list_v)
+
+    total = make_list(n_a, read_labels(a_raw), row_col, hot_k, slot_b, list_v)
     store_list(list_v, list_ref, list_sem)
     for copy in b_copies + a_copies:
         copy.wait()
     add_products(total, list_ref, a_ref, b_ref, acc_ref)
 
-
-def last_kernel(
-    n_a, place_ref, acc_in, b_ref, row_col_ref, hot_k_ref, slot_b_ref, *refs,
-):
-    a_in = refs[:n_a]
-    (out_ref, acc_ref, a_ref, a_raw, list_v, list_ref, a_sems, raw_sems, list_sem) = refs[n_a:]
-    raw_copies = copy_blocks(
-        [(ref.at[pl.ds(A_ROWS, LABEL)], a_raw.at[m]) for m, ref in enumerate(a_in)], raw_sems)
-    a_copies = copy_blocks(
-        [(ref.at[pl.ds(0, A_ROWS)], a_ref.at[pl.ds(m * A_ROWS, A_ROWS)])
-         for m, ref in enumerate(a_in)], a_sems)
-    for copy in raw_copies:
-        copy.wait()
-    total = make_list(
-        n_a, read_labels(a_raw), row_col_ref[...], hot_k_ref[...], slot_b_ref[...], list_v)
-    store_list(list_v, list_ref, list_sem)
-    out_ref[...] = jnp.zeros_like(out_ref)
-    acc_ref[...] = acc_in[...]
-    for copy in a_copies:
-        copy.wait()
-    add_products(total, list_ref, a_ref, b_ref, acc_ref)
-
-    def body(n, _):
+    def finish(n, _):
         out_ref[place_ref[n]] = acc_ref[n].astype(jnp.bfloat16)
         return 0
 
-    lax.fori_loop(0, CT, body, 0)
+    lax.fori_loop(0, CT, finish, 0, unroll=4)
+
+
+def label_kernel(tiles_ref, index_ref, out_ref, index_v, labels_ref, sems):
+    n = tiles_ref.shape[0]
+    tiles_copy = pltpu.make_async_copy(tiles_ref, out_ref.at[pl.ds(0, n)], sems.at[0])
+    index_copy = pltpu.make_async_copy(index_ref, index_v, sems.at[1])
+    index_copy.start()
+    tiles_copy.start()
+    labels_ref[...] = jnp.zeros_like(labels_ref)
+    index_copy.wait()
+    labels_ref[0:2, 0:n // TILE] = index_v[...].astype(jnp.float32)
+    out_ref[n:n + LABEL] = labels_ref[...].astype(jnp.bfloat16)
+    tiles_copy.wait()
 
 
 def per_device(a_tiles, a_index, b_tiles, b_index, row_dist, col_dist, c_index):
     core = lax.axis_index("col") % 2
     where = jnp.stack([lax.axis_index("row"), lax.axis_index("col")]).astype(jnp.int32)
+    tokens = []
+
+    def by_core(first, second):
+        return jnp.where(core == 0, first, second)
+
+    def after(x, *others):
+        tied = lax.optimization_barrier((x, *[other[:16] for other in others]))
+        tokens.extend(tied[1:])
+        return tied[0]
+
     a_own = with_labels(a_tiles, a_index)
     b_own = with_labels(b_tiles, b_index)
-
-    def by_core(first, second):
-        return jnp.where(core == 0, first, second)
-
-    def tie(x, *others):
-        return lax.optimization_barrier((x, *others))[0]
-
     up0, down0 = col_move(a_own, dy=1), col_move(a_own, dy=-1)
     far = col_move(a_own, dz=1)
-    b_near = jnp.concatenate([b_own, row_move(b_own, dz=1)])
-    b_up, b_down = row_move(b_near, dx=1), row_move(b_near, dx=-1)
+    b_up0, b_down0 = row_move(b_own, dx=1), row_move(b_own, dx=-1)
     pick0 = by_core(up0, down0)
     across0 = col_move(pick0, dy=1, by_core=True)
-    far_sent = tie(far, pick0)
-    up1, down1 = col_move(far_sent, dy=1), col_move(far_sent, dy=-1)
-    b_across = row_move_by_core(by_core(b_up, b_down))
-    pick1 = tie(by_core(up1, down1), across0)
-    across1 = col_move(pick1, dy=1, by_core=True)
-
-    early = [a_own, far, up0, down0, across0, up1, down1]
-    early += [col_move(block, dc=1) for block in early]
-    late = [across1, col_move(across1, dc=1)]
-    b_blocks = [b_near, b_up, b_down, b_across]
-
+    b_pick0 = by_core(b_up0, b_down0)
+    b_across0 = row_move_by_core(after(b_pick0, pick0))
+    b_far = row_move(b_own, dz=1)
+    up1, down1 = col_move(after(far, pick0), dy=1), col_move(after(far, pick0), dy=-1)
+    b_up1, b_down1 = row_move(b_far, dx=1), row_move(b_far, dx=-1)
+    across1 = col_move(across0, dz=1)
+    b_across1 = row_move_by_core(by_core(b_up1, b_down1))
+    a_blocks = [a_own, up0, down0, across0, far, up1, down1, across1]
+    sent = [a_own, up0, down0, across0, far, up1, down1, across1]
+    a_blocks += [col_move(block, dc=1) for block in sent]
+    b_blocks = [b_own, b_up0, b_down0, b_across0, b_far, b_up1, b_down1, b_across1]
     vmem = pl.BlockSpec(memory_space=pltpu.VMEM)
     smem = pl.BlockSpec(memory_space=pltpu.SMEM)
     anywhere = pl.BlockSpec(memory_space=pl.ANY)
     i32 = jnp.int32
-    n_a, n_b = len(early), len(b_blocks)
-    acc, b_all, row_col, hot_k, slot_b, places = pl.pallas_call(
-        functools.partial(first_kernel, n_a, n_b),
-        out_shape=(
-            jax.ShapeDtypeStruct((CT + 1, TILE, TILE), jnp.float32),
-            jax.ShapeDtypeStruct((2 * n_b * B_ROWS, TILE), jnp.bfloat16),
-            jax.ShapeDtypeStruct((8, TILE), jnp.float32),
-            jax.ShapeDtypeStruct((KW, TILE), jnp.float32),
-            jax.ShapeDtypeStruct((8, TILE), jnp.float32),
-            jax.ShapeDtypeStruct((CT,), i32),
-        ),
-        in_specs=[smem] * 4 + [anywhere] * (n_a + n_b),
-        out_specs=(vmem,) * 5 + (smem,),
+    n_a, n_b, n_t = len(a_blocks), len(b_blocks), len(tokens)
+
+    def kernel(*refs):
+        inputs = 4 + n_a + n_b
+        product_kernel(n_a, n_b, *refs[:inputs], *refs[inputs + n_t:])
+
+    out = pl.pallas_call(
+        kernel,
+        out_shape=jax.ShapeDtypeStruct((RL * CL, TILE, TILE), jnp.bfloat16),
+        in_specs=[smem] * 4 + [anywhere] * (n_a + n_b + n_t),
+        out_specs=vmem,
         scratch_shapes=[
+            pltpu.VMEM((CT + 1, TILE, TILE), jnp.float32),
             pltpu.VMEM((n_a * A_ROWS, TILE), jnp.bfloat16),
+            pltpu.VMEM((n_b * B_ROWS, TILE), jnp.bfloat16),
             pltpu.VMEM((n_a, LABEL, TILE), jnp.bfloat16),
-            pltpu.VMEM((2 * n_b, LABEL, TILE), jnp.bfloat16),
+            pltpu.VMEM((n_b, LABEL, TILE), jnp.bfloat16),
             pltpu.VMEM((8, TILE), i32),
             pltpu.SMEM((MR,), i32),
             pltpu.SMEM((MC,), i32),
             pltpu.SMEM((MR,), i32),
             pltpu.SMEM((MC,), i32),
             pltpu.SMEM((RL * CL,), i32),
+            pltpu.SMEM((CT,), i32),
             pltpu.SMEM((8, TILE), i32),
             pltpu.SemaphoreType.DMA((n_a,)),
-            pltpu.SemaphoreType.DMA((2 * n_b,)),
-            pltpu.SemaphoreType.DMA((n_a + 2 * n_b,)),
+            pltpu.SemaphoreType.DMA((n_b,)),
+            pltpu.SemaphoreType.DMA((n_a + n_b,)),
             pltpu.SemaphoreType.DMA,
         ],
-        compiler_params=pltpu.CompilerParams(vmem_limit_bytes=16 << 20),
+        compiler_params=pltpu.CompilerParams(vmem_limit_bytes=20 << 20),
         cost_estimate=pl.CostEstimate(flops=3_000_000_000, bytes_accessed=14_000_000, transcendentals=0),
-    )(where, row_dist, col_dist, c_index, *early, *b_blocks)
-    n_late = len(late)
-    out = pl.pallas_call(
-        functools.partial(last_kernel, n_late),
-        out_shape=jax.ShapeDtypeStruct((RL * CL, TILE, TILE), jnp.bfloat16),
-        in_specs=[smem] + [vmem] * 5 + [anywhere] * n_late,
-        out_specs=vmem,
-        scratch_shapes=[
-            pltpu.VMEM((CT + 1, TILE, TILE), jnp.float32),
-            pltpu.VMEM((n_late * A_ROWS, TILE), jnp.bfloat16),
-            pltpu.VMEM((n_late, LABEL, TILE), jnp.bfloat16),
-            pltpu.VMEM((8, TILE), i32),
-            pltpu.SMEM((8, TILE), i32),
-            pltpu.SemaphoreType.DMA((n_late,)),
-            pltpu.SemaphoreType.DMA((n_late,)),
-            pltpu.SemaphoreType.DMA,
-        ],
-        compiler_params=pltpu.CompilerParams(vmem_limit_bytes=12 << 20),
-        cost_estimate=pl.CostEstimate(flops=500_000_000, bytes_accessed=8_000_000, transcendentals=0),
-    )(places, acc, b_all, row_col, hot_k, slot_b, *late)
+    )(where, row_dist, col_dist, c_index, *[pltpu.with_memory_space_constraint(x, pltpu.HBM) for x in a_blocks + b_blocks], *tokens)
     return out.reshape(RL, CL, TILE, TILE)
 
 

time: 85.3 us -> 68.9 us (0.81)
  starting transfers between devices: 34.5 us -> 43.3 us
  waiting for transfers between devices: 18.3 us -> 9.66 us
  local copies, waits for them, and re-layouts: 7.64 us -> 0.16 us
  other arithmetic: 5.57 us -> 0.21 us
  Pallas kernels: 18.2 us -> 15.2 us
    ppermute x15, waiting for transfers between devices: 16.5 us -> 6.65 us  [col_move(): return lax.ppermute(x, 'col', pairs)]
    unnamed x25 -> x35, local copies, waits for them, and re-layouts: 7.64 us -> 0.16 us
    ppermute x3 -> x5, starting transfers between devices: 3.56 us -> 8.09 us  [row_move(): return lax.ppermute(x, 'row', pairs)]
    pallas_call x2 -> x3, Pallas kernels: 18.2 us -> 15.2 us  [the longest x1 13.1 us: per_device(): pl.pallas_call(kernel, out_shape=jax.ShapeDtypeStruct((RL * CL, TILE, TIL...]
    ppermute x15, starting transfers between devices: 28.4 us -> 31 us  [col_move(): return lax.ppermute(x, 'col', pairs)]
    select_n x3, other arithmetic: 2.12 us -> 0.13 us  [by_core(): return jnp.where(core == 0, first, second)]
    concatenate x3 -> x0, other arithmetic: 1.97 us -> none  [the longest x2 1.92 us: with_labels(): return jnp.concatenate([tiles.reshape(n * TILE, TILE), labels])]
    ppermute x3 -> x5, waiting for transfers between devices: 1.09 us -> 3.01 us  [row_move(): return lax.ppermute(x, 'row', pairs)]
  transfers between devices with their start and end apart: 19 -> 22, of which waited for: 7 -> 6; matrix products, arithmetic and copies ran while one was open for 4% -> 0% of each run, Pallas kernels for 15% -> 2%
where the time goes in v3:
time: 68.9 us; the launch traced here: 68.7 us
  starting transfers between devices  43.3 us (63%)
  Pallas kernels  15.2 us (22%)
  waiting for transfers between devices  9.66 us (14%)
    ppermute x15, starting transfers between devices, col_move(): return lax.ppermute(x, 'col', pairs)  31 us
    pallas_call x1, Pallas kernels, per_device(): pl.pallas_call(kernel, out_shape=jax.ShapeDtypeStruct((RL * CL, TILE, TIL...  13.1 us
    ppermute x5, starting transfers between devices, row_move(): return lax.ppermute(x, 'row', pairs)  8.09 us
    ppermute x15, waiting for transfers between devices, col_move(): return lax.ppermute(x, 'col', pairs)  6.65 us
    ppermute x2, starting transfers between devices, row_move_by_core(): return lax.ppermute(x, ('row', 'col'), pairs)  4.14 us
    ppermute x5, waiting for transfers between devices, row_move(): return lax.ppermute(x, 'row', pairs)  3.01 us
    pallas_call x2, Pallas kernels, with_labels(): pl.pallas_call(label_kernel, out_shape=jax.ShapeDtypeStruct((n + LABEL, T...  2.09 us
  transfers between devices with their start and end apart: 22, of which 6 were waited for; matrix products, arithmetic and copies ran while one was open for 0% of the time, Pallas kernels for 2%

profile of v3, /device:TPU:1, one launch (start us, length us, event | category | flops | bytes accessed | tf_op | source)
XLA Modules:
  0.0 68.7 jit_solution(15544670390918773983)
XLA Ops:
  0.0 1.0 %shard_map.74.refs_20_ = bf16[1296,128]{1,0:T(8,128)(2,1)S(1)} custom-call(bf16[1280,128]{1,0:T(8,128)(2,1)} %bitcast.8, s32[2,10]{1,0:T(2,128)} %bitcast.9), custom_call_target="tpu_custom_call" | custom-call | tf_op jit(solution)/shard_map/pallas_call | solution.py:59
  1.0 2.5 %collective-permute-start.18 = (bf16[1296,128]{1,0:T(8,128)(2,1)S(1)}, bf16[1296,128]{1,0:T(8,128)(2,1)}, u32[]{:S(2)}, u32[]{:S(2)}) collective-permute-start(bf16[1296,128]{1,0:T(8,128)(2,1)S(1)} %shard_map.74.refs_20_), channel_id=1, source_target_pairs={{0,64},{16,80},{32,96},{48,112},{64,0},{80,16},{96,32},{112,48},{1... | collective-permute-start | bytes 995336 | tf_op jit(solution)/shard_map/ppermute | solution.py:44
  3.6 2.5 %collective-permute-start.16 = (bf16[1296,128]{1,0:T(8,128)(2,1)S(1)}, bf16[1296,128]{1,0:T(8,128)(2,1)S(1)}, u32[]{:S(2)}, u32[]{:S(2)}) collective-permute-start(bf16[1296,128]{1,0:T(8,128)(2,1)S(1)} %shard_map.74.refs_20_), channel_id=1, source_target_pairs={{0,48},{16,0},{32,16},{48,32},{64,112},{80,64},{96,80},{112,96},{1... | collective-permute-start | bytes 995336 | tf_op jit(solution)/shard_map/ppermute | solution.py:44
  6.1 1.1 %shard_map.73.refs_4_ = bf16[2192,128]{1,0:T(8,128)(2,1)S(1)} custom-call(bf16[2176,128]{1,0:T(8,128)(2,1)} %bitcast.7, s32[2,17]{1,0:T(2,128)} %bitcast.10), custom_call_target="tpu_custom_call" | custom-call | tf_op jit(solution)/shard_map/pallas_call | solution.py:59
  7.2 2.8 %collective-permute-start.1 = (bf16[2192,128]{1,0:T(8,128)(2,1)S(1)}, bf16[2192,128]{1,0:T(8,128)(2,1)S(1)}, u32[]{:S(2)}, u32[]{:S(2)}) collective-permute-start(bf16[2192,128]{1,0:T(8,128)(2,1)S(1)} %shard_map.73.refs_4_), channel_id=1, source_target_pairs={{0,12},{1,13},{2,14},{3,15},{4,0},{5,1},{6,2},{7,3},{8,4},{9,5},{1... | collective-permute-start | bytes 1683464 | tf_op jit(solution)/shard_map/ppermute | solution.py:36
  10.0 1.2 %collective-permute-done.18.refs_24_ = bf16[1296,128]{1,0:T(8,128)(2,1)} collective-permute-done((bf16[1296,128]{1,0:T(8,128)(2,1)S(1)}, bf16[1296,128]{1,0:T(8,128)(2,1)}, u32[]{:S(2)}, u32[]{:S(2)}) %collective-permute-start.18) | collective-permute-done | bytes 331808 | tf_op jit(solution)/shard_map/ppermute | solution.py:44
  11.2 1.3 %collective-permute-start.7 = (bf16[2192,128]{1,0:T(8,128)(2,1)S(1)}, bf16[2192,128]{1,0:T(8,128)(2,1)S(1)}, u32[]{:S(2)}, u32[]{:S(2)}) collective-permute-start(bf16[2192,128]{1,0:T(8,128)(2,1)S(1)} %shard_map.73.refs_4_), channel_id=1, source_target_pairs={{0,1},{1,0},{2,3},{3,2},{4,5},{5,4},{6,7},{7,6},{8,9},{9,8},{10,11... | collective-permute-start | bytes 1683464 | tf_op jit(solution)/shard_map/ppermute | solution.py:36
  12.4 3.4 %collective-permute-start.3 = (bf16[2192,128]{1,0:T(8,128)(2,1)S(1)}, bf16[2192,128]{1,0:T(8,128)(2,1)S(1)}, u32[]{:S(2)}, u32[]{:S(2)}) collective-permute-start(bf16[2192,128]{1,0:T(8,128)(2,1)S(1)} %shard_map.73.refs_4_), channel_id=1, source_target_pairs={{0,2},{1,3},{2,0},{3,1},{4,6},{5,7},{6,4},{7,5},{8,10},{9,11},{10,... | collective-permute-start | bytes 1683464 | tf_op jit(solution)/shard_map/ppermute | solution.py:36
  15.9 3.1 %collective-permute-start.20 = (bf16[1296,128]{1,0:T(8,128)(2,1)}, bf16[1296,128]{1,0:T(8,128)(2,1)S(1)}, u32[]{:S(2)}, u32[]{:S(2)}) collective-permute-start(bf16[1296,128]{1,0:T(8,128)(2,1)} %collective-permute-done.18.refs_24_), channel_id=1, source_target_pairs={{0,48},{16,0},{32,16},{48,32},{64,112},{80,64},{96,80},{112,96},{1... | collective-permute-start | bytes 995336 | tf_op jit(solution)/shard_map/ppermute | solution.py:44
  19.0 0.0 copy-start.16
  19.0 1.7 %collective-permute-done.1.refs_6_ = bf16[2192,128]{1,0:T(8,128)(2,1)S(1)} collective-permute-done((bf16[2192,128]{1,0:T(8,128)(2,1)S(1)}, bf16[2192,128]{1,0:T(8,128)(2,1)S(1)}, u32[]{:S(2)}, u32[]{:S(2)}) %collective-permute-start.1) | collective-permute-done | bytes 561184 | tf_op jit(solution)/shard_map/ppermute | solution.py:36
  20.7 3.1 %collective-permute-done.refs_5_ = bf16[2192,128]{1,0:T(8,128)(2,1)S(1)} collective-permute-done((bf16[2192,128]{1,0:T(8,128)(2,1)S(1)}, bf16[2192,128]{1,0:T(8,128)(2,1)S(1)}, u32[]{:S(2)}, u32[]{:S(2)}) %collective-permute-start) | collective-permute-done | bytes 561184 | tf_op jit(solution)/shard_map/ppermute | solution.py:36
  23.9 0.1 broadcast_select_fusion
  23.9 0.4 collective-permute-start.2
  24.3 3.2 %collective-permute-start.17 = (bf16[1296,128]{1,0:T(8,128)(2,1)S(1)}, bf16[1296,128]{1,0:T(8,128)(2,1)S(1)}, u32[]{:S(2)}, u32[]{:S(2)}) collective-permute-start(bf16[1296,128]{1,0:T(8,128)(2,1)S(1)} %broadcast_select_fusion.2), channel_id=1, source_target_pairs={{0,16},{1,49},{2,18},{3,51},{4,20},{5,53},{6,22},{7,55},{8,24},{9,... | collective-permute-start | bytes 995336 | tf_op jit(solution)/shard_map/ppermute | solution.py:53
  27.5 1.8 %collective-permute-done.19.refs_25_ = bf16[1296,128]{1,0:T(8,128)(2,1)S(1)} collective-permute-done((bf16[1296,128]{1,0:T(8,128)(2,1)}, bf16[1296,128]{1,0:T(8,128)(2,1)S(1)}, u32[]{:S(2)}, u32[]{:S(2)}) %collective-permute-start.19) | collective-permute-done | bytes 331808 | tf_op jit(solution)/shard_map/ppermute | solution.py:44
  29.4 1.0 %collective-permute-start.21 = (bf16[1296,128]{1,0:T(8,128)(2,1)S(1)}, bf16[1296,128]{1,0:T(8,128)(2,1)S(1)}, u32[]{:S(2)}, u32[]{:S(2)}) collective-permute-start(bf16[1296,128]{1,0:T(8,128)(2,1)S(1)} %broadcast_select_fusion.1), channel_id=1, source_target_pairs={{0,16},{1,49},{2,18},{3,51},{4,20},{5,53},{6,22},{7,55},{8,24},{9,... | collective-permute-start | bytes 995336 | tf_op jit(solution)/shard_map/ppermute | solution.py:53
  30.3 2.3 %collective-permute-start.11 = (bf16[2192,128]{1,0:T(8,128)(2,1)S(1)}, bf16[2192,128]{1,0:T(8,128)(2,1)S(1)}, u32[]{:S(2)}, u32[]{:S(2)}) collective-permute-start(bf16[2192,128]{1,0:T(8,128)(2,1)S(1)} %collective-permute-done.3.refs_8_), channel_id=1, source_target_pairs={{0,1},{1,0},{2,3},{3,2},{4,5},{5,4},{6,7},{7,6},{8,9},{9,8},{10,11... | collective-permute-start | bytes 1683464 | tf_op jit(solution)/shard_map/ppermute | solution.py:36
  32.6 0.1 collective-permute-start.9
  32.7 3.4 %collective-permute-start.5 = (bf16[2192,128]{1,0:T(8,128)(2,1)S(1)}, bf16[2192,128]{1,0:T(8,128)(2,1)}, u32[]{:S(2)}, u32[]{:S(2)}) collective-permute-start(bf16[2192,128]{1,0:T(8,128)(2,1)S(1)} %collective-permute-done.3.refs_8_), channel_id=1, source_target_pairs={{0,12},{1,13},{2,14},{3,15},{4,0},{5,1},{6,2},{7,3},{8,4},{9,5},{1... | collective-permute-start | bytes 1683464 | tf_op jit(solution)/shard_map/ppermute | solution.py:36
  36.2 0.3 collective-permute-start.4
  36.5 3.1 %collective-permute-start.6 = (bf16[2192,128]{1,0:T(8,128)(2,1)}, bf16[2192,128]{1,0:T(8,128)(2,1)}, u32[]{:S(2)}, u32[]{:S(2)}) collective-permute-start(bf16[2192,128]{1,0:T(8,128)(2,1)} %collective-permute-done.2.refs_7_), channel_id=1, source_target_pairs={{0,2},{1,3},{2,0},{3,1},{4,6},{5,7},{6,4},{7,5},{8,10},{9,11},{10,... | collective-permute-start | bytes 1683464 | tf_op jit(solution)/shard_map/ppermute | solution.py:36
  39.6 5.9 %collective-permute-start.8 = (bf16[2192,128]{1,0:T(8,128)(2,1)S(1)}, bf16[2192,128]{1,0:T(8,128)(2,1)}, u32[]{:S(2)}, u32[]{:S(2)}) collective-permute-start(bf16[2192,128]{1,0:T(8,128)(2,1)S(1)} %collective-permute-done.refs_5_), channel_id=1, source_target_pairs={{0,1},{1,0},{2,3},{3,2},{4,5},{5,4},{6,7},{7,6},{8,9},{9,8},{10,11... | collective-permute-start | bytes 1683464 | tf_op jit(solution)/shard_map/ppermute | solution.py:36
  45.5 0.1 collective-permute-start.10
  45.6 3.5 %collective-permute-start.13 = (bf16[2192,128]{1,0:T(8,128)(2,1)}, bf16[2192,128]{1,0:T(8,128)(2,1)}, u32[]{:S(2)}, u32[]{:S(2)}) collective-permute-start(bf16[2192,128]{1,0:T(8,128)(2,1)} %collective-permute-done.5.refs_10_), channel_id=1, source_target_pairs={{0,1},{1,0},{2,3},{3,2},{4,5},{5,4},{6,7},{7,6},{8,9},{9,8},{10,11... | collective-permute-start | bytes 1683464 | tf_op jit(solution)/shard_map/ppermute | solution.py:36
  49.1 3.6 %collective-permute-start.12 = (bf16[2192,128]{1,0:T(8,128)(2,1)}, bf16[2192,128]{1,0:T(8,128)(2,1)}, u32[]{:S(2)}, u32[]{:S(2)}) collective-permute-start(bf16[2192,128]{1,0:T(8,128)(2,1)} %collective-permute-done.4.refs_9_), channel_id=1, source_target_pairs={{0,1},{1,0},{2,3},{3,2},{4,5},{5,4},{6,7},{7,6},{8,9},{9,8},{10,11... | collective-permute-start | bytes 1683464 | tf_op jit(solution)/shard_map/ppermute | solution.py:36
  52.7 0.9 %collective-permute-start.14 = (bf16[2192,128]{1,0:T(8,128)(2,1)}, bf16[2192,128]{1,0:T(8,128)(2,1)}, u32[]{:S(2)}, u32[]{:S(2)}) collective-permute-start(bf16[2192,128]{1,0:T(8,128)(2,1)} %collective-permute-done.6.refs_11_), channel_id=1, source_target_pairs={{0,1},{1,0},{2,3},{3,2},{4,5},{5,4},{6,7},{7,6},{8,9},{9,8},{10,11... | collective-permute-start | bytes 1683464 | tf_op jit(solution)/shard_map/ppermute | solution.py:36
  53.6 0.1 copy.8.refs_3_
  53.7 0.1 pad_add_fusion.refs_0_
  53.8 0.9 %collective-permute-done.12.refs_17_ = bf16[2192,128]{1,0:T(8,128)(2,1)} collective-permute-done((bf16[2192,128]{1,0:T(8,128)(2,1)}, bf16[2192,128]{1,0:T(8,128)(2,1)}, u32[]{:S(2)}, u32[]{:S(2)}) %collective-permute-start.12) | collective-permute-done | bytes 561184 | tf_op jit(solution)/shard_map/ppermute | solution.py:36
  54.6 0.9 %collective-permute-done.14.refs_19_ = bf16[2192,128]{1,0:T(8,128)(2,1)} collective-permute-done((bf16[2192,128]{1,0:T(8,128)(2,1)}, bf16[2192,128]{1,0:T(8,128)(2,1)}, u32[]{:S(2)}, u32[]{:S(2)}) %collective-permute-start.14) | collective-permute-done | bytes 561184 | tf_op jit(solution)/shard_map/ppermute | solution.py:36
  55.6 13.1 %shard_map.75 = bf16[48,128,128]{2,1,0:T(8,128)(2,1)} custom-call(s32[2]{0:T(128)S(1)} %pad_add_fusion.refs_0_, s32[64]{0:T(128)S(1)} %copy-done.2, s32[96]{0:T(128)S(1)} %copy-done.3, s32[24,2]{1,0:T(8,128)S(1)} %copy.8.refs_3_, bf16[2192,128]{1,0:T(8,128)(2,1)} %copy-done, bf16[2192,128]{1,0:T(8,128)(2,1)} %copy-done.5, bf16[2192,128]{1,0:T(8,128)(2,1)} %copy-done.4, ...), custom_call_target="tpu_custom_call" | custom-call | flops 3000000000 | bytes 14000000 | tf_op jit(solution)/shard_map/pallas_call | solution.py:301
  (55 shorter events, 0.2 us)
Async XLA Ops:
  1.0 22.9 %copy-start.1 = (bf16[1296,128]{1,0:T(8,128)(2,1)}, bf16[1296,128]{1,0:T(8,128)(2,1)S(1)}, u32[]{:S(2)}) copy-start(bf16[1296,128]{1,0:T(8,128)(2,1)S(1)} %shard_map.74.refs_20_) | copy-start | bytes 995332
  1.0 10.2 %collective-permute-start.18 = (bf16[1296,128]{1,0:T(8,128)(2,1)S(1)}, bf16[1296,128]{1,0:T(8,128)(2,1)}, u32[]{:S(2)}, u32[]{:S(2)}) collective-permute-start(bf16[1296,128]{1,0:T(8,128)(2,1)S(1)} %shard_map.74.refs_20_), channel_id=1, source_target_pairs={{0,64},{16,80},{32,96},{48,112},{64,0},{80,16},{96,32},{112,48},{1... | collective-permute-start | bytes 995336 | tf_op jit(solution)/shard_map/ppermute | solution.py:44
  3.6 8.9 %collective-permute-start.16 = (bf16[1296,128]{1,0:T(8,128)(2,1)S(1)}, bf16[1296,128]{1,0:T(8,128)(2,1)S(1)}, u32[]{:S(2)}, u32[]{:S(2)}) collective-permute-start(bf16[1296,128]{1,0:T(8,128)(2,1)S(1)} %shard_map.74.refs_20_), channel_id=1, source_target_pairs={{0,48},{16,0},{32,16},{48,32},{64,112},{80,64},{96,80},{112,96},{1... | collective-permute-start | bytes 995336 | tf_op jit(solution)/shard_map/ppermute | solution.py:44
  6.0 9.8 %collective-permute-start.15 = (bf16[1296,128]{1,0:T(8,128)(2,1)S(1)}, bf16[1296,128]{1,0:T(8,128)(2,1)S(1)}, u32[]{:S(2)}, u32[]{:S(2)}) collective-permute-start(bf16[1296,128]{1,0:T(8,128)(2,1)S(1)} %shard_map.74.refs_20_), channel_id=1, source_target_pairs={{0,16},{16,32},{32,48},{48,0},{64,80},{80,96},{96,112},{112,64},{1... | collective-permute-start | bytes 995336 | tf_op jit(solution)/shard_map/ppermute | solution.py:44
  7.1 22.2 %copy-start = (bf16[2192,128]{1,0:T(8,128)(2,1)}, bf16[2192,128]{1,0:T(8,128)(2,1)S(1)}, u32[]{:S(2)}) copy-start(bf16[2192,128]{1,0:T(8,128)(2,1)S(1)} %shard_map.73.refs_4_) | copy-start | bytes 1683460
  7.2 13.6 %collective-permute-start.1 = (bf16[2192,128]{1,0:T(8,128)(2,1)S(1)}, bf16[2192,128]{1,0:T(8,128)(2,1)S(1)}, u32[]{:S(2)}, u32[]{:S(2)}) collective-permute-start(bf16[2192,128]{1,0:T(8,128)(2,1)S(1)} %shard_map.73.refs_4_), channel_id=1, source_target_pairs={{0,12},{1,13},{2,14},{3,15},{4,0},{5,1},{6,2},{7,3},{8,4},{9,5},{1... | collective-permute-start | bytes 1683464 | tf_op jit(solution)/shard_map/ppermute | solution.py:36
  10.0 13.9 %collective-permute-start = (bf16[2192,128]{1,0:T(8,128)(2,1)S(1)}, bf16[2192,128]{1,0:T(8,128)(2,1)S(1)}, u32[]{:S(2)}, u32[]{:S(2)}) collective-permute-start(bf16[2192,128]{1,0:T(8,128)(2,1)S(1)} %shard_map.73.refs_4_), channel_id=1, source_target_pairs={{0,4},{1,5},{2,6},{3,7},{4,8},{5,9},{6,10},{7,11},{8,12},{9,13},{1... | collective-permute-start | bytes 1683464 | tf_op jit(solution)/shard_map/ppermute | solution.py:36
  11.2 21.4 %collective-permute-start.7 = (bf16[2192,128]{1,0:T(8,128)(2,1)S(1)}, bf16[2192,128]{1,0:T(8,128)(2,1)S(1)}, u32[]{:S(2)}, u32[]{:S(2)}) collective-permute-start(bf16[2192,128]{1,0:T(8,128)(2,1)S(1)} %shard_map.73.refs_4_), channel_id=1, source_target_pairs={{0,1},{1,0},{2,3},{3,2},{4,5},{5,4},{6,7},{7,6},{8,9},{9,8},{10,11... | collective-permute-start | bytes 1683464 | tf_op jit(solution)/shard_map/ppermute | solution.py:36
  12.4 16.9 %copy-start.6 = (bf16[1296,128]{1,0:T(8,128)(2,1)}, bf16[1296,128]{1,0:T(8,128)(2,1)S(1)}, u32[]{:S(2)}) copy-start(bf16[1296,128]{1,0:T(8,128)(2,1)S(1)} %collective-permute-done.16.refs_22_) | copy-start | bytes 995332
  12.4 17.9 %collective-permute-start.3 = (bf16[2192,128]{1,0:T(8,128)(2,1)S(1)}, bf16[2192,128]{1,0:T(8,128)(2,1)S(1)}, u32[]{:S(2)}, u32[]{:S(2)}) collective-permute-start(bf16[2192,128]{1,0:T(8,128)(2,1)S(1)} %shard_map.73.refs_4_), channel_id=1, source_target_pairs={{0,2},{1,3},{2,0},{3,1},{4,6},{5,7},{6,4},{7,5},{8,10},{9,11},{10,... | collective-permute-start | bytes 1683464 | tf_op jit(solution)/shard_map/ppermute | solution.py:36
  15.9 8.5 %collective-permute-start.20 = (bf16[1296,128]{1,0:T(8,128)(2,1)}, bf16[1296,128]{1,0:T(8,128)(2,1)S(1)}, u32[]{:S(2)}, u32[]{:S(2)}) collective-permute-start(bf16[1296,128]{1,0:T(8,128)(2,1)} %collective-permute-done.18.refs_24_), channel_id=1, source_target_pairs={{0,48},{16,0},{32,16},{48,32},{64,112},{80,64},{96,80},{112,96},{1... | collective-permute-start | bytes 995336 | tf_op jit(solution)/shard_map/ppermute | solution.py:44
  19.0 34.6 %copy-start.16 = (s32[24,2]{0,1:T(2,128)S(1)}, s32[24,2]{0,1:T(2,128)}, u32[]{:S(2)}) copy-start(s32[24,2]{0,1:T(2,128)} %param.13) | copy-start | bytes 580
  19.0 36.6 %copy-start.2 = (s32[64]{0:T(128)S(1)}, s32[64]{0:T(128)}, u32[]{:S(2)}) copy-start(s32[64]{0:T(128)} %refs_1_.1) | copy-start | bytes 772
  19.0 36.6 %copy-start.3 = (s32[96]{0:T(128)S(1)}, s32[96]{0:T(128)}, u32[]{:S(2)}) copy-start(s32[96]{0:T(128)} %refs_2_.1) | copy-start | bytes 1156
  20.7 34.8 %copy-start.4 = (bf16[2192,128]{1,0:T(8,128)(2,1)}, bf16[2192,128]{1,0:T(8,128)(2,1)S(1)}, u32[]{:S(2)}) copy-start(bf16[2192,128]{1,0:T(8,128)(2,1)S(1)} %collective-permute-done.1.refs_6_) | copy-start | bytes 1683460
  20.7 8.6 %collective-permute-start.19 = (bf16[1296,128]{1,0:T(8,128)(2,1)}, bf16[1296,128]{1,0:T(8,128)(2,1)S(1)}, u32[]{:S(2)}, u32[]{:S(2)}) collective-permute-start(bf16[1296,128]{1,0:T(8,128)(2,1)} %collective-permute-done.18.refs_24_), channel_id=1, source_target_pairs={{0,16},{16,32},{32,48},{48,0},{64,80},{80,96},{96,112},{112,64},{1... | collective-permute-start | bytes 995336 | tf_op jit(solution)/shard_map/ppermute | solution.py:44
  23.9 31.7 %copy-start.5 = (bf16[2192,128]{1,0:T(8,128)(2,1)}, bf16[2192,128]{1,0:T(8,128)(2,1)S(1)}, u32[]{:S(2)}) copy-start(bf16[2192,128]{1,0:T(8,128)(2,1)S(1)} %collective-permute-done.refs_5_) | copy-start | bytes 1683460
  23.9 12.5 %collective-permute-start.2 = (bf16[2192,128]{1,0:T(8,128)(2,1)S(1)}, bf16[2192,128]{1,0:T(8,128)(2,1)}, u32[]{:S(2)}, u32[]{:S(2)}) collective-permute-start(bf16[2192,128]{1,0:T(8,128)(2,1)S(1)} %broadcast_select_fusion), channel_id=1, source_target_pairs={{0,4},{1,13},{2,6},{3,15},{4,8},{5,1},{6,10},{7,3},{8,12},{9,5},{1... | collective-permute-start | bytes 1683464 | tf_op jit(solution)/shard_map/ppermute | solution.py:36
  24.3 31.2 %copy-start.8 = (bf16[1296,128]{1,0:T(8,128)(2,1)}, bf16[1296,128]{1,0:T(8,128)(2,1)S(1)}, u32[]{:S(2)}) copy-start(bf16[1296,128]{1,0:T(8,128)(2,1)S(1)} %collective-permute-done.20.refs_26_) | copy-start | bytes 995332
  24.3 8.4 %collective-permute-start.17 = (bf16[1296,128]{1,0:T(8,128)(2,1)S(1)}, bf16[1296,128]{1,0:T(8,128)(2,1)S(1)}, u32[]{:S(2)}, u32[]{:S(2)}) collective-permute-start(bf16[1296,128]{1,0:T(8,128)(2,1)S(1)} %broadcast_select_fusion.2), channel_id=1, source_target_pairs={{0,16},{1,49},{2,18},{3,51},{4,20},{5,53},{6,22},{7,55},{8,24},{9,... | collective-permute-start | bytes 995336 | tf_op jit(solution)/shard_map/ppermute | solution.py:53
  29.3 26.2 %copy-start.9 = (bf16[1296,128]{1,0:T(8,128)(2,1)}, bf16[1296,128]{1,0:T(8,128)(2,1)S(1)}, u32[]{:S(2)}) copy-start(bf16[1296,128]{1,0:T(8,128)(2,1)S(1)} %collective-permute-done.19.refs_25_) | copy-start | bytes 995332
  29.4 6.8 %collective-permute-start.21 = (bf16[1296,128]{1,0:T(8,128)(2,1)S(1)}, bf16[1296,128]{1,0:T(8,128)(2,1)S(1)}, u32[]{:S(2)}, u32[]{:S(2)}) collective-permute-start(bf16[1296,128]{1,0:T(8,128)(2,1)S(1)} %broadcast_select_fusion.1), channel_id=1, source_target_pairs={{0,16},{1,49},{2,18},{3,51},{4,20},{5,53},{6,22},{7,55},{8,24},{9,... | collective-permute-start | bytes 995336 | tf_op jit(solution)/shard_map/ppermute | solution.py:53
  30.3 9.3 %collective-permute-start.11 = (bf16[2192,128]{1,0:T(8,128)(2,1)S(1)}, bf16[2192,128]{1,0:T(8,128)(2,1)S(1)}, u32[]{:S(2)}, u32[]{:S(2)}) collective-permute-start(bf16[2192,128]{1,0:T(8,128)(2,1)S(1)} %collective-permute-done.3.refs_8_), channel_id=1, source_target_pairs={{0,1},{1,0},{2,3},{3,2},{4,5},{5,4},{6,7},{7,6},{8,9},{9,8},{10,11... | collective-permute-start | bytes 1683464 | tf_op jit(solution)/shard_map/ppermute | solution.py:36
  32.6 12.9 %collective-permute-start.9 = (bf16[2192,128]{1,0:T(8,128)(2,1)S(1)}, bf16[2192,128]{1,0:T(8,128)(2,1)S(1)}, u32[]{:S(2)}, u32[]{:S(2)}) collective-permute-start(bf16[2192,128]{1,0:T(8,128)(2,1)S(1)} %collective-permute-done.1.refs_6_), channel_id=1, source_target_pairs={{0,1},{1,0},{2,3},{3,2},{4,5},{5,4},{6,7},{7,6},{8,9},{9,8},{10,11... | collective-permute-start | bytes 1683464 | tf_op jit(solution)/shard_map/ppermute | solution.py:36
  32.7 12.9 %collective-permute-start.5 = (bf16[2192,128]{1,0:T(8,128)(2,1)S(1)}, bf16[2192,128]{1,0:T(8,128)(2,1)}, u32[]{:S(2)}, u32[]{:S(2)}) collective-permute-start(bf16[2192,128]{1,0:T(8,128)(2,1)S(1)} %collective-permute-done.3.refs_8_), channel_id=1, source_target_pairs={{0,12},{1,13},{2,14},{3,15},{4,0},{5,1},{6,2},{7,3},{8,4},{9,5},{1... | collective-permute-start | bytes 1683464 | tf_op jit(solution)/shard_map/ppermute | solution.py:36
  36.2 12.9 %collective-permute-start.4 = (bf16[2192,128]{1,0:T(8,128)(2,1)S(1)}, bf16[2192,128]{1,0:T(8,128)(2,1)}, u32[]{:S(2)}, u32[]{:S(2)}) collective-permute-start(bf16[2192,128]{1,0:T(8,128)(2,1)S(1)} %collective-permute-done.3.refs_8_), channel_id=1, source_target_pairs={{0,4},{1,5},{2,6},{3,7},{4,8},{5,9},{6,10},{7,11},{8,12},{9,13},{1... | collective-permute-start | bytes 1683464 | tf_op jit(solution)/shard_map/ppermute | solution.py:36
  36.5 16.3 %collective-permute-start.6 = (bf16[2192,128]{1,0:T(8,128)(2,1)}, bf16[2192,128]{1,0:T(8,128)(2,1)}, u32[]{:S(2)}, u32[]{:S(2)}) collective-permute-start(bf16[2192,128]{1,0:T(8,128)(2,1)} %collective-permute-done.2.refs_7_), channel_id=1, source_target_pairs={{0,2},{1,3},{2,0},{3,1},{4,6},{5,7},{6,4},{7,5},{8,10},{9,11},{10,... | collective-permute-start | bytes 1683464 | tf_op jit(solution)/shard_map/ppermute | solution.py:36
  39.6 14.1 %collective-permute-start.8 = (bf16[2192,128]{1,0:T(8,128)(2,1)S(1)}, bf16[2192,128]{1,0:T(8,128)(2,1)}, u32[]{:S(2)}, u32[]{:S(2)}) collective-permute-start(bf16[2192,128]{1,0:T(8,128)(2,1)S(1)} %collective-permute-done.refs_5_), channel_id=1, source_target_pairs={{0,1},{1,0},{2,3},{3,2},{4,5},{5,4},{6,7},{7,6},{8,9},{9,8},{10,11... | collective-permute-start | bytes 1683464 | tf_op jit(solution)/shard_map/ppermute | solution.py:36
  45.5 9.2 %collective-permute-start.10 = (bf16[2192,128]{1,0:T(8,128)(2,1)}, bf16[2192,128]{1,0:T(8,128)(2,1)}, u32[]{:S(2)}, u32[]{:S(2)}) collective-permute-start(bf16[2192,128]{1,0:T(8,128)(2,1)} %collective-permute-done.2.refs_7_), channel_id=1, source_target_pairs={{0,1},{1,0},{2,3},{3,2},{4,5},{5,4},{6,7},{7,6},{8,9},{9,8},{10,11... | collective-permute-start | bytes 1683464 | tf_op jit(solution)/shard_map/ppermute | solution.py:36
  45.6 8.2 %collective-permute-start.13 = (bf16[2192,128]{1,0:T(8,128)(2,1)}, bf16[2192,128]{1,0:T(8,128)(2,1)}, u32[]{:S(2)}, u32[]{:S(2)}) collective-permute-start(bf16[2192,128]{1,0:T(8,128)(2,1)} %collective-permute-done.5.refs_10_), channel_id=1, source_target_pairs={{0,1},{1,0},{2,3},{3,2},{4,5},{5,4},{6,7},{7,6},{8,9},{9,8},{10,11... | collective-permute-start | bytes 1683464 | tf_op jit(solution)/shard_map/ppermute | solution.py:36
  49.1 5.6 %collective-permute-start.12 = (bf16[2192,128]{1,0:T(8,128)(2,1)}, bf16[2192,128]{1,0:T(8,128)(2,1)}, u32[]{:S(2)}, u32[]{:S(2)}) collective-permute-start(bf16[2192,128]{1,0:T(8,128)(2,1)} %collective-permute-done.4.refs_9_), channel_id=1, source_target_pairs={{0,1},{1,0},{2,3},{3,2},{4,5},{5,4},{6,7},{7,6},{8,9},{9,8},{10,11... | collective-permute-start | bytes 1683464 | tf_op jit(solution)/shard_map/ppermute | solution.py:36
  52.7 2.8 %collective-permute-start.14 = (bf16[2192,128]{1,0:T(8,128)(2,1)}, bf16[2192,128]{1,0:T(8,128)(2,1)}, u32[]{:S(2)}, u32[]{:S(2)}) collective-permute-start(bf16[2192,128]{1,0:T(8,128)(2,1)} %collective-permute-done.6.refs_11_), channel_id=1, source_target_pairs={{0,1},{1,0},{2,3},{3,2},{4,5},{5,4},{6,7},{7,6},{8,9},{9,8},{10,11... | collective-permute-start | bytes 1683464 | tf_op jit(solution)/shard_map/ppermute | solution.py:36
  (7 other events, 100.5 us)

commit v4 on v3

--- a/solution.py
+++ b/solution.py
@@ -24,7 +24,7 @@
 A_BLOCK = A_ROWS + LABEL
 B_BLOCK = B_ROWS + LABEL
 LIST = 640
-GROUP = 8
+GROUP = 32
 
 
 def col_move(x, dy=0, dz=0, dc=0, by_core=False):
@@ -280,13 +280,13 @@
     b_pick0 = by_core(b_up0, b_down0)
     b_across0 = row_move_by_core(after(b_pick0, pick0))
     b_far = row_move(b_own, dz=1)
-    up1, down1 = col_move(after(far, pick0), dy=1), col_move(after(far, pick0), dy=-1)
+    far_sent = after(far, pick0)
+    up1, down1 = col_move(far_sent, dy=1), col_move(far_sent, dy=-1)
     b_up1, b_down1 = row_move(b_far, dx=1), row_move(b_far, dx=-1)
     across1 = col_move(across0, dz=1)
     b_across1 = row_move_by_core(by_core(b_up1, b_down1))
     a_blocks = [a_own, up0, down0, across0, far, up1, down1, across1]
-    sent = [a_own, up0, down0, across0, far, up1, down1, across1]
-    a_blocks += [col_move(block, dc=1) for block in sent]
+    a_blocks += [col_move(block, dc=1) for block in a_blocks]
     b_blocks = [b_own, b_up0, b_down0, b_across0, b_far, b_up1, b_down1, b_across1]
     vmem = pl.BlockSpec(memory_space=pltpu.VMEM)
     smem = pl.BlockSpec(memory_space=pltpu.SMEM)

time: 68.9 us -> 66.6 us (0.967)
  Pallas kernels: 15.2 us -> 12.4 us
    pallas_call x1, Pallas kernels: 13.1 us -> 10.3 us  [per_device(): pl.pallas_call(kernel, out_shape=jax.ShapeDtypeStruct((RL * CL, TILE, TIL...]
where the time goes in v4:
time: 66.6 us; the launch traced here: 65.9 us
  starting transfers between devices  43.3 us (65%)
  Pallas kernels  12.4 us (19%)
  waiting for transfers between devices  9.66 us (15%)
    ppermute x15, starting transfers between devices, col_move(): return lax.ppermute(x, 'col', pairs)  31 us
    pallas_call x1, Pallas kernels, per_device(): pl.pallas_call(kernel, out_shape=jax.ShapeDtypeStruct((RL * CL, TILE, TIL...  10.3 us
    ppermute x5, starting transfers between devices, row_move(): return lax.ppermute(x, 'row', pairs)  8.09 us
    ppermute x15, waiting for transfers between devices, col_move(): return lax.ppermute(x, 'col', pairs)  6.65 us
    ppermute x2, starting transfers between devices, row_move_by_core(): return lax.ppermute(x, ('row', 'col'), pairs)  4.14 us
    ppermute x5, waiting for transfers between devices, row_move(): return lax.ppermute(x, 'row', pairs)  3.01 us
    pallas_call x2, Pallas kernels, with_labels(): pl.pallas_call(label_kernel, out_shape=jax.ShapeDtypeStruct((n + LABEL, T...  2.09 us
  transfers between devices with their start and end apart: 22, of which 6 were waited for; matrix products, arithmetic and copies ran while one was open for 0% of the time, Pallas kernels for 2%

profile of v4, /device:TPU:1, one launch (start us, length us, event | category | flops | bytes accessed | tf_op | source)
XLA Modules:
  0.0 65.9 jit_solution(18286878090104782381)
XLA Ops:
  0.0 1.0 %shard_map.74.refs_20_ = bf16[1296,128]{1,0:T(8,128)(2,1)S(1)} custom-call(bf16[1280,128]{1,0:T(8,128)(2,1)} %bitcast.8, s32[2,10]{1,0:T(2,128)} %bitcast.9), custom_call_target="tpu_custom_call" | custom-call | tf_op jit(solution)/shard_map/pallas_call | solution.py:59
  1.0 2.5 %collective-permute-start.18 = (bf16[1296,128]{1,0:T(8,128)(2,1)S(1)}, bf16[1296,128]{1,0:T(8,128)(2,1)}, u32[]{:S(2)}, u32[]{:S(2)}) collective-permute-start(bf16[1296,128]{1,0:T(8,128)(2,1)S(1)} %shard_map.74.refs_20_), channel_id=1, source_target_pairs={{0,64},{16,80},{32,96},{48,112},{64,0},{80,16},{96,32},{112,48},{1... | collective-permute-start | bytes 995336 | tf_op jit(solution)/shard_map/ppermute | solution.py:44
  3.6 2.5 %collective-permute-start.16 = (bf16[1296,128]{1,0:T(8,128)(2,1)S(1)}, bf16[1296,128]{1,0:T(8,128)(2,1)S(1)}, u32[]{:S(2)}, u32[]{:S(2)}) collective-permute-start(bf16[1296,128]{1,0:T(8,128)(2,1)S(1)} %shard_map.74.refs_20_), channel_id=1, source_target_pairs={{0,48},{16,0},{32,16},{48,32},{64,112},{80,64},{96,80},{112,96},{1... | collective-permute-start | bytes 995336 | tf_op jit(solution)/shard_map/ppermute | solution.py:44
  6.1 1.1 %shard_map.73.refs_4_ = bf16[2192,128]{1,0:T(8,128)(2,1)S(1)} custom-call(bf16[2176,128]{1,0:T(8,128)(2,1)} %bitcast.7, s32[2,17]{1,0:T(2,128)} %bitcast.10), custom_call_target="tpu_custom_call" | custom-call | tf_op jit(solution)/shard_map/pallas_call | solution.py:59
  7.2 2.8 %collective-permute-start.1 = (bf16[2192,128]{1,0:T(8,128)(2,1)S(1)}, bf16[2192,128]{1,0:T(8,128)(2,1)S(1)}, u32[]{:S(2)}, u32[]{:S(2)}) collective-permute-start(bf16[2192,128]{1,0:T(8,128)(2,1)S(1)} %shard_map.73.refs_4_), channel_id=1, source_target_pairs={{0,12},{1,13},{2,14},{3,15},{4,0},{5,1},{6,2},{7,3},{8,4},{9,5},{1... | collective-permute-start | bytes 1683464 | tf_op jit(solution)/shard_map/ppermute | solution.py:36
  10.0 1.2 %collective-permute-done.18.refs_24_ = bf16[1296,128]{1,0:T(8,128)(2,1)} collective-permute-done((bf16[1296,128]{1,0:T(8,128)(2,1)S(1)}, bf16[1296,128]{1,0:T(8,128)(2,1)}, u32[]{:S(2)}, u32[]{:S(2)}) %collective-permute-start.18) | collective-permute-done | bytes 331808 | tf_op jit(solution)/shard_map/ppermute | solution.py:44
  11.2 1.3 %collective-permute-start.7 = (bf16[2192,128]{1,0:T(8,128)(2,1)S(1)}, bf16[2192,128]{1,0:T(8,128)(2,1)S(1)}, u32[]{:S(2)}, u32[]{:S(2)}) collective-permute-start(bf16[2192,128]{1,0:T(8,128)(2,1)S(1)} %shard_map.73.refs_4_), channel_id=1, source_target_pairs={{0,1},{1,0},{2,3},{3,2},{4,5},{5,4},{6,7},{7,6},{8,9},{9,8},{10,11... | collective-permute-start | bytes 1683464 | tf_op jit(solution)/shard_map/ppermute | solution.py:36
  12.4 3.4 %collective-permute-start.3 = (bf16[2192,128]{1,0:T(8,128)(2,1)S(1)}, bf16[2192,128]{1,0:T(8,128)(2,1)S(1)}, u32[]{:S(2)}, u32[]{:S(2)}) collective-permute-start(bf16[2192,128]{1,0:T(8,128)(2,1)S(1)} %shard_map.73.refs_4_), channel_id=1, source_target_pairs={{0,2},{1,3},{2,0},{3,1},{4,6},{5,7},{6,4},{7,5},{8,10},{9,11},{10,... | collective-permute-start | bytes 1683464 | tf_op jit(solution)/shard_map/ppermute | solution.py:36
  15.9 3.1 %collective-permute-start.20 = (bf16[1296,128]{1,0:T(8,128)(2,1)}, bf16[1296,128]{1,0:T(8,128)(2,1)S(1)}, u32[]{:S(2)}, u32[]{:S(2)}) collective-permute-start(bf16[1296,128]{1,0:T(8,128)(2,1)} %collective-permute-done.18.refs_24_), channel_id=1, source_target_pairs={{0,48},{16,0},{32,16},{48,32},{64,112},{80,64},{96,80},{112,96},{1... | collective-permute-start | bytes 995336 | tf_op jit(solution)/shard_map/ppermute | solution.py:44
  19.0 0.0 copy-start.2
  19.0 1.7 %collective-permute-done.1.refs_6_ = bf16[2192,128]{1,0:T(8,128)(2,1)S(1)} collective-permute-done((bf16[2192,128]{1,0:T(8,128)(2,1)S(1)}, bf16[2192,128]{1,0:T(8,128)(2,1)S(1)}, u32[]{:S(2)}, u32[]{:S(2)}) %collective-permute-start.1) | collective-permute-done | bytes 561184 | tf_op jit(solution)/shard_map/ppermute | solution.py:36
  20.7 3.1 %collective-permute-done.refs_5_ = bf16[2192,128]{1,0:T(8,128)(2,1)S(1)} collective-permute-done((bf16[2192,128]{1,0:T(8,128)(2,1)S(1)}, bf16[2192,128]{1,0:T(8,128)(2,1)S(1)}, u32[]{:S(2)}, u32[]{:S(2)}) %collective-permute-start) | collective-permute-done | bytes 561184 | tf_op jit(solution)/shard_map/ppermute | solution.py:36
  23.9 0.1 broadcast_select_fusion
  23.9 0.4 collective-permute-start.2
  24.3 3.2 %collective-permute-start.17 = (bf16[1296,128]{1,0:T(8,128)(2,1)S(1)}, bf16[1296,128]{1,0:T(8,128)(2,1)S(1)}, u32[]{:S(2)}, u32[]{:S(2)}) collective-permute-start(bf16[1296,128]{1,0:T(8,128)(2,1)S(1)} %broadcast_select_fusion.2), channel_id=1, source_target_pairs={{0,16},{1,49},{2,18},{3,51},{4,20},{5,53},{6,22},{7,55},{8,24},{9,... | collective-permute-start | bytes 995336 | tf_op jit(solution)/shard_map/ppermute | solution.py:53
  27.5 1.8 %collective-permute-done.19.refs_25_ = bf16[1296,128]{1,0:T(8,128)(2,1)S(1)} collective-permute-done((bf16[1296,128]{1,0:T(8,128)(2,1)}, bf16[1296,128]{1,0:T(8,128)(2,1)S(1)}, u32[]{:S(2)}, u32[]{:S(2)}) %collective-permute-start.19) | collective-permute-done | bytes 331808 | tf_op jit(solution)/shard_map/ppermute | solution.py:44
  29.4 1.0 %collective-permute-start.21 = (bf16[1296,128]{1,0:T(8,128)(2,1)S(1)}, bf16[1296,128]{1,0:T(8,128)(2,1)S(1)}, u32[]{:S(2)}, u32[]{:S(2)}) collective-permute-start(bf16[1296,128]{1,0:T(8,128)(2,1)S(1)} %broadcast_select_fusion.1), channel_id=1, source_target_pairs={{0,16},{1,49},{2,18},{3,51},{4,20},{5,53},{6,22},{7,55},{8,24},{9,... | collective-permute-start | bytes 995336 | tf_op jit(solution)/shard_map/ppermute | solution.py:53
  30.3 2.3 %collective-permute-start.11 = (bf16[2192,128]{1,0:T(8,128)(2,1)S(1)}, bf16[2192,128]{1,0:T(8,128)(2,1)S(1)}, u32[]{:S(2)}, u32[]{:S(2)}) collective-permute-start(bf16[2192,128]{1,0:T(8,128)(2,1)S(1)} %collective-permute-done.3.refs_8_), channel_id=1, source_target_pairs={{0,1},{1,0},{2,3},{3,2},{4,5},{5,4},{6,7},{7,6},{8,9},{9,8},{10,11... | collective-permute-start | bytes 1683464 | tf_op jit(solution)/shard_map/ppermute | solution.py:36
  32.6 0.1 collective-permute-start.9
  32.7 3.4 %collective-permute-start.5 = (bf16[2192,128]{1,0:T(8,128)(2,1)S(1)}, bf16[2192,128]{1,0:T(8,128)(2,1)}, u32[]{:S(2)}, u32[]{:S(2)}) collective-permute-start(bf16[2192,128]{1,0:T(8,128)(2,1)S(1)} %collective-permute-done.3.refs_8_), channel_id=1, source_target_pairs={{0,12},{1,13},{2,14},{3,15},{4,0},{5,1},{6,2},{7,3},{8,4},{9,5},{1... | collective-permute-start | bytes 1683464 | tf_op jit(solution)/shard_map/ppermute | solution.py:36
  36.2 0.3 collective-permute-start.4
  36.5 3.1 %collective-permute-start.6 = (bf16[2192,128]{1,0:T(8,128)(2,1)}, bf16[2192,128]{1,0:T(8,128)(2,1)}, u32[]{:S(2)}, u32[]{:S(2)}) collective-permute-start(bf16[2192,128]{1,0:T(8,128)(2,1)} %collective-permute-done.2.refs_7_), channel_id=1, source_target_pairs={{0,2},{1,3},{2,0},{3,1},{4,6},{5,7},{6,4},{7,5},{8,10},{9,11},{10,... | collective-permute-start | bytes 1683464 | tf_op jit(solution)/shard_map/ppermute | solution.py:36
  39.6 5.9 %collective-permute-start.8 = (bf16[2192,128]{1,0:T(8,128)(2,1)S(1)}, bf16[2192,128]{1,0:T(8,128)(2,1)}, u32[]{:S(2)}, u32[]{:S(2)}) collective-permute-start(bf16[2192,128]{1,0:T(8,128)(2,1)S(1)} %collective-permute-done.refs_5_), channel_id=1, source_target_pairs={{0,1},{1,0},{2,3},{3,2},{4,5},{5,4},{6,7},{7,6},{8,9},{9,8},{10,11... | collective-permute-start | bytes 1683464 | tf_op jit(solution)/shard_map/ppermute | solution.py:36
  45.5 0.1 collective-permute-start.10
  45.6 3.5 %collective-permute-start.13 = (bf16[2192,128]{1,0:T(8,128)(2,1)}, bf16[2192,128]{1,0:T(8,128)(2,1)}, u32[]{:S(2)}, u32[]{:S(2)}) collective-permute-start(bf16[2192,128]{1,0:T(8,128)(2,1)} %collective-permute-done.5.refs_10_), channel_id=1, source_target_pairs={{0,1},{1,0},{2,3},{3,2},{4,5},{5,4},{6,7},{7,6},{8,9},{9,8},{10,11... | collective-permute-start | bytes 1683464 | tf_op jit(solution)/shard_map/ppermute | solution.py:36
  49.1 3.6 %collective-permute-start.12 = (bf16[2192,128]{1,0:T(8,128)(2,1)}, bf16[2192,128]{1,0:T(8,128)(2,1)}, u32[]{:S(2)}, u32[]{:S(2)}) collective-permute-start(bf16[2192,128]{1,0:T(8,128)(2,1)} %collective-permute-done.4.refs_9_), channel_id=1, source_target_pairs={{0,1},{1,0},{2,3},{3,2},{4,5},{5,4},{6,7},{7,6},{8,9},{9,8},{10,11... | collective-permute-start | bytes 1683464 | tf_op jit(solution)/shard_map/ppermute | solution.py:36
  52.7 0.9 %collective-permute-start.14 = (bf16[2192,128]{1,0:T(8,128)(2,1)}, bf16[2192,128]{1,0:T(8,128)(2,1)}, u32[]{:S(2)}, u32[]{:S(2)}) collective-permute-start(bf16[2192,128]{1,0:T(8,128)(2,1)} %collective-permute-done.6.refs_11_), channel_id=1, source_target_pairs={{0,1},{1,0},{2,3},{3,2},{4,5},{5,4},{6,7},{7,6},{8,9},{9,8},{10,11... | collective-permute-start | bytes 1683464 | tf_op jit(solution)/shard_map/ppermute | solution.py:36
  53.6 0.1 copy.8.refs_3_
  53.7 0.1 pad_add_fusion.refs_0_
  53.8 0.9 %collective-permute-done.12.refs_17_ = bf16[2192,128]{1,0:T(8,128)(2,1)} collective-permute-done((bf16[2192,128]{1,0:T(8,128)(2,1)}, bf16[2192,128]{1,0:T(8,128)(2,1)}, u32[]{:S(2)}, u32[]{:S(2)}) %collective-permute-start.12) | collective-permute-done | bytes 561184 | tf_op jit(solution)/shard_map/ppermute | solution.py:36
  54.6 0.9 %collective-permute-done.14.refs_19_ = bf16[2192,128]{1,0:T(8,128)(2,1)} collective-permute-done((bf16[2192,128]{1,0:T(8,128)(2,1)}, bf16[2192,128]{1,0:T(8,128)(2,1)}, u32[]{:S(2)}, u32[]{:S(2)}) %collective-permute-start.14) | collective-permute-done | bytes 561184 | tf_op jit(solution)/shard_map/ppermute | solution.py:36
  55.6 10.3 %shard_map.75 = bf16[48,128,128]{2,1,0:T(8,128)(2,1)} custom-call(s32[2]{0:T(128)S(1)} %pad_add_fusion.refs_0_, s32[64]{0:T(128)S(1)} %copy-done.2, s32[96]{0:T(128)S(1)} %copy-done.3, s32[24,2]{1,0:T(8,128)S(1)} %copy.8.refs_3_, bf16[2192,128]{1,0:T(8,128)(2,1)} %copy-done, bf16[2192,128]{1,0:T(8,128)(2,1)} %copy-done.5, bf16[2192,128]{1,0:T(8,128)(2,1)} %copy-done.4, ...), custom_call_target="tpu_custom_call" | custom-call | flops 3000000000 | bytes 14000000 | tf_op jit(solution)/shard_map/pallas_call | solution.py:301
  (55 shorter events, 0.2 us)
Async XLA Ops:
  1.0 22.9 %copy-start.1 = (bf16[1296,128]{1,0:T(8,128)(2,1)}, bf16[1296,128]{1,0:T(8,128)(2,1)S(1)}, u32[]{:S(2)}) copy-start(bf16[1296,128]{1,0:T(8,128)(2,1)S(1)} %shard_map.74.refs_20_) | copy-start | bytes 995332
  1.0 10.2 %collective-permute-start.18 = (bf16[1296,128]{1,0:T(8,128)(2,1)S(1)}, bf16[1296,128]{1,0:T(8,128)(2,1)}, u32[]{:S(2)}, u32[]{:S(2)}) collective-permute-start(bf16[1296,128]{1,0:T(8,128)(2,1)S(1)} %shard_map.74.refs_20_), channel_id=1, source_target_pairs={{0,64},{16,80},{32,96},{48,112},{64,0},{80,16},{96,32},{112,48},{1... | collective-permute-start | bytes 995336 | tf_op jit(solution)/shard_map/ppermute | solution.py:44
  3.6 8.9 %collective-permute-start.16 = (bf16[1296,128]{1,0:T(8,128)(2,1)S(1)}, bf16[1296,128]{1,0:T(8,128)(2,1)S(1)}, u32[]{:S(2)}, u32[]{:S(2)}) collective-permute-start(bf16[1296,128]{1,0:T(8,128)(2,1)S(1)} %shard_map.74.refs_20_), channel_id=1, source_target_pairs={{0,48},{16,0},{32,16},{48,32},{64,112},{80,64},{96,80},{112,96},{1... | collective-permute-start | bytes 995336 | tf_op jit(solution)/shard_map/ppermute | solution.py:44
  6.0 9.8 %collective-permute-start.15 = (bf16[1296,128]{1,0:T(8,128)(2,1)S(1)}, bf16[1296,128]{1,0:T(8,128)(2,1)S(1)}, u32[]{:S(2)}, u32[]{:S(2)}) collective-permute-start(bf16[1296,128]{1,0:T(8,128)(2,1)S(1)} %shard_map.74.refs_20_), channel_id=1, source_target_pairs={{0,16},{16,32},{32,48},{48,0},{64,80},{80,96},{96,112},{112,64},{1... | collective-permute-start | bytes 995336 | tf_op jit(solution)/shard_map/ppermute | solution.py:44
  7.1 22.2 %copy-start = (bf16[2192,128]{1,0:T(8,128)(2,1)}, bf16[2192,128]{1,0:T(8,128)(2,1)S(1)}, u32[]{:S(2)}) copy-start(bf16[2192,128]{1,0:T(8,128)(2,1)S(1)} %shard_map.73.refs_4_) | copy-start | bytes 1683460
  7.2 13.6 %collective-permute-start.1 = (bf16[2192,128]{1,0:T(8,128)(2,1)S(1)}, bf16[2192,128]{1,0:T(8,128)(2,1)S(1)}, u32[]{:S(2)}, u32[]{:S(2)}) collective-permute-start(bf16[2192,128]{1,0:T(8,128)(2,1)S(1)} %shard_map.73.refs_4_), channel_id=1, source_target_pairs={{0,12},{1,13},{2,14},{3,15},{4,0},{5,1},{6,2},{7,3},{8,4},{9,5},{1... | collective-permute-start | bytes 1683464 | tf_op jit(solution)/shard_map/ppermute | solution.py:36
  10.0 13.9 %collective-permute-start = (bf16[2192,128]{1,0:T(8,128)(2,1)S(1)}, bf16[2192,128]{1,0:T(8,128)(2,1)S(1)}, u32[]{:S(2)}, u32[]{:S(2)}) collective-permute-start(bf16[2192,128]{1,0:T(8,128)(2,1)S(1)} %shard_map.73.refs_4_), channel_id=1, source_target_pairs={{0,4},{1,5},{2,6},{3,7},{4,8},{5,9},{6,10},{7,11},{8,12},{9,13},{1... | collective-permute-start | bytes 1683464 | tf_op jit(solution)/shard_map/ppermute | solution.py:36
  11.2 21.4 %collective-permute-start.7 = (bf16[2192,128]{1,0:T(8,128)(2,1)S(1)}, bf16[2192,128]{1,0:T(8,128)(2,1)S(1)}, u32[]{:S(2)}, u32[]{:S(2)}) collective-permute-start(bf16[2192,128]{1,0:T(8,128)(2,1)S(1)} %shard_map.73.refs_4_), channel_id=1, source_target_pairs={{0,1},{1,0},{2,3},{3,2},{4,5},{5,4},{6,7},{7,6},{8,9},{9,8},{10,11... | collective-permute-start | bytes 1683464 | tf_op jit(solution)/shard_map/ppermute | solution.py:36
  12.4 16.9 %copy-start.6 = (bf16[1296,128]{1,0:T(8,128)(2,1)}, bf16[1296,128]{1,0:T(8,128)(2,1)S(1)}, u32[]{:S(2)}) copy-start(bf16[1296,128]{1,0:T(8,128)(2,1)S(1)} %collective-permute-done.16.refs_22_) | copy-start | bytes 995332
  12.4 17.9 %collective-permute-start.3 = (bf16[2192,128]{1,0:T(8,128)(2,1)S(1)}, bf16[2192,128]{1,0:T(8,128)(2,1)S(1)}, u32[]{:S(2)}, u32[]{:S(2)}) collective-permute-start(bf16[2192,128]{1,0:T(8,128)(2,1)S(1)} %shard_map.73.refs_4_), channel_id=1, source_target_pairs={{0,2},{1,3},{2,0},{3,1},{4,6},{5,7},{6,4},{7,5},{8,10},{9,11},{10,... | collective-permute-start | bytes 1683464 | tf_op jit(solution)/shard_map/ppermute | solution.py:36
  15.9 8.5 %collective-permute-start.20 = (bf16[1296,128]{1,0:T(8,128)(2,1)}, bf16[1296,128]{1,0:T(8,128)(2,1)S(1)}, u32[]{:S(2)}, u32[]{:S(2)}) collective-permute-start(bf16[1296,128]{1,0:T(8,128)(2,1)} %collective-permute-done.18.refs_24_), channel_id=1, source_target_pairs={{0,48},{16,0},{32,16},{48,32},{64,112},{80,64},{96,80},{112,96},{1... | collective-permute-start | bytes 995336 | tf_op jit(solution)/shard_map/ppermute | solution.py:44
  19.0 34.6 %copy-start.16 = (s32[24,2]{0,1:T(2,128)S(1)}, s32[24,2]{0,1:T(2,128)}, u32[]{:S(2)}) copy-start(s32[24,2]{0,1:T(2,128)} %param.13) | copy-start | bytes 580
  19.0 36.6 %copy-start.2 = (s32[64]{0:T(128)S(1)}, s32[64]{0:T(128)}, u32[]{:S(2)}) copy-start(s32[64]{0:T(128)} %refs_1_.1) | copy-start | bytes 772
  19.0 36.6 %copy-start.3 = (s32[96]{0:T(128)S(1)}, s32[96]{0:T(128)}, u32[]{:S(2)}) copy-start(s32[96]{0:T(128)} %refs_2_.1) | copy-start | bytes 1156
  20.7 34.8 %copy-start.4 = (bf16[2192,128]{1,0:T(8,128)(2,1)}, bf16[2192,128]{1,0:T(8,128)(2,1)S(1)}, u32[]{:S(2)}) copy-start(bf16[2192,128]{1,0:T(8,128)(2,1)S(1)} %collective-permute-done.1.refs_6_) | copy-start | bytes 1683460
  20.7 8.6 %collective-permute-start.19 = (bf16[1296,128]{1,0:T(8,128)(2,1)}, bf16[1296,128]{1,0:T(8,128)(2,1)S(1)}, u32[]{:S(2)}, u32[]{:S(2)}) collective-permute-start(bf16[1296,128]{1,0:T(8,128)(2,1)} %collective-permute-done.18.refs_24_), channel_id=1, source_target_pairs={{0,16},{16,32},{32,48},{48,0},{64,80},{80,96},{96,112},{112,64},{1... | collective-permute-start | bytes 995336 | tf_op jit(solution)/shard_map/ppermute | solution.py:44
  23.9 31.7 %copy-start.5 = (bf16[2192,128]{1,0:T(8,128)(2,1)}, bf16[2192,128]{1,0:T(8,128)(2,1)S(1)}, u32[]{:S(2)}) copy-start(bf16[2192,128]{1,0:T(8,128)(2,1)S(1)} %collective-permute-done.refs_5_) | copy-start | bytes 1683460
  23.9 12.5 %collective-permute-start.2 = (bf16[2192,128]{1,0:T(8,128)(2,1)S(1)}, bf16[2192,128]{1,0:T(8,128)(2,1)}, u32[]{:S(2)}, u32[]{:S(2)}) collective-permute-start(bf16[2192,128]{1,0:T(8,128)(2,1)S(1)} %broadcast_select_fusion), channel_id=1, source_target_pairs={{0,4},{1,13},{2,6},{3,15},{4,8},{5,1},{6,10},{7,3},{8,12},{9,5},{1... | collective-permute-start | bytes 1683464 | tf_op jit(solution)/shard_map/ppermute | solution.py:36
  24.3 31.2 %copy-start.8 = (bf16[1296,128]{1,0:T(8,128)(2,1)}, bf16[1296,128]{1,0:T(8,128)(2,1)S(1)}, u32[]{:S(2)}) copy-start(bf16[1296,128]{1,0:T(8,128)(2,1)S(1)} %collective-permute-done.20.refs_26_) | copy-start | bytes 995332
  24.3 8.4 %collective-permute-start.17 = (bf16[1296,128]{1,0:T(8,128)(2,1)S(1)}, bf16[1296,128]{1,0:T(8,128)(2,1)S(1)}, u32[]{:S(2)}, u32[]{:S(2)}) collective-permute-start(bf16[1296,128]{1,0:T(8,128)(2,1)S(1)} %broadcast_select_fusion.2), channel_id=1, source_target_pairs={{0,16},{1,49},{2,18},{3,51},{4,20},{5,53},{6,22},{7,55},{8,24},{9,... | collective-permute-start | bytes 995336 | tf_op jit(solution)/shard_map/ppermute | solution.py:53
  29.3 26.2 %copy-start.9 = (bf16[1296,128]{1,0:T(8,128)(2,1)}, bf16[1296,128]{1,0:T(8,128)(2,1)S(1)}, u32[]{:S(2)}) copy-start(bf16[1296,128]{1,0:T(8,128)(2,1)S(1)} %collective-permute-done.19.refs_25_) | copy-start | bytes 995332
  29.4 6.8 %collective-permute-start.21 = (bf16[1296,128]{1,0:T(8,128)(2,1)S(1)}, bf16[1296,128]{1,0:T(8,128)(2,1)S(1)}, u32[]{:S(2)}, u32[]{:S(2)}) collective-permute-start(bf16[1296,128]{1,0:T(8,128)(2,1)S(1)} %broadcast_select_fusion.1), channel_id=1, source_target_pairs={{0,16},{1,49},{2,18},{3,51},{4,20},{5,53},{6,22},{7,55},{8,24},{9,... | collective-permute-start | bytes 995336 | tf_op jit(solution)/shard_map/ppermute | solution.py:53
  30.3 9.3 %collective-permute-start.11 = (bf16[2192,128]{1,0:T(8,128)(2,1)S(1)}, bf16[2192,128]{1,0:T(8,128)(2,1)S(1)}, u32[]{:S(2)}, u32[]{:S(2)}) collective-permute-start(bf16[2192,128]{1,0:T(8,128)(2,1)S(1)} %collective-permute-done.3.refs_8_), channel_id=1, source_target_pairs={{0,1},{1,0},{2,3},{3,2},{4,5},{5,4},{6,7},{7,6},{8,9},{9,8},{10,11... | collective-permute-start | bytes 1683464 | tf_op jit(solution)/shard_map/ppermute | solution.py:36
  32.6 12.9 %collective-permute-start.9 = (bf16[2192,128]{1,0:T(8,128)(2,1)S(1)}, bf16[2192,128]{1,0:T(8,128)(2,1)S(1)}, u32[]{:S(2)}, u32[]{:S(2)}) collective-permute-start(bf16[2192,128]{1,0:T(8,128)(2,1)S(1)} %collective-permute-done.1.refs_6_), channel_id=1, source_target_pairs={{0,1},{1,0},{2,3},{3,2},{4,5},{5,4},{6,7},{7,6},{8,9},{9,8},{10,11... | collective-permute-start | bytes 1683464 | tf_op jit(solution)/shard_map/ppermute | solution.py:36
  32.7 12.9 %collective-permute-start.5 = (bf16[2192,128]{1,0:T(8,128)(2,1)S(1)}, bf16[2192,128]{1,0:T(8,128)(2,1)}, u32[]{:S(2)}, u32[]{:S(2)}) collective-permute-start(bf16[2192,128]{1,0:T(8,128)(2,1)S(1)} %collective-permute-done.3.refs_8_), channel_id=1, source_target_pairs={{0,12},{1,13},{2,14},{3,15},{4,0},{5,1},{6,2},{7,3},{8,4},{9,5},{1... | collective-permute-start | bytes 1683464 | tf_op jit(solution)/shard_map/ppermute | solution.py:36
  36.2 12.9 %collective-permute-start.4 = (bf16[2192,128]{1,0:T(8,128)(2,1)S(1)}, bf16[2192,128]{1,0:T(8,128)(2,1)}, u32[]{:S(2)}, u32[]{:S(2)}) collective-permute-start(bf16[2192,128]{1,0:T(8,128)(2,1)S(1)} %collective-permute-done.3.refs_8_), channel_id=1, source_target_pairs={{0,4},{1,5},{2,6},{3,7},{4,8},{5,9},{6,10},{7,11},{8,12},{9,13},{1... | collective-permute-start | bytes 1683464 | tf_op jit(solution)/shard_map/ppermute | solution.py:36
  36.5 16.3 %collective-permute-start.6 = (bf16[2192,128]{1,0:T(8,128)(2,1)}, bf16[2192,128]{1,0:T(8,128)(2,1)}, u32[]{:S(2)}, u32[]{:S(2)}) collective-permute-start(bf16[2192,128]{1,0:T(8,128)(2,1)} %collective-permute-done.2.refs_7_), channel_id=1, source_target_pairs={{0,2},{1,3},{2,0},{3,1},{4,6},{5,7},{6,4},{7,5},{8,10},{9,11},{10,... | collective-permute-start | bytes 1683464 | tf_op jit(solution)/shard_map/ppermute | solution.py:36
  39.6 14.1 %collective-permute-start.8 = (bf16[2192,128]{1,0:T(8,128)(2,1)S(1)}, bf16[2192,128]{1,0:T(8,128)(2,1)}, u32[]{:S(2)}, u32[]{:S(2)}) collective-permute-start(bf16[2192,128]{1,0:T(8,128)(2,1)S(1)} %collective-permute-done.refs_5_), channel_id=1, source_target_pairs={{0,1},{1,0},{2,3},{3,2},{4,5},{5,4},{6,7},{7,6},{8,9},{9,8},{10,11... | collective-permute-start | bytes 1683464 | tf_op jit(solution)/shard_map/ppermute | solution.py:36
  45.5 9.2 %collective-permute-start.10 = (bf16[2192,128]{1,0:T(8,128)(2,1)}, bf16[2192,128]{1,0:T(8,128)(2,1)}, u32[]{:S(2)}, u32[]{:S(2)}) collective-permute-start(bf16[2192,128]{1,0:T(8,128)(2,1)} %collective-permute-done.2.refs_7_), channel_id=1, source_target_pairs={{0,1},{1,0},{2,3},{3,2},{4,5},{5,4},{6,7},{7,6},{8,9},{9,8},{10,11... | collective-permute-start | bytes 1683464 | tf_op jit(solution)/shard_map/ppermute | solution.py:36
  45.6 8.2 %collective-permute-start.13 = (bf16[2192,128]{1,0:T(8,128)(2,1)}, bf16[2192,128]{1,0:T(8,128)(2,1)}, u32[]{:S(2)}, u32[]{:S(2)}) collective-permute-start(bf16[2192,128]{1,0:T(8,128)(2,1)} %collective-permute-done.5.refs_10_), channel_id=1, source_target_pairs={{0,1},{1,0},{2,3},{3,2},{4,5},{5,4},{6,7},{7,6},{8,9},{9,8},{10,11... | collective-permute-start | bytes 1683464 | tf_op jit(solution)/shard_map/ppermute | solution.py:36
  49.1 5.6 %collective-permute-start.12 = (bf16[2192,128]{1,0:T(8,128)(2,1)}, bf16[2192,128]{1,0:T(8,128)(2,1)}, u32[]{:S(2)}, u32[]{:S(2)}) collective-permute-start(bf16[2192,128]{1,0:T(8,128)(2,1)} %collective-permute-done.4.refs_9_), channel_id=1, source_target_pairs={{0,1},{1,0},{2,3},{3,2},{4,5},{5,4},{6,7},{7,6},{8,9},{9,8},{10,11... | collective-permute-start | bytes 1683464 | tf_op jit(solution)/shard_map/ppermute | solution.py:36
  52.7 2.8 %collective-permute-start.14 = (bf16[2192,128]{1,0:T(8,128)(2,1)}, bf16[2192,128]{1,0:T(8,128)(2,1)}, u32[]{:S(2)}, u32[]{:S(2)}) collective-permute-start(bf16[2192,128]{1,0:T(8,128)(2,1)} %collective-permute-done.6.refs_11_), channel_id=1, source_target_pairs={{0,1},{1,0},{2,3},{3,2},{4,5},{5,4},{6,7},{7,6},{8,9},{9,8},{10,11... | collective-permute-start | bytes 1683464 | tf_op jit(solution)/shard_map/ppermute | solution.py:36
  (7 other events, 100.5 us)

commit v5 on v4

--- a/solution.py
+++ b/solution.py
@@ -24,6 +24,7 @@
 A_BLOCK = A_ROWS + LABEL
 B_BLOCK = B_ROWS + LABEL
 LIST = 640
+LAST = (5, 6, 7, 13, 14, 15)
 GROUP = 32
 
 
@@ -53,21 +54,25 @@
     return lax.ppermute(x, ("row", "col"), pairs)
 
 
-def with_labels(tiles, index):
-    n = tiles.shape[0] * TILE
-    inputs = [pltpu.with_memory_space_constraint(x, pltpu.HBM) for x in (tiles.reshape(n, TILE), index.T)]
-    return pl.pallas_call(
-        label_kernel,
-        out_shape=jax.ShapeDtypeStruct((n + LABEL, TILE), jnp.bfloat16),
-        in_specs=[pl.BlockSpec(memory_space=pl.ANY)] * 2,
-        out_specs=pl.BlockSpec(memory_space=pltpu.VMEM),
-        scratch_shapes=[
+def with_labels(a_tiles, a_index, b_tiles, b_index):
+    inputs, shapes, scratch = [], [], []
+    for tiles, index in ((a_tiles, a_index), (b_tiles, b_index)):
+        n = tiles.shape[0] * TILE
+        inputs += [tiles.reshape(n, TILE), index.T]
+        shapes.append(jax.ShapeDtypeStruct((n + LABEL, TILE), jnp.bfloat16))
+        scratch += [
             pltpu.VMEM((2, tiles.shape[0]), jnp.int32),
             pltpu.VMEM((LABEL, TILE), jnp.float32),
             pltpu.SemaphoreType.DMA((2,)),
-        ],
-        compiler_params=pltpu.CompilerParams(vmem_limit_bytes=2 << 20),
-    )(*inputs)
+        ]
+    return pl.pallas_call(
+        label_kernel,
+        out_shape=tuple(shapes),
+        in_specs=[pl.BlockSpec(memory_space=pl.ANY)] * 4,
+        out_specs=(pl.BlockSpec(memory_space=pltpu.VMEM),) * 2,
+        scratch_shapes=scratch,
+        compiler_params=pltpu.CompilerParams(vmem_limit_bytes=3 << 20),
+    )(*[pltpu.with_memory_space_constraint(x, pltpu.HBM) for x in inputs])
 
 
 def copy_blocks(pieces, sems):
@@ -244,17 +249,31 @@
     lax.fori_loop(0, CT, finish, 0, unroll=4)
 
 
-def label_kernel(tiles_ref, index_ref, out_ref, index_v, labels_ref, sems):
-    n = tiles_ref.shape[0]
-    tiles_copy = pltpu.make_async_copy(tiles_ref, out_ref.at[pl.ds(0, n)], sems.at[0])
-    index_copy = pltpu.make_async_copy(index_ref, index_v, sems.at[1])
-    index_copy.start()
-    tiles_copy.start()
-    labels_ref[...] = jnp.zeros_like(labels_ref)
-    index_copy.wait()
-    labels_ref[0:2, 0:n // TILE] = index_v[...].astype(jnp.float32)
-    out_ref[n:n + LABEL] = labels_ref[...].astype(jnp.bfloat16)
-    tiles_copy.wait()
+def label_kernel(
+    a_ref, a_index_ref, b_ref, b_index_ref, a_out, b_out,
+    a_index_v, a_labels, a_sems, b_index_v, b_labels, b_sems,
+):
+    sides = (
+        (a_ref, a_index_ref, a_out, a_index_v, a_labels, a_sems),
+        (b_ref, b_index_ref, b_out, b_index_v, b_labels, b_sems),
+    )
+    waits = []
+    for tiles_ref, index_ref, out_ref, index_v, labels_ref, sems in sides:
+        n = tiles_ref.shape[0]
+        index_copy = pltpu.make_async_copy(index_ref, index_v, sems.at[1])
+        index_copy.start()
+        tiles_copy = pltpu.make_async_copy(tiles_ref, out_ref.at[pl.ds(0, n)], sems.at[0])
+        tiles_copy.start()
+        labels_ref[...] = jnp.zeros_like(labels_ref)
+        waits.append((tiles_copy, index_copy))
+    for (tiles_copy, index_copy), side in zip(waits, sides):
+        tiles_ref, _, out_ref, index_v, labels_ref, _ = side
+        n = tiles_ref.shape[0]
+        index_copy.wait()
+        labels_ref[0:2, 0:n // TILE] = index_v[...].astype(jnp.float32)
+        out_ref[n:n + LABEL] = labels_ref[...].astype(jnp.bfloat16)
+    for tiles_copy, _ in waits:
+        tiles_copy.wait()
 
 
 def per_device(a_tiles, a_index, b_tiles, b_index, row_dist, col_dist, c_index):
@@ -270,29 +289,36 @@
         tokens.extend(tied[1:])
         return tied[0]
 
-    a_own = with_labels(a_tiles, a_index)
-    b_own = with_labels(b_tiles, b_index)
+    a_own, b_own = with_labels(a_tiles, a_index, b_tiles, b_index)
+    b_far = row_move(b_own, dz=1)
+    b_first = b_own
+    far = col_move(a_own, dz=1)
     up0, down0 = col_move(a_own, dy=1), col_move(a_own, dy=-1)
-    far = col_move(a_own, dz=1)
-    b_up0, b_down0 = row_move(b_own, dx=1), row_move(b_own, dx=-1)
+    b_up0, b_down0 = row_move(b_first, dx=1), row_move(b_first, dx=-1)
     pick0 = by_core(up0, down0)
     across0 = col_move(pick0, dy=1, by_core=True)
     b_pick0 = by_core(b_up0, b_down0)
     b_across0 = row_move_by_core(after(b_pick0, pick0))
-    b_far = row_move(b_own, dz=1)
+    b_sent = b_far
+    b_up1, b_down1 = row_move(b_sent, dx=1), row_move(b_sent, dx=-1)
     far_sent = after(far, pick0)
     up1, down1 = col_move(far_sent, dy=1), col_move(far_sent, dy=-1)
-    b_up1, b_down1 = row_move(b_far, dx=1), row_move(b_far, dx=-1)
+    b_across1 = row_move_by_core(by_core(b_up1, b_down1))
     across1 = col_move(across0, dz=1)
-    b_across1 = row_move_by_core(by_core(b_up1, b_down1))
     a_blocks = [a_own, up0, down0, across0, far, up1, down1, across1]
-    a_blocks += [col_move(block, dc=1) for block in a_blocks]
+    sent = [a_own, up0, down0, across0, far, up1, down1, across1]
+    a_blocks += [col_move(block, dc=1) for block in sent]
     b_blocks = [b_own, b_up0, b_down0, b_across0, b_far, b_up1, b_down1, b_across1]
     vmem = pl.BlockSpec(memory_space=pltpu.VMEM)
     smem = pl.BlockSpec(memory_space=pltpu.SMEM)
     anywhere = pl.BlockSpec(memory_space=pl.ANY)
     i32 = jnp.int32
     n_a, n_b, n_t = len(a_blocks), len(b_blocks), len(tokens)
+
+    placed = [
+        x if n in LAST else pltpu.with_memory_space_constraint(x, pltpu.HBM)
+        for n, x in enumerate(a_blocks + b_blocks)
+    ]
 
     def kernel(*refs):
         inputs = 4 + n_a + n_b
@@ -324,7 +350,7 @@
         ],
         compiler_params=pltpu.CompilerParams(vmem_limit_bytes=20 << 20),
         cost_estimate=pl.CostEstimate(flops=3_000_000_000, bytes_accessed=14_000_000, transcendentals=0),
-    )(where, row_dist, col_dist, c_index, *[pltpu.with_memory_space_constraint(x, pltpu.HBM) for x in a_blocks + b_blocks], *tokens)
+    )(where, row_dist, col_dist, c_index, *placed, *tokens)
     return out.reshape(RL, CL, TILE, TILE)
 
 

time: 66.6 us -> 64.1 us (0.962)
  Pallas kernels: 12.4 us -> 10.2 us
  starting transfers between devices: 43.3 us -> 44.2 us
    ppermute x15, waiting for transfers between devices: 6.65 us -> 5.22 us  [col_move(): return lax.ppermute(x, 'col', pairs)]
    pallas_call x1, Pallas kernels: 10.3 us -> 9 us  [per_device(): pl.pallas_call(kernel, out_shape=jax.ShapeDtypeStruct((RL * CL, TILE, TIL...]
    pallas_call x2 -> x1, Pallas kernels: 2.09 us -> 1.21 us  [with_labels(): pl.pallas_call(label_kernel, out_shape=tuple(shapes), in_specs=[pl.BlockS...]
  transfers between devices with their start and end apart: 22 -> 22, of which waited for: 6 -> 8; matrix products, arithmetic and copies ran while one was open for 0% -> 0% of each run, Pallas kernels for 2% -> 0%
where the time goes in v5:
time: 64.1 us; the launch traced here: 64 us
  starting transfers between devices  44.2 us (69%)
  Pallas kernels  10.2 us (16%)
  waiting for transfers between devices  9.05 us (14%)
    ppermute x15, starting transfers between devices, col_move(): return lax.ppermute(x, 'col', pairs)  31.5 us
    pallas_call x1, Pallas kernels, per_device(): pl.pallas_call(kernel, out_shape=jax.ShapeDtypeStruct((RL * CL, TILE, TIL...  9 us
    ppermute x5, starting transfers between devices, row_move(): return lax.ppermute(x, 'row', pairs)  8.19 us
    ppermute x15, waiting for transfers between devices, col_move(): return lax.ppermute(x, 'col', pairs)  5.22 us
    ppermute x2, starting transfers between devices, row_move_by_core(): return lax.ppermute(x, ('row', 'col'), pairs)  4.49 us
    ppermute x5, waiting for transfers between devices, row_move(): return lax.ppermute(x, 'row', pairs)  3.53 us
  transfers between devices with their start and end apart: 22, of which 8 were waited for; matrix products, arithmetic and copies ran while one was open for 0% of the time, Pallas kernels for 0%

profile of v5, /device:TPU:1, one launch (start us, length us, event | category | flops | bytes accessed | tf_op | source)
XLA Modules:
  0.0 64.0 jit_solution(554740585808380306)
XLA Ops:
  0.0 1.2 %shard_map.73 = (bf16[2192,128]{1,0:T(8,128)(2,1)S(1)}, bf16[1296,128]{1,0:T(8,128)(2,1)S(1)}) custom-call(bf16[2176,128]{1,0:T(8,128)(2,1)} %bitcast.7, s32[2,17]{1,0:T(2,128)} %bitcast.9, bf16[1280,128]{1,0:T(8,128)(2,1)} %bitcast.8, s32[2,10]{1,0:T(2,128)} %bitcast.10), custom_call_target="tpu_custom_call" | custom-call | tf_op jit(solution)/shard_map/pallas_call | solution.py:68
  1.2 2.5 %collective-permute-start.18 = (bf16[1296,128]{1,0:T(8,128)(2,1)S(1)}, bf16[1296,128]{1,0:T(8,128)(2,1)S(1)}, u32[]{:S(2)}, u32[]{:S(2)}) collective-permute-start(bf16[1296,128]{1,0:T(8,128)(2,1)S(1)} %get-tuple-element.13.refs_20_), channel_id=1, source_target_pairs={{0,64},{16,80},{32,96},{48,112},{64,0},{80,16},{96,32},{112,48},{1... | collective-permute-start | bytes 995336 | tf_op jit(solution)/shard_map/ppermute | solution.py:45
  3.8 2.5 %collective-permute-start.16 = (bf16[1296,128]{1,0:T(8,128)(2,1)S(1)}, bf16[1296,128]{1,0:T(8,128)(2,1)S(1)}, u32[]{:S(2)}, u32[]{:S(2)}) collective-permute-start(bf16[1296,128]{1,0:T(8,128)(2,1)S(1)} %get-tuple-element.13.refs_20_), channel_id=1, source_target_pairs={{0,48},{16,0},{32,16},{48,32},{64,112},{80,64},{96,80},{112,96},{1... | collective-permute-start | bytes 995336 | tf_op jit(solution)/shard_map/ppermute | solution.py:45
  6.3 2.7 %collective-permute-start.1 = (bf16[2192,128]{1,0:T(8,128)(2,1)S(1)}, bf16[2192,128]{1,0:T(8,128)(2,1)S(1)}, u32[]{:S(2)}, u32[]{:S(2)}) collective-permute-start(bf16[2192,128]{1,0:T(8,128)(2,1)S(1)} %get-tuple-element.11.refs_4_), channel_id=1, source_target_pairs={{0,12},{1,13},{2,14},{3,15},{4,0},{5,1},{6,2},{7,3},{8,4},{9,5},{1... | collective-permute-start | bytes 1683464 | tf_op jit(solution)/shard_map/ppermute | solution.py:37
  9.0 2.3 %collective-permute-done.18.refs_24_ = bf16[1296,128]{1,0:T(8,128)(2,1)S(1)} collective-permute-done((bf16[1296,128]{1,0:T(8,128)(2,1)S(1)}, bf16[1296,128]{1,0:T(8,128)(2,1)S(1)}, u32[]{:S(2)}, u32[]{:S(2)}) %collective-permute-start.18) | collective-permute-done | bytes 331808 | tf_op jit(solution)/shard_map/ppermute | solution.py:45
  11.3 1.3 %collective-permute-start.7 = (bf16[2192,128]{1,0:T(8,128)(2,1)S(1)}, bf16[2192,128]{1,0:T(8,128)(2,1)S(1)}, u32[]{:S(2)}, u32[]{:S(2)}) collective-permute-start(bf16[2192,128]{1,0:T(8,128)(2,1)S(1)} %get-tuple-element.11.refs_4_), channel_id=1, source_target_pairs={{0,1},{1,0},{2,3},{3,2},{4,5},{5,4},{6,7},{7,6},{8,9},{9,8},{10,11... | collective-permute-start | bytes 1683464 | tf_op jit(solution)/shard_map/ppermute | solution.py:37
  12.5 3.4 %collective-permute-start.3 = (bf16[2192,128]{1,0:T(8,128)(2,1)S(1)}, bf16[2192,128]{1,0:T(8,128)(2,1)S(1)}, u32[]{:S(2)}, u32[]{:S(2)}) collective-permute-start(bf16[2192,128]{1,0:T(8,128)(2,1)S(1)} %get-tuple-element.11.refs_4_), channel_id=1, source_target_pairs={{0,2},{1,3},{2,0},{3,1},{4,6},{5,7},{6,4},{7,5},{8,10},{9,11},{10,... | collective-permute-start | bytes 1683464 | tf_op jit(solution)/shard_map/ppermute | solution.py:37
  16.0 3.2 %collective-permute-start.20 = (bf16[1296,128]{1,0:T(8,128)(2,1)S(1)}, bf16[1296,128]{1,0:T(8,128)(2,1)S(1)}, u32[]{:S(2)}, u32[]{:S(2)}) collective-permute-start(bf16[1296,128]{1,0:T(8,128)(2,1)S(1)} %collective-permute-done.18.refs_24_), channel_id=1, source_target_pairs={{0,48},{16,0},{32,16},{48,32},{64,112},{80,64},{96,80},{112,96},{1... | collective-permute-start | bytes 995336 | tf_op jit(solution)/shard_map/ppermute | solution.py:45
  19.2 0.6 collective-permute-done.1.refs_6_
  19.8 3.2 %collective-permute-done.refs_5_ = bf16[2192,128]{1,0:T(8,128)(2,1)} collective-permute-done((bf16[2192,128]{1,0:T(8,128)(2,1)S(1)}, bf16[2192,128]{1,0:T(8,128)(2,1)}, u32[]{:S(2)}, u32[]{:S(2)}) %collective-permute-start) | collective-permute-done | bytes 561184 | tf_op jit(solution)/shard_map/ppermute | solution.py:37
  23.0 0.1 broadcast_select_fusion
  23.1 0.3 collective-permute-start.2
  23.3 0.7 %collective-permute-done.20.refs_26_ = bf16[1296,128]{1,0:T(8,128)(2,1)S(1)} collective-permute-done((bf16[1296,128]{1,0:T(8,128)(2,1)S(1)}, bf16[1296,128]{1,0:T(8,128)(2,1)S(1)}, u32[]{:S(2)}, u32[]{:S(2)}) %collective-permute-start.20) | collective-permute-done | bytes 331808 | tf_op jit(solution)/shard_map/ppermute | solution.py:45
  24.1 3.5 %collective-permute-start.17 = (bf16[1296,128]{1,0:T(8,128)(2,1)S(1)}, bf16[1296,128]{1,0:T(8,128)(2,1)S(1)}, u32[]{:S(2)}, u32[]{:S(2)}) collective-permute-start(bf16[1296,128]{1,0:T(8,128)(2,1)S(1)} %broadcast_select_fusion.2), channel_id=1, source_target_pairs={{0,16},{1,49},{2,18},{3,51},{4,20},{5,53},{6,22},{7,55},{8,24},{9,... | collective-permute-start | bytes 995336 | tf_op jit(solution)/shard_map/ppermute | solution.py:54
  27.6 0.5 collective-permute-done.19.refs_25_
  28.2 1.0 %collective-permute-start.21 = (bf16[1296,128]{1,0:T(8,128)(2,1)S(1)}, bf16[1296,128]{1,0:T(8,128)(2,1)S(1)}, u32[]{:S(2)}, u32[]{:S(2)}) collective-permute-start(bf16[1296,128]{1,0:T(8,128)(2,1)S(1)} %broadcast_select_fusion.1), channel_id=1, source_target_pairs={{0,16},{1,49},{2,18},{3,51},{4,20},{5,53},{6,22},{7,55},{8,24},{9,... | collective-permute-start | bytes 995336 | tf_op jit(solution)/shard_map/ppermute | solution.py:54
  29.2 2.3 %collective-permute-start.11 = (bf16[2192,128]{1,0:T(8,128)(2,1)S(1)}, bf16[2192,128]{1,0:T(8,128)(2,1)S(1)}, u32[]{:S(2)}, u32[]{:S(2)}) collective-permute-start(bf16[2192,128]{1,0:T(8,128)(2,1)S(1)} %collective-permute-done.3.refs_8_), channel_id=1, source_target_pairs={{0,1},{1,0},{2,3},{3,2},{4,5},{5,4},{6,7},{7,6},{8,9},{9,8},{10,11... | collective-permute-start | bytes 1683464 | tf_op jit(solution)/shard_map/ppermute | solution.py:37
  31.5 0.1 collective-permute-start.9
  31.6 0.1 collective-permute-done.17.refs_23_
  31.7 3.3 %collective-permute-start.5 = (bf16[2192,128]{1,0:T(8,128)(2,1)S(1)}, bf16[2192,128]{1,0:T(8,128)(2,1)S(1)}, u32[]{:S(2)}, u32[]{:S(2)}) collective-permute-start(bf16[2192,128]{1,0:T(8,128)(2,1)S(1)} %collective-permute-done.3.refs_8_), channel_id=1, source_target_pairs={{0,12},{1,13},{2,14},{3,15},{4,0},{5,1},{6,2},{7,3},{8,4},{9,5},{1... | collective-permute-start | bytes 1683464 | tf_op jit(solution)/shard_map/ppermute | solution.py:37
  35.0 0.2 collective-permute-done.21.refs_27_
  35.2 1.2 %collective-permute-start.4 = (bf16[2192,128]{1,0:T(8,128)(2,1)S(1)}, bf16[2192,128]{1,0:T(8,128)(2,1)S(1)}, u32[]{:S(2)}, u32[]{:S(2)}) collective-permute-start(bf16[2192,128]{1,0:T(8,128)(2,1)S(1)} %collective-permute-done.3.refs_8_), channel_id=1, source_target_pairs={{0,4},{1,5},{2,6},{3,7},{4,8},{5,9},{6,10},{7,11},{8,12},{9,13},{1... | collective-permute-start | bytes 1683464 | tf_op jit(solution)/shard_map/ppermute | solution.py:37
  36.4 2.5 %collective-permute-start.6 = (bf16[2192,128]{1,0:T(8,128)(2,1)}, bf16[2192,128]{1,0:T(8,128)(2,1)S(1)}, u32[]{:S(2)}, u32[]{:S(2)}) collective-permute-start(bf16[2192,128]{1,0:T(8,128)(2,1)} %collective-permute-done.2.refs_7_), channel_id=1, source_target_pairs={{0,2},{1,3},{2,0},{3,1},{4,6},{5,7},{6,4},{7,5},{8,10},{9,11},{10,... | collective-permute-start | bytes 1683464 | tf_op jit(solution)/shard_map/ppermute | solution.py:37
  38.9 5.5 %collective-permute-start.8 = (bf16[2192,128]{1,0:T(8,128)(2,1)}, bf16[2192,128]{1,0:T(8,128)(2,1)}, u32[]{:S(2)}, u32[]{:S(2)}) collective-permute-start(bf16[2192,128]{1,0:T(8,128)(2,1)} %collective-permute-done.refs_5_), channel_id=1, source_target_pairs={{0,1},{1,0},{2,3},{3,2},{4,5},{5,4},{6,7},{7,6},{8,9},{9,8},{10,11... | collective-permute-start | bytes 1683464 | tf_op jit(solution)/shard_map/ppermute | solution.py:37
  44.4 0.1 collective-permute-start.10
  44.5 3.4 %collective-permute-start.13 = (bf16[2192,128]{1,0:T(8,128)(2,1)S(1)}, bf16[2192,128]{1,0:T(8,128)(2,1)S(1)}, u32[]{:S(2)}, u32[]{:S(2)}) collective-permute-start(bf16[2192,128]{1,0:T(8,128)(2,1)S(1)} %collective-permute-done.5.refs_10_), channel_id=1, source_target_pairs={{0,1},{1,0},{2,3},{3,2},{4,5},{5,4},{6,7},{7,6},{8,9},{9,8},{10,11... | collective-permute-start | bytes 1683464 | tf_op jit(solution)/shard_map/ppermute | solution.py:37
  47.9 3.7 %collective-permute-start.12 = (bf16[2192,128]{1,0:T(8,128)(2,1)S(1)}, bf16[2192,128]{1,0:T(8,128)(2,1)S(1)}, u32[]{:S(2)}, u32[]{:S(2)}) collective-permute-start(bf16[2192,128]{1,0:T(8,128)(2,1)S(1)} %collective-permute-done.4.refs_9_), channel_id=1, source_target_pairs={{0,1},{1,0},{2,3},{3,2},{4,5},{5,4},{6,7},{7,6},{8,9},{9,8},{10,11... | collective-permute-start | bytes 1683464 | tf_op jit(solution)/shard_map/ppermute | solution.py:37
  51.7 1.7 %collective-permute-start.14 = (bf16[2192,128]{1,0:T(8,128)(2,1)S(1)}, bf16[2192,128]{1,0:T(8,128)(2,1)S(1)}, u32[]{:S(2)}, u32[]{:S(2)}) collective-permute-start(bf16[2192,128]{1,0:T(8,128)(2,1)S(1)} %collective-permute-done.6.refs_11_), channel_id=1, source_target_pairs={{0,1},{1,0},{2,3},{3,2},{4,5},{5,4},{6,7},{7,6},{8,9},{9,8},{10,11... | collective-permute-start | bytes 1683464 | tf_op jit(solution)/shard_map/ppermute | solution.py:37
  53.4 0.1 copy.8.refs_3_
  53.5 0.1 pad_add_fusion.refs_0_
  53.6 1.4 %collective-permute-done.14.refs_19_ = bf16[2192,128]{1,0:T(8,128)(2,1)S(1)} collective-permute-done((bf16[2192,128]{1,0:T(8,128)(2,1)S(1)}, bf16[2192,128]{1,0:T(8,128)(2,1)S(1)}, u32[]{:S(2)}, u32[]{:S(2)}) %collective-permute-start.14) | collective-permute-done | bytes 561184 | tf_op jit(solution)/shard_map/ppermute | solution.py:37
  55.0 9.0 %shard_map.74 = bf16[48,128,128]{2,1,0:T(8,128)(2,1)} custom-call(s32[2]{0:T(128)S(1)} %pad_add_fusion.refs_0_, s32[64]{0:T(128)S(1)} %copy-done.2, s32[96]{0:T(128)S(1)} %copy-done.3, s32[24,2]{1,0:T(8,128)S(1)} %copy.8.refs_3_, bf16[2192,128]{1,0:T(8,128)(2,1)} %copy-done, bf16[2192,128]{1,0:T(8,128)(2,1)} %collective-permute-done.refs_5_, ...), custom_call_target="tpu_custom_call" | custom-call | flops 3000000000 | bytes 14000000 | tf_op jit(solution)/shard_map/pallas_call | solution.py:327
  (54 shorter events, 0.2 us)
Async XLA Ops:
  1.2 26.9 %copy-start = (bf16[2192,128]{1,0:T(8,128)(2,1)}, bf16[2192,128]{1,0:T(8,128)(2,1)S(1)}, u32[]{:S(2)}) copy-start(bf16[2192,128]{1,0:T(8,128)(2,1)S(1)} %get-tuple-element.11.refs_4_) | copy-start | bytes 1683460
  1.2 26.9 %copy-start.1 = (bf16[1296,128]{1,0:T(8,128)(2,1)}, bf16[1296,128]{1,0:T(8,128)(2,1)S(1)}, u32[]{:S(2)}) copy-start(bf16[1296,128]{1,0:T(8,128)(2,1)S(1)} %get-tuple-element.13.refs_20_) | copy-start | bytes 995332
  1.2 10.0 %collective-permute-start.18 = (bf16[1296,128]{1,0:T(8,128)(2,1)S(1)}, bf16[1296,128]{1,0:T(8,128)(2,1)S(1)}, u32[]{:S(2)}, u32[]{:S(2)}) collective-permute-start(bf16[1296,128]{1,0:T(8,128)(2,1)S(1)} %get-tuple-element.13.refs_20_), channel_id=1, source_target_pairs={{0,64},{16,80},{32,96},{48,112},{64,0},{80,16},{96,32},{112,48},{1... | collective-permute-start | bytes 995336 | tf_op jit(solution)/shard_map/ppermute | solution.py:45
  3.8 8.8 %collective-permute-start.16 = (bf16[1296,128]{1,0:T(8,128)(2,1)S(1)}, bf16[1296,128]{1,0:T(8,128)(2,1)S(1)}, u32[]{:S(2)}, u32[]{:S(2)}) collective-permute-start(bf16[1296,128]{1,0:T(8,128)(2,1)S(1)} %get-tuple-element.13.refs_20_), channel_id=1, source_target_pairs={{0,48},{16,0},{32,16},{48,32},{64,112},{80,64},{96,80},{112,96},{1... | collective-permute-start | bytes 995336 | tf_op jit(solution)/shard_map/ppermute | solution.py:45
  6.3 9.7 %collective-permute-start.15 = (bf16[1296,128]{1,0:T(8,128)(2,1)S(1)}, bf16[1296,128]{1,0:T(8,128)(2,1)S(1)}, u32[]{:S(2)}, u32[]{:S(2)}) collective-permute-start(bf16[1296,128]{1,0:T(8,128)(2,1)S(1)} %get-tuple-element.13.refs_20_), channel_id=1, source_target_pairs={{0,16},{16,32},{32,48},{48,0},{64,80},{80,96},{96,112},{112,64},{1... | collective-permute-start | bytes 995336 | tf_op jit(solution)/shard_map/ppermute | solution.py:45
  6.3 13.5 %collective-permute-start.1 = (bf16[2192,128]{1,0:T(8,128)(2,1)S(1)}, bf16[2192,128]{1,0:T(8,128)(2,1)S(1)}, u32[]{:S(2)}, u32[]{:S(2)}) collective-permute-start(bf16[2192,128]{1,0:T(8,128)(2,1)S(1)} %get-tuple-element.11.refs_4_), channel_id=1, source_target_pairs={{0,12},{1,13},{2,14},{3,15},{4,0},{5,1},{6,2},{7,3},{8,4},{9,5},{1... | collective-permute-start | bytes 1683464 | tf_op jit(solution)/shard_map/ppermute | solution.py:37
  9.0 14.0 %collective-permute-start = (bf16[2192,128]{1,0:T(8,128)(2,1)S(1)}, bf16[2192,128]{1,0:T(8,128)(2,1)}, u32[]{:S(2)}, u32[]{:S(2)}) collective-permute-start(bf16[2192,128]{1,0:T(8,128)(2,1)S(1)} %get-tuple-element.11.refs_4_), channel_id=1, source_target_pairs={{0,4},{1,5},{2,6},{3,7},{4,8},{5,9},{6,10},{7,11},{8,12},{9,13},{1... | collective-permute-start | bytes 1683464 | tf_op jit(solution)/shard_map/ppermute | solution.py:37
  11.3 20.2 %collective-permute-start.7 = (bf16[2192,128]{1,0:T(8,128)(2,1)S(1)}, bf16[2192,128]{1,0:T(8,128)(2,1)S(1)}, u32[]{:S(2)}, u32[]{:S(2)}) collective-permute-start(bf16[2192,128]{1,0:T(8,128)(2,1)S(1)} %get-tuple-element.11.refs_4_), channel_id=1, source_target_pairs={{0,1},{1,0},{2,3},{3,2},{4,5},{5,4},{6,7},{7,6},{8,9},{9,8},{10,11... | collective-permute-start | bytes 1683464 | tf_op jit(solution)/shard_map/ppermute | solution.py:37
  12.5 16.6 %collective-permute-start.3 = (bf16[2192,128]{1,0:T(8,128)(2,1)S(1)}, bf16[2192,128]{1,0:T(8,128)(2,1)S(1)}, u32[]{:S(2)}, u32[]{:S(2)}) collective-permute-start(bf16[2192,128]{1,0:T(8,128)(2,1)S(1)} %get-tuple-element.11.refs_4_), channel_id=1, source_target_pairs={{0,2},{1,3},{2,0},{3,1},{4,6},{5,7},{6,4},{7,5},{8,10},{9,11},{10,... | collective-permute-start | bytes 1683464 | tf_op jit(solution)/shard_map/ppermute | solution.py:37
  16.0 8.1 %collective-permute-start.20 = (bf16[1296,128]{1,0:T(8,128)(2,1)S(1)}, bf16[1296,128]{1,0:T(8,128)(2,1)S(1)}, u32[]{:S(2)}, u32[]{:S(2)}) collective-permute-start(bf16[1296,128]{1,0:T(8,128)(2,1)S(1)} %collective-permute-done.18.refs_24_), channel_id=1, source_target_pairs={{0,48},{16,0},{32,16},{48,32},{64,112},{80,64},{96,80},{112,96},{1... | collective-permute-start | bytes 995336 | tf_op jit(solution)/shard_map/ppermute | solution.py:45
  19.2 34.2 %copy-start.16 = (s32[24,2]{0,1:T(2,128)S(1)}, s32[24,2]{0,1:T(2,128)}, u32[]{:S(2)}) copy-start(s32[24,2]{0,1:T(2,128)} %param.13) | copy-start | bytes 580
  19.2 35.8 %copy-start.2 = (s32[64]{0:T(128)S(1)}, s32[64]{0:T(128)}, u32[]{:S(2)}) copy-start(s32[64]{0:T(128)} %refs_1_.1) | copy-start | bytes 772
  19.2 35.8 %copy-start.3 = (s32[96]{0:T(128)S(1)}, s32[96]{0:T(128)}, u32[]{:S(2)}) copy-start(s32[96]{0:T(128)} %refs_2_.1) | copy-start | bytes 1156
  19.8 24.8 %copy-start.4 = (bf16[2192,128]{1,0:T(8,128)(2,1)}, bf16[2192,128]{1,0:T(8,128)(2,1)S(1)}, u32[]{:S(2)}) copy-start(bf16[2192,128]{1,0:T(8,128)(2,1)S(1)} %collective-permute-done.1.refs_6_) | copy-start | bytes 1683460
  19.8 8.3 %collective-permute-start.19 = (bf16[1296,128]{1,0:T(8,128)(2,1)S(1)}, bf16[1296,128]{1,0:T(8,128)(2,1)S(1)}, u32[]{:S(2)}, u32[]{:S(2)}) collective-permute-start(bf16[1296,128]{1,0:T(8,128)(2,1)S(1)} %collective-permute-done.18.refs_24_), channel_id=1, source_target_pairs={{0,16},{16,32},{32,48},{48,0},{64,80},{80,96},{96,112},{112,64},{1... | collective-permute-start | bytes 995336 | tf_op jit(solution)/shard_map/ppermute | solution.py:45
  23.1 13.3 %collective-permute-start.2 = (bf16[2192,128]{1,0:T(8,128)(2,1)S(1)}, bf16[2192,128]{1,0:T(8,128)(2,1)}, u32[]{:S(2)}, u32[]{:S(2)}) collective-permute-start(bf16[2192,128]{1,0:T(8,128)(2,1)S(1)} %broadcast_select_fusion), channel_id=1, source_target_pairs={{0,4},{1,13},{2,6},{3,15},{4,8},{5,1},{6,10},{7,3},{8,12},{9,5},{1... | collective-permute-start | bytes 1683464 | tf_op jit(solution)/shard_map/ppermute | solution.py:37
  24.1 23.9 %copy-start.7 = (bf16[1296,128]{1,0:T(8,128)(2,1)}, bf16[1296,128]{1,0:T(8,128)(2,1)S(1)}, u32[]{:S(2)}) copy-start(bf16[1296,128]{1,0:T(8,128)(2,1)S(1)} %collective-permute-done.20.refs_26_) | copy-start | bytes 995332
  24.1 7.6 %collective-permute-start.17 = (bf16[1296,128]{1,0:T(8,128)(2,1)S(1)}, bf16[1296,128]{1,0:T(8,128)(2,1)S(1)}, u32[]{:S(2)}, u32[]{:S(2)}) collective-permute-start(bf16[1296,128]{1,0:T(8,128)(2,1)S(1)} %broadcast_select_fusion.2), channel_id=1, source_target_pairs={{0,16},{1,49},{2,18},{3,51},{4,20},{5,53},{6,22},{7,55},{8,24},{9,... | collective-permute-start | bytes 995336 | tf_op jit(solution)/shard_map/ppermute | solution.py:54
  28.2 7.0 %collective-permute-start.21 = (bf16[1296,128]{1,0:T(8,128)(2,1)S(1)}, bf16[1296,128]{1,0:T(8,128)(2,1)S(1)}, u32[]{:S(2)}, u32[]{:S(2)}) collective-permute-start(bf16[1296,128]{1,0:T(8,128)(2,1)S(1)} %broadcast_select_fusion.1), channel_id=1, source_target_pairs={{0,16},{1,49},{2,18},{3,51},{4,20},{5,53},{6,22},{7,55},{8,24},{9,... | collective-permute-start | bytes 995336 | tf_op jit(solution)/shard_map/ppermute | solution.py:54
  29.2 22.4 %copy-start.10 = (bf16[2192,128]{1,0:T(8,128)(2,1)}, bf16[2192,128]{1,0:T(8,128)(2,1)S(1)}, u32[]{:S(2)}) copy-start(bf16[2192,128]{1,0:T(8,128)(2,1)S(1)} %collective-permute-done.3.refs_8_) | copy-start | bytes 1683460
  29.2 9.7 %collective-permute-start.11 = (bf16[2192,128]{1,0:T(8,128)(2,1)S(1)}, bf16[2192,128]{1,0:T(8,128)(2,1)S(1)}, u32[]{:S(2)}, u32[]{:S(2)}) collective-permute-start(bf16[2192,128]{1,0:T(8,128)(2,1)S(1)} %collective-permute-done.3.refs_8_), channel_id=1, source_target_pairs={{0,1},{1,0},{2,3},{3,2},{4,5},{5,4},{6,7},{7,6},{8,9},{9,8},{10,11... | collective-permute-start | bytes 1683464 | tf_op jit(solution)/shard_map/ppermute | solution.py:37
  31.5 20.2 %copy-start.9 = (bf16[2192,128]{1,0:T(8,128)(2,1)}, bf16[2192,128]{1,0:T(8,128)(2,1)S(1)}, u32[]{:S(2)}) copy-start(bf16[2192,128]{1,0:T(8,128)(2,1)S(1)} %collective-permute-done.7.refs_12_) | copy-start | bytes 1683460
  31.5 13.0 %collective-permute-start.9 = (bf16[2192,128]{1,0:T(8,128)(2,1)S(1)}, bf16[2192,128]{1,0:T(8,128)(2,1)S(1)}, u32[]{:S(2)}, u32[]{:S(2)}) collective-permute-start(bf16[2192,128]{1,0:T(8,128)(2,1)S(1)} %collective-permute-done.1.refs_6_), channel_id=1, source_target_pairs={{0,1},{1,0},{2,3},{3,2},{4,5},{5,4},{6,7},{7,6},{8,9},{9,8},{10,11... | collective-permute-start | bytes 1683464 | tf_op jit(solution)/shard_map/ppermute | solution.py:37
  31.7 20.0 %copy-start.14 = (bf16[1296,128]{1,0:T(8,128)(2,1)}, bf16[1296,128]{1,0:T(8,128)(2,1)S(1)}, u32[]{:S(2)}) copy-start(bf16[1296,128]{1,0:T(8,128)(2,1)S(1)} %collective-permute-done.17.refs_23_) | copy-start | bytes 995332
  31.7 12.9 %collective-permute-start.5 = (bf16[2192,128]{1,0:T(8,128)(2,1)S(1)}, bf16[2192,128]{1,0:T(8,128)(2,1)S(1)}, u32[]{:S(2)}, u32[]{:S(2)}) collective-permute-start(bf16[2192,128]{1,0:T(8,128)(2,1)S(1)} %collective-permute-done.3.refs_8_), channel_id=1, source_target_pairs={{0,12},{1,13},{2,14},{3,15},{4,0},{5,1},{6,2},{7,3},{8,4},{9,5},{1... | collective-permute-start | bytes 1683464 | tf_op jit(solution)/shard_map/ppermute | solution.py:37
  35.2 12.7 %collective-permute-start.4 = (bf16[2192,128]{1,0:T(8,128)(2,1)S(1)}, bf16[2192,128]{1,0:T(8,128)(2,1)S(1)}, u32[]{:S(2)}, u32[]{:S(2)}) collective-permute-start(bf16[2192,128]{1,0:T(8,128)(2,1)S(1)} %collective-permute-done.3.refs_8_), channel_id=1, source_target_pairs={{0,4},{1,5},{2,6},{3,7},{4,8},{5,9},{6,10},{7,11},{8,12},{9,13},{1... | collective-permute-start | bytes 1683464 | tf_op jit(solution)/shard_map/ppermute | solution.py:37
  36.4 15.2 %collective-permute-start.6 = (bf16[2192,128]{1,0:T(8,128)(2,1)}, bf16[2192,128]{1,0:T(8,128)(2,1)S(1)}, u32[]{:S(2)}, u32[]{:S(2)}) collective-permute-start(bf16[2192,128]{1,0:T(8,128)(2,1)} %collective-permute-done.2.refs_7_), channel_id=1, source_target_pairs={{0,2},{1,3},{2,0},{3,1},{4,6},{5,7},{6,4},{7,5},{8,10},{9,11},{10,... | collective-permute-start | bytes 1683464 | tf_op jit(solution)/shard_map/ppermute | solution.py:37
  38.9 14.6 %collective-permute-start.8 = (bf16[2192,128]{1,0:T(8,128)(2,1)}, bf16[2192,128]{1,0:T(8,128)(2,1)}, u32[]{:S(2)}, u32[]{:S(2)}) collective-permute-start(bf16[2192,128]{1,0:T(8,128)(2,1)} %collective-permute-done.refs_5_), channel_id=1, source_target_pairs={{0,1},{1,0},{2,3},{3,2},{4,5},{5,4},{6,7},{7,6},{8,9},{9,8},{10,11... | collective-permute-start | bytes 1683464 | tf_op jit(solution)/shard_map/ppermute | solution.py:37
  44.4 9.1 %collective-permute-start.10 = (bf16[2192,128]{1,0:T(8,128)(2,1)}, bf16[2192,128]{1,0:T(8,128)(2,1)}, u32[]{:S(2)}, u32[]{:S(2)}) collective-permute-start(bf16[2192,128]{1,0:T(8,128)(2,1)} %collective-permute-done.2.refs_7_), channel_id=1, source_target_pairs={{0,1},{1,0},{2,3},{3,2},{4,5},{5,4},{6,7},{7,6},{8,9},{9,8},{10,11... | collective-permute-start | bytes 1683464 | tf_op jit(solution)/shard_map/ppermute | solution.py:37
  44.5 9.0 %collective-permute-start.13 = (bf16[2192,128]{1,0:T(8,128)(2,1)S(1)}, bf16[2192,128]{1,0:T(8,128)(2,1)S(1)}, u32[]{:S(2)}, u32[]{:S(2)}) collective-permute-start(bf16[2192,128]{1,0:T(8,128)(2,1)S(1)} %collective-permute-done.5.refs_10_), channel_id=1, source_target_pairs={{0,1},{1,0},{2,3},{3,2},{4,5},{5,4},{6,7},{7,6},{8,9},{9,8},{10,11... | collective-permute-start | bytes 1683464 | tf_op jit(solution)/shard_map/ppermute | solution.py:37
  47.9 5.6 %collective-permute-start.12 = (bf16[2192,128]{1,0:T(8,128)(2,1)S(1)}, bf16[2192,128]{1,0:T(8,128)(2,1)S(1)}, u32[]{:S(2)}, u32[]{:S(2)}) collective-permute-start(bf16[2192,128]{1,0:T(8,128)(2,1)S(1)} %collective-permute-done.4.refs_9_), channel_id=1, source_target_pairs={{0,1},{1,0},{2,3},{3,2},{4,5},{5,4},{6,7},{7,6},{8,9},{9,8},{10,11... | collective-permute-start | bytes 1683464 | tf_op jit(solution)/shard_map/ppermute | solution.py:37
  51.7 3.3 %collective-permute-start.14 = (bf16[2192,128]{1,0:T(8,128)(2,1)S(1)}, bf16[2192,128]{1,0:T(8,128)(2,1)S(1)}, u32[]{:S(2)}, u32[]{:S(2)}) collective-permute-start(bf16[2192,128]{1,0:T(8,128)(2,1)S(1)} %collective-permute-done.6.refs_11_), channel_id=1, source_target_pairs={{0,1},{1,0},{2,3},{3,2},{4,5},{5,4},{6,7},{7,6},{8,9},{9,8},{10,11... | collective-permute-start | bytes 1683464 | tf_op jit(solution)/shard_map/ppermute | solution.py:37
  (7 other events, 101.0 us)

commit v6 on v5

--- a/solution.py
+++ b/solution.py
@@ -236,11 +236,16 @@
             column = jnp.where(sub == i, slot_ref[i * CL + j].astype(jnp.float32), column)
         slot_b = jnp.where(packed[1:2] - 1 == col_at[j].astype(jnp.float32), column, slot_b)
 
-    total = make_list(n_a, read_labels(a_raw), row_col, hot_k, slot_b, list_v)
-    store_list(list_v, list_ref, list_sem)
-    for copy in b_copies + a_copies:
-        copy.wait()
-    add_products(total, list_ref, a_ref, b_ref, acc_ref)
+    labels = read_labels(a_raw)
+    half = n_a // 2
+    for part in range(2):
+        blocks = slice(part * half, (part + 1) * half)
+        total = make_list(half, labels[blocks], row_col, hot_k, slot_b, list_v)
+        store_list(list_v, list_ref, list_sem)
+        for copy in (b_copies if part == 0 else []) + a_copies[blocks]:
+            copy.wait()
+        held = a_ref.at[pl.ds(part * half * A_ROWS, half * A_ROWS)]
+        add_products(total, list_ref, held, b_ref, acc_ref)
 
     def finish(n, _):
         out_ref[place_ref[n]] = acc_ref[n].astype(jnp.bfloat16)

time: 64.1 us -> 65.4 us (1.020)
  Pallas kernels: 10.2 us -> 11.2 us
    pallas_call x1, Pallas kernels: 9 us -> 10 us  [per_device(): pl.pallas_call(kernel, out_shape=jax.ShapeDtypeStruct((RL * CL, TILE, TIL...]
where the time goes in v6:
time: 65.4 us; the launch traced here: 65 us
  starting transfers between devices  44.2 us (68%)
  Pallas kernels  11.2 us (17%)
  waiting for transfers between devices  9.05 us (14%)
    ppermute x15, starting transfers between devices, col_move(): return lax.ppermute(x, 'col', pairs)  31.5 us
    pallas_call x1, Pallas kernels, per_device(): pl.pallas_call(kernel, out_shape=jax.ShapeDtypeStruct((RL * CL, TILE, TIL...  10 us
    ppermute x5, starting transfers between devices, row_move(): return lax.ppermute(x, 'row', pairs)  8.19 us
    ppermute x15, waiting for transfers between devices, col_move(): return lax.ppermute(x, 'col', pairs)  5.22 us
    ppermute x2, starting transfers between devices, row_move_by_core(): return lax.ppermute(x, ('row', 'col'), pairs)  4.49 us
    ppermute x5, waiting for transfers between devices, row_move(): return lax.ppermute(x, 'row', pairs)  3.53 us
  transfers between devices with their start and end apart: 22, of which 8 were waited for; matrix products, arithmetic and copies ran while one was open for 0% of the time, Pallas kernels for 0%

profile of v6, /device:TPU:1, one launch (start us, length us, event | category | flops | bytes accessed | tf_op | source)
XLA Modules:
  0.0 65.0 jit_solution(17230551353976804920)
XLA Ops:
  0.0 1.2 %shard_map.73 = (bf16[2192,128]{1,0:T(8,128)(2,1)S(1)}, bf16[1296,128]{1,0:T(8,128)(2,1)S(1)}) custom-call(bf16[2176,128]{1,0:T(8,128)(2,1)} %bitcast.7, s32[2,17]{1,0:T(2,128)} %bitcast.9, bf16[1280,128]{1,0:T(8,128)(2,1)} %bitcast.8, s32[2,10]{1,0:T(2,128)} %bitcast.10), custom_call_target="tpu_custom_call" | custom-call | tf_op jit(solution)/shard_map/pallas_call | solution.py:68
  1.2 2.5 %collective-permute-start.18 = (bf16[1296,128]{1,0:T(8,128)(2,1)S(1)}, bf16[1296,128]{1,0:T(8,128)(2,1)S(1)}, u32[]{:S(2)}, u32[]{:S(2)}) collective-permute-start(bf16[1296,128]{1,0:T(8,128)(2,1)S(1)} %get-tuple-element.13.refs_20_), channel_id=1, source_target_pairs={{0,64},{16,80},{32,96},{48,112},{64,0},{80,16},{96,32},{112,48},{1... | collective-permute-start | bytes 995336 | tf_op jit(solution)/shard_map/ppermute | solution.py:45
  3.8 2.5 %collective-permute-start.16 = (bf16[1296,128]{1,0:T(8,128)(2,1)S(1)}, bf16[1296,128]{1,0:T(8,128)(2,1)S(1)}, u32[]{:S(2)}, u32[]{:S(2)}) collective-permute-start(bf16[1296,128]{1,0:T(8,128)(2,1)S(1)} %get-tuple-element.13.refs_20_), channel_id=1, source_target_pairs={{0,48},{16,0},{32,16},{48,32},{64,112},{80,64},{96,80},{112,96},{1... | collective-permute-start | bytes 995336 | tf_op jit(solution)/shard_map/ppermute | solution.py:45
  6.3 2.7 %collective-permute-start.1 = (bf16[2192,128]{1,0:T(8,128)(2,1)S(1)}, bf16[2192,128]{1,0:T(8,128)(2,1)S(1)}, u32[]{:S(2)}, u32[]{:S(2)}) collective-permute-start(bf16[2192,128]{1,0:T(8,128)(2,1)S(1)} %get-tuple-element.11.refs_4_), channel_id=1, source_target_pairs={{0,12},{1,13},{2,14},{3,15},{4,0},{5,1},{6,2},{7,3},{8,4},{9,5},{1... | collective-permute-start | bytes 1683464 | tf_op jit(solution)/shard_map/ppermute | solution.py:37
  9.0 2.3 %collective-permute-done.18.refs_24_ = bf16[1296,128]{1,0:T(8,128)(2,1)S(1)} collective-permute-done((bf16[1296,128]{1,0:T(8,128)(2,1)S(1)}, bf16[1296,128]{1,0:T(8,128)(2,1)S(1)}, u32[]{:S(2)}, u32[]{:S(2)}) %collective-permute-start.18) | collective-permute-done | bytes 331808 | tf_op jit(solution)/shard_map/ppermute | solution.py:45
  11.3 1.3 %collective-permute-start.7 = (bf16[2192,128]{1,0:T(8,128)(2,1)S(1)}, bf16[2192,128]{1,0:T(8,128)(2,1)S(1)}, u32[]{:S(2)}, u32[]{:S(2)}) collective-permute-start(bf16[2192,128]{1,0:T(8,128)(2,1)S(1)} %get-tuple-element.11.refs_4_), channel_id=1, source_target_pairs={{0,1},{1,0},{2,3},{3,2},{4,5},{5,4},{6,7},{7,6},{8,9},{9,8},{10,11... | collective-permute-start | bytes 1683464 | tf_op jit(solution)/shard_map/ppermute | solution.py:37
  12.5 3.4 %collective-permute-start.3 = (bf16[2192,128]{1,0:T(8,128)(2,1)S(1)}, bf16[2192,128]{1,0:T(8,128)(2,1)S(1)}, u32[]{:S(2)}, u32[]{:S(2)}) collective-permute-start(bf16[2192,128]{1,0:T(8,128)(2,1)S(1)} %get-tuple-element.11.refs_4_), channel_id=1, source_target_pairs={{0,2},{1,3},{2,0},{3,1},{4,6},{5,7},{6,4},{7,5},{8,10},{9,11},{10,... | collective-permute-start | bytes 1683464 | tf_op jit(solution)/shard_map/ppermute | solution.py:37
  16.0 3.2 %collective-permute-start.20 = (bf16[1296,128]{1,0:T(8,128)(2,1)S(1)}, bf16[1296,128]{1,0:T(8,128)(2,1)S(1)}, u32[]{:S(2)}, u32[]{:S(2)}) collective-permute-start(bf16[1296,128]{1,0:T(8,128)(2,1)S(1)} %collective-permute-done.18.refs_24_), channel_id=1, source_target_pairs={{0,48},{16,0},{32,16},{48,32},{64,112},{80,64},{96,80},{112,96},{1... | collective-permute-start | bytes 995336 | tf_op jit(solution)/shard_map/ppermute | solution.py:45
  19.2 0.6 collective-permute-done.1.refs_6_
  19.8 3.2 %collective-permute-done.refs_5_ = bf16[2192,128]{1,0:T(8,128)(2,1)} collective-permute-done((bf16[2192,128]{1,0:T(8,128)(2,1)S(1)}, bf16[2192,128]{1,0:T(8,128)(2,1)}, u32[]{:S(2)}, u32[]{:S(2)}) %collective-permute-start) | collective-permute-done | bytes 561184 | tf_op jit(solution)/shard_map/ppermute | solution.py:37
  23.0 0.1 broadcast_select_fusion
  23.1 0.3 collective-permute-start.2
  23.3 0.7 %collective-permute-done.20.refs_26_ = bf16[1296,128]{1,0:T(8,128)(2,1)S(1)} collective-permute-done((bf16[1296,128]{1,0:T(8,128)(2,1)S(1)}, bf16[1296,128]{1,0:T(8,128)(2,1)S(1)}, u32[]{:S(2)}, u32[]{:S(2)}) %collective-permute-start.20) | collective-permute-done | bytes 331808 | tf_op jit(solution)/shard_map/ppermute | solution.py:45
  24.1 3.5 %collective-permute-start.17 = (bf16[1296,128]{1,0:T(8,128)(2,1)S(1)}, bf16[1296,128]{1,0:T(8,128)(2,1)S(1)}, u32[]{:S(2)}, u32[]{:S(2)}) collective-permute-start(bf16[1296,128]{1,0:T(8,128)(2,1)S(1)} %broadcast_select_fusion.2), channel_id=1, source_target_pairs={{0,16},{1,49},{2,18},{3,51},{4,20},{5,53},{6,22},{7,55},{8,24},{9,... | collective-permute-start | bytes 995336 | tf_op jit(solution)/shard_map/ppermute | solution.py:54
  27.6 0.5 collective-permute-done.19.refs_25_
  28.2 1.0 %collective-permute-start.21 = (bf16[1296,128]{1,0:T(8,128)(2,1)S(1)}, bf16[1296,128]{1,0:T(8,128)(2,1)S(1)}, u32[]{:S(2)}, u32[]{:S(2)}) collective-permute-start(bf16[1296,128]{1,0:T(8,128)(2,1)S(1)} %broadcast_select_fusion.1), channel_id=1, source_target_pairs={{0,16},{1,49},{2,18},{3,51},{4,20},{5,53},{6,22},{7,55},{8,24},{9,... | collective-permute-start | bytes 995336 | tf_op jit(solution)/shard_map/ppermute | solution.py:54
  29.2 2.3 %collective-permute-start.11 = (bf16[2192,128]{1,0:T(8,128)(2,1)S(1)}, bf16[2192,128]{1,0:T(8,128)(2,1)S(1)}, u32[]{:S(2)}, u32[]{:S(2)}) collective-permute-start(bf16[2192,128]{1,0:T(8,128)(2,1)S(1)} %collective-permute-done.3.refs_8_), channel_id=1, source_target_pairs={{0,1},{1,0},{2,3},{3,2},{4,5},{5,4},{6,7},{7,6},{8,9},{9,8},{10,11... | collective-permute-start | bytes 1683464 | tf_op jit(solution)/shard_map/ppermute | solution.py:37
  31.5 0.1 collective-permute-start.9
  31.6 0.1 collective-permute-done.17.refs_23_
  31.7 3.3 %collective-permute-start.5 = (bf16[2192,128]{1,0:T(8,128)(2,1)S(1)}, bf16[2192,128]{1,0:T(8,128)(2,1)S(1)}, u32[]{:S(2)}, u32[]{:S(2)}) collective-permute-start(bf16[2192,128]{1,0:T(8,128)(2,1)S(1)} %collective-permute-done.3.refs_8_), channel_id=1, source_target_pairs={{0,12},{1,13},{2,14},{3,15},{4,0},{5,1},{6,2},{7,3},{8,4},{9,5},{1... | collective-permute-start | bytes 1683464 | tf_op jit(solution)/shard_map/ppermute | solution.py:37
  35.0 0.2 collective-permute-done.21.refs_27_
  35.2 1.2 %collective-permute-start.4 = (bf16[2192,128]{1,0:T(8,128)(2,1)S(1)}, bf16[2192,128]{1,0:T(8,128)(2,1)S(1)}, u32[]{:S(2)}, u32[]{:S(2)}) collective-permute-start(bf16[2192,128]{1,0:T(8,128)(2,1)S(1)} %collective-permute-done.3.refs_8_), channel_id=1, source_target_pairs={{0,4},{1,5},{2,6},{3,7},{4,8},{5,9},{6,10},{7,11},{8,12},{9,13},{1... | collective-permute-start | bytes 1683464 | tf_op jit(solution)/shard_map/ppermute | solution.py:37
  36.4 2.5 %collective-permute-start.6 = (bf16[2192,128]{1,0:T(8,128)(2,1)}, bf16[2192,128]{1,0:T(8,128)(2,1)S(1)}, u32[]{:S(2)}, u32[]{:S(2)}) collective-permute-start(bf16[2192,128]{1,0:T(8,128)(2,1)} %collective-permute-done.2.refs_7_), channel_id=1, source_target_pairs={{0,2},{1,3},{2,0},{3,1},{4,6},{5,7},{6,4},{7,5},{8,10},{9,11},{10,... | collective-permute-start | bytes 1683464 | tf_op jit(solution)/shard_map/ppermute | solution.py:37
  38.9 5.5 %collective-permute-start.8 = (bf16[2192,128]{1,0:T(8,128)(2,1)}, bf16[2192,128]{1,0:T(8,128)(2,1)}, u32[]{:S(2)}, u32[]{:S(2)}) collective-permute-start(bf16[2192,128]{1,0:T(8,128)(2,1)} %collective-permute-done.refs_5_), channel_id=1, source_target_pairs={{0,1},{1,0},{2,3},{3,2},{4,5},{5,4},{6,7},{7,6},{8,9},{9,8},{10,11... | collective-permute-start | bytes 1683464 | tf_op jit(solution)/shard_map/ppermute | solution.py:37
  44.4 0.1 collective-permute-start.10
  44.5 3.4 %collective-permute-start.13 = (bf16[2192,128]{1,0:T(8,128)(2,1)S(1)}, bf16[2192,128]{1,0:T(8,128)(2,1)S(1)}, u32[]{:S(2)}, u32[]{:S(2)}) collective-permute-start(bf16[2192,128]{1,0:T(8,128)(2,1)S(1)} %collective-permute-done.5.refs_10_), channel_id=1, source_target_pairs={{0,1},{1,0},{2,3},{3,2},{4,5},{5,4},{6,7},{7,6},{8,9},{9,8},{10,11... | collective-permute-start | bytes 1683464 | tf_op jit(solution)/shard_map/ppermute | solution.py:37
  47.9 3.7 %collective-permute-start.12 = (bf16[2192,128]{1,0:T(8,128)(2,1)S(1)}, bf16[2192,128]{1,0:T(8,128)(2,1)S(1)}, u32[]{:S(2)}, u32[]{:S(2)}) collective-permute-start(bf16[2192,128]{1,0:T(8,128)(2,1)S(1)} %collective-permute-done.4.refs_9_), channel_id=1, source_target_pairs={{0,1},{1,0},{2,3},{3,2},{4,5},{5,4},{6,7},{7,6},{8,9},{9,8},{10,11... | collective-permute-start | bytes 1683464 | tf_op jit(solution)/shard_map/ppermute | solution.py:37
  51.7 1.7 %collective-permute-start.14 = (bf16[2192,128]{1,0:T(8,128)(2,1)S(1)}, bf16[2192,128]{1,0:T(8,128)(2,1)S(1)}, u32[]{:S(2)}, u32[]{:S(2)}) collective-permute-start(bf16[2192,128]{1,0:T(8,128)(2,1)S(1)} %collective-permute-done.6.refs_11_), channel_id=1, source_target_pairs={{0,1},{1,0},{2,3},{3,2},{4,5},{5,4},{6,7},{7,6},{8,9},{9,8},{10,11... | collective-permute-start | bytes 1683464 | tf_op jit(solution)/shard_map/ppermute | solution.py:37
  53.4 0.1 copy.8.refs_3_
  53.5 0.1 pad_add_fusion.refs_0_
  53.6 1.4 %collective-permute-done.14.refs_19_ = bf16[2192,128]{1,0:T(8,128)(2,1)S(1)} collective-permute-done((bf16[2192,128]{1,0:T(8,128)(2,1)S(1)}, bf16[2192,128]{1,0:T(8,128)(2,1)S(1)}, u32[]{:S(2)}, u32[]{:S(2)}) %collective-permute-start.14) | collective-permute-done | bytes 561184 | tf_op jit(solution)/shard_map/ppermute | solution.py:37
  55.0 10.0 %shard_map.74 = bf16[48,128,128]{2,1,0:T(8,128)(2,1)} custom-call(s32[2]{0:T(128)S(1)} %pad_add_fusion.refs_0_, s32[64]{0:T(128)S(1)} %copy-done.2, s32[96]{0:T(128)S(1)} %copy-done.3, s32[24,2]{1,0:T(8,128)S(1)} %copy.8.refs_3_, bf16[2192,128]{1,0:T(8,128)(2,1)} %copy-done, bf16[2192,128]{1,0:T(8,128)(2,1)} %collective-permute-done.refs_5_, ...), custom_call_target="tpu_custom_call" | custom-call | flops 3000000000 | bytes 14000000 | tf_op jit(solution)/shard_map/pallas_call | solution.py:332
  (54 shorter events, 0.2 us)
Async XLA Ops:
  1.2 26.9 %copy-start = (bf16[2192,128]{1,0:T(8,128)(2,1)}, bf16[2192,128]{1,0:T(8,128)(2,1)S(1)}, u32[]{:S(2)}) copy-start(bf16[2192,128]{1,0:T(8,128)(2,1)S(1)} %get-tuple-element.11.refs_4_) | copy-start | bytes 1683460
  1.2 26.9 %copy-start.1 = (bf16[1296,128]{1,0:T(8,128)(2,1)}, bf16[1296,128]{1,0:T(8,128)(2,1)S(1)}, u32[]{:S(2)}) copy-start(bf16[1296,128]{1,0:T(8,128)(2,1)S(1)} %get-tuple-element.13.refs_20_) | copy-start | bytes 995332
  1.2 10.0 %collective-permute-start.18 = (bf16[1296,128]{1,0:T(8,128)(2,1)S(1)}, bf16[1296,128]{1,0:T(8,128)(2,1)S(1)}, u32[]{:S(2)}, u32[]{:S(2)}) collective-permute-start(bf16[1296,128]{1,0:T(8,128)(2,1)S(1)} %get-tuple-element.13.refs_20_), channel_id=1, source_target_pairs={{0,64},{16,80},{32,96},{48,112},{64,0},{80,16},{96,32},{112,48},{1... | collective-permute-start | bytes 995336 | tf_op jit(solution)/shard_map/ppermute | solution.py:45
  3.8 8.8 %collective-permute-start.16 = (bf16[1296,128]{1,0:T(8,128)(2,1)S(1)}, bf16[1296,128]{1,0:T(8,128)(2,1)S(1)}, u32[]{:S(2)}, u32[]{:S(2)}) collective-permute-start(bf16[1296,128]{1,0:T(8,128)(2,1)S(1)} %get-tuple-element.13.refs_20_), channel_id=1, source_target_pairs={{0,48},{16,0},{32,16},{48,32},{64,112},{80,64},{96,80},{112,96},{1... | collective-permute-start | bytes 995336 | tf_op jit(solution)/shard_map/ppermute | solution.py:45
  6.3 9.7 %collective-permute-start.15 = (bf16[1296,128]{1,0:T(8,128)(2,1)S(1)}, bf16[1296,128]{1,0:T(8,128)(2,1)S(1)}, u32[]{:S(2)}, u32[]{:S(2)}) collective-permute-start(bf16[1296,128]{1,0:T(8,128)(2,1)S(1)} %get-tuple-element.13.refs_20_), channel_id=1, source_target_pairs={{0,16},{16,32},{32,48},{48,0},{64,80},{80,96},{96,112},{112,64},{1... | collective-permute-start | bytes 995336 | tf_op jit(solution)/shard_map/ppermute | solution.py:45
  6.3 13.5 %collective-permute-start.1 = (bf16[2192,128]{1,0:T(8,128)(2,1)S(1)}, bf16[2192,128]{1,0:T(8,128)(2,1)S(1)}, u32[]{:S(2)}, u32[]{:S(2)}) collective-permute-start(bf16[2192,128]{1,0:T(8,128)(2,1)S(1)} %get-tuple-element.11.refs_4_), channel_id=1, source_target_pairs={{0,12},{1,13},{2,14},{3,15},{4,0},{5,1},{6,2},{7,3},{8,4},{9,5},{1... | collective-permute-start | bytes 1683464 | tf_op jit(solution)/shard_map/ppermute | solution.py:37
  9.0 14.0 %collective-permute-start = (bf16[2192,128]{1,0:T(8,128)(2,1)S(1)}, bf16[2192,128]{1,0:T(8,128)(2,1)}, u32[]{:S(2)}, u32[]{:S(2)}) collective-permute-start(bf16[2192,128]{1,0:T(8,128)(2,1)S(1)} %get-tuple-element.11.refs_4_), channel_id=1, source_target_pairs={{0,4},{1,5},{2,6},{3,7},{4,8},{5,9},{6,10},{7,11},{8,12},{9,13},{1... | collective-permute-start | bytes 1683464 | tf_op jit(solution)/shard_map/ppermute | solution.py:37
  11.3 20.2 %collective-permute-start.7 = (bf16[2192,128]{1,0:T(8,128)(2,1)S(1)}, bf16[2192,128]{1,0:T(8,128)(2,1)S(1)}, u32[]{:S(2)}, u32[]{:S(2)}) collective-permute-start(bf16[2192,128]{1,0:T(8,128)(2,1)S(1)} %get-tuple-element.11.refs_4_), channel_id=1, source_target_pairs={{0,1},{1,0},{2,3},{3,2},{4,5},{5,4},{6,7},{7,6},{8,9},{9,8},{10,11... | collective-permute-start | bytes 1683464 | tf_op jit(solution)/shard_map/ppermute | solution.py:37
  12.5 16.6 %collective-permute-start.3 = (bf16[2192,128]{1,0:T(8,128)(2,1)S(1)}, bf16[2192,128]{1,0:T(8,128)(2,1)S(1)}, u32[]{:S(2)}, u32[]{:S(2)}) collective-permute-start(bf16[2192,128]{1,0:T(8,128)(2,1)S(1)} %get-tuple-element.11.refs_4_), channel_id=1, source_target_pairs={{0,2},{1,3},{2,0},{3,1},{4,6},{5,7},{6,4},{7,5},{8,10},{9,11},{10,... | collective-permute-start | bytes 1683464 | tf_op jit(solution)/shard_map/ppermute | solution.py:37
  16.0 8.1 %collective-permute-start.20 = (bf16[1296,128]{1,0:T(8,128)(2,1)S(1)}, bf16[1296,128]{1,0:T(8,128)(2,1)S(1)}, u32[]{:S(2)}, u32[]{:S(2)}) collective-permute-start(bf16[1296,128]{1,0:T(8,128)(2,1)S(1)} %collective-permute-done.18.refs_24_), channel_id=1, source_target_pairs={{0,48},{16,0},{32,16},{48,32},{64,112},{80,64},{96,80},{112,96},{1... | collective-permute-start | bytes 995336 | tf_op jit(solution)/shard_map/ppermute | solution.py:45
  19.2 34.2 %copy-start.16 = (s32[24,2]{0,1:T(2,128)S(1)}, s32[24,2]{0,1:T(2,128)}, u32[]{:S(2)}) copy-start(s32[24,2]{0,1:T(2,128)} %param.13) | copy-start | bytes 580
  19.2 35.8 %copy-start.2 = (s32[64]{0:T(128)S(1)}, s32[64]{0:T(128)}, u32[]{:S(2)}) copy-start(s32[64]{0:T(128)} %refs_1_.1) | copy-start | bytes 772
  19.2 35.8 %copy-start.3 = (s32[96]{0:T(128)S(1)}, s32[96]{0:T(128)}, u32[]{:S(2)}) copy-start(s32[96]{0:T(128)} %refs_2_.1) | copy-start | bytes 1156
  19.8 24.8 %copy-start.4 = (bf16[2192,128]{1,0:T(8,128)(2,1)}, bf16[2192,128]{1,0:T(8,128)(2,1)S(1)}, u32[]{:S(2)}) copy-start(bf16[2192,128]{1,0:T(8,128)(2,1)S(1)} %collective-permute-done.1.refs_6_) | copy-start | bytes 1683460
  19.8 8.3 %collective-permute-start.19 = (bf16[1296,128]{1,0:T(8,128)(2,1)S(1)}, bf16[1296,128]{1,0:T(8,128)(2,1)S(1)}, u32[]{:S(2)}, u32[]{:S(2)}) collective-permute-start(bf16[1296,128]{1,0:T(8,128)(2,1)S(1)} %collective-permute-done.18.refs_24_), channel_id=1, source_target_pairs={{0,16},{16,32},{32,48},{48,0},{64,80},{80,96},{96,112},{112,64},{1... | collective-permute-start | bytes 995336 | tf_op jit(solution)/shard_map/ppermute | solution.py:45
  23.1 13.3 %collective-permute-start.2 = (bf16[2192,128]{1,0:T(8,128)(2,1)S(1)}, bf16[2192,128]{1,0:T(8,128)(2,1)}, u32[]{:S(2)}, u32[]{:S(2)}) collective-permute-start(bf16[2192,128]{1,0:T(8,128)(2,1)S(1)} %broadcast_select_fusion), channel_id=1, source_target_pairs={{0,4},{1,13},{2,6},{3,15},{4,8},{5,1},{6,10},{7,3},{8,12},{9,5},{1... | collective-permute-start | bytes 1683464 | tf_op jit(solution)/shard_map/ppermute | solution.py:37
  24.1 23.9 %copy-start.7 = (bf16[1296,128]{1,0:T(8,128)(2,1)}, bf16[1296,128]{1,0:T(8,128)(2,1)S(1)}, u32[]{:S(2)}) copy-start(bf16[1296,128]{1,0:T(8,128)(2,1)S(1)} %collective-permute-done.20.refs_26_) | copy-start | bytes 995332
  24.1 7.6 %collective-permute-start.17 = (bf16[1296,128]{1,0:T(8,128)(2,1)S(1)}, bf16[1296,128]{1,0:T(8,128)(2,1)S(1)}, u32[]{:S(2)}, u32[]{:S(2)}) collective-permute-start(bf16[1296,128]{1,0:T(8,128)(2,1)S(1)} %broadcast_select_fusion.2), channel_id=1, source_target_pairs={{0,16},{1,49},{2,18},{3,51},{4,20},{5,53},{6,22},{7,55},{8,24},{9,... | collective-permute-start | bytes 995336 | tf_op jit(solution)/shard_map/ppermute | solution.py:54
  28.2 7.0 %collective-permute-start.21 = (bf16[1296,128]{1,0:T(8,128)(2,1)S(1)}, bf16[1296,128]{1,0:T(8,128)(2,1)S(1)}, u32[]{:S(2)}, u32[]{:S(2)}) collective-permute-start(bf16[1296,128]{1,0:T(8,128)(2,1)S(1)} %broadcast_select_fusion.1), channel_id=1, source_target_pairs={{0,16},{1,49},{2,18},{3,51},{4,20},{5,53},{6,22},{7,55},{8,24},{9,... | collective-permute-start | bytes 995336 | tf_op jit(solution)/shard_map/ppermute | solution.py:54
  29.2 22.4 %copy-start.10 = (bf16[2192,128]{1,0:T(8,128)(2,1)}, bf16[2192,128]{1,0:T(8,128)(2,1)S(1)}, u32[]{:S(2)}) copy-start(bf16[2192,128]{1,0:T(8,128)(2,1)S(1)} %collective-permute-done.3.refs_8_) | copy-start | bytes 1683460
  29.2 9.7 %collective-permute-start.11 = (bf16[2192,128]{1,0:T(8,128)(2,1)S(1)}, bf16[2192,128]{1,0:T(8,128)(2,1)S(1)}, u32[]{:S(2)}, u32[]{:S(2)}) collective-permute-start(bf16[2192,128]{1,0:T(8,128)(2,1)S(1)} %collective-permute-done.3.refs_8_), channel_id=1, source_target_pairs={{0,1},{1,0},{2,3},{3,2},{4,5},{5,4},{6,7},{7,6},{8,9},{9,8},{10,11... | collective-permute-start | bytes 1683464 | tf_op jit(solution)/shard_map/ppermute | solution.py:37
  31.5 20.2 %copy-start.9 = (bf16[2192,128]{1,0:T(8,128)(2,1)}, bf16[2192,128]{1,0:T(8,128)(2,1)S(1)}, u32[]{:S(2)}) copy-start(bf16[2192,128]{1,0:T(8,128)(2,1)S(1)} %collective-permute-done.7.refs_12_) | copy-start | bytes 1683460
  31.5 13.0 %collective-permute-start.9 = (bf16[2192,128]{1,0:T(8,128)(2,1)S(1)}, bf16[2192,128]{1,0:T(8,128)(2,1)S(1)}, u32[]{:S(2)}, u32[]{:S(2)}) collective-permute-start(bf16[2192,128]{1,0:T(8,128)(2,1)S(1)} %collective-permute-done.1.refs_6_), channel_id=1, source_target_pairs={{0,1},{1,0},{2,3},{3,2},{4,5},{5,4},{6,7},{7,6},{8,9},{9,8},{10,11... | collective-permute-start | bytes 1683464 | tf_op jit(solution)/shard_map/ppermute | solution.py:37
  31.7 20.0 %copy-start.14 = (bf16[1296,128]{1,0:T(8,128)(2,1)}, bf16[1296,128]{1,0:T(8,128)(2,1)S(1)}, u32[]{:S(2)}) copy-start(bf16[1296,128]{1,0:T(8,128)(2,1)S(1)} %collective-permute-done.17.refs_23_) | copy-start | bytes 995332
  31.7 12.9 %collective-permute-start.5 = (bf16[2192,128]{1,0:T(8,128)(2,1)S(1)}, bf16[2192,128]{1,0:T(8,128)(2,1)S(1)}, u32[]{:S(2)}, u32[]{:S(2)}) collective-permute-start(bf16[2192,128]{1,0:T(8,128)(2,1)S(1)} %collective-permute-done.3.refs_8_), channel_id=1, source_target_pairs={{0,12},{1,13},{2,14},{3,15},{4,0},{5,1},{6,2},{7,3},{8,4},{9,5},{1... | collective-permute-start | bytes 1683464 | tf_op jit(solution)/shard_map/ppermute | solution.py:37
  35.2 12.7 %collective-permute-start.4 = (bf16[2192,128]{1,0:T(8,128)(2,1)S(1)}, bf16[2192,128]{1,0:T(8,128)(2,1)S(1)}, u32[]{:S(2)}, u32[]{:S(2)}) collective-permute-start(bf16[2192,128]{1,0:T(8,128)(2,1)S(1)} %collective-permute-done.3.refs_8_), channel_id=1, source_target_pairs={{0,4},{1,5},{2,6},{3,7},{4,8},{5,9},{6,10},{7,11},{8,12},{9,13},{1... | collective-permute-start | bytes 1683464 | tf_op jit(solution)/shard_map/ppermute | solution.py:37
  36.4 15.2 %collective-permute-start.6 = (bf16[2192,128]{1,0:T(8,128)(2,1)}, bf16[2192,128]{1,0:T(8,128)(2,1)S(1)}, u32[]{:S(2)}, u32[]{:S(2)}) collective-permute-start(bf16[2192,128]{1,0:T(8,128)(2,1)} %collective-permute-done.2.refs_7_), channel_id=1, source_target_pairs={{0,2},{1,3},{2,0},{3,1},{4,6},{5,7},{6,4},{7,5},{8,10},{9,11},{10,... | collective-permute-start | bytes 1683464 | tf_op jit(solution)/shard_map/ppermute | solution.py:37
  38.9 14.6 %collective-permute-start.8 = (bf16[2192,128]{1,0:T(8,128)(2,1)}, bf16[2192,128]{1,0:T(8,128)(2,1)}, u32[]{:S(2)}, u32[]{:S(2)}) collective-permute-start(bf16[2192,128]{1,0:T(8,128)(2,1)} %collective-permute-done.refs_5_), channel_id=1, source_target_pairs={{0,1},{1,0},{2,3},{3,2},{4,5},{5,4},{6,7},{7,6},{8,9},{9,8},{10,11... | collective-permute-start | bytes 1683464 | tf_op jit(solution)/shard_map/ppermute | solution.py:37
  44.4 9.1 %collective-permute-start.10 = (bf16[2192,128]{1,0:T(8,128)(2,1)}, bf16[2192,128]{1,0:T(8,128)(2,1)}, u32[]{:S(2)}, u32[]{:S(2)}) collective-permute-start(bf16[2192,128]{1,0:T(8,128)(2,1)} %collective-permute-done.2.refs_7_), channel_id=1, source_target_pairs={{0,1},{1,0},{2,3},{3,2},{4,5},{5,4},{6,7},{7,6},{8,9},{9,8},{10,11... | collective-permute-start | bytes 1683464 | tf_op jit(solution)/shard_map/ppermute | solution.py:37
  44.5 9.0 %collective-permute-start.13 = (bf16[2192,128]{1,0:T(8,128)(2,1)S(1)}, bf16[2192,128]{1,0:T(8,128)(2,1)S(1)}, u32[]{:S(2)}, u32[]{:S(2)}) collective-permute-start(bf16[2192,128]{1,0:T(8,128)(2,1)S(1)} %collective-permute-done.5.refs_10_), channel_id=1, source_target_pairs={{0,1},{1,0},{2,3},{3,2},{4,5},{5,4},{6,7},{7,6},{8,9},{9,8},{10,11... | collective-permute-start | bytes 1683464 | tf_op jit(solution)/shard_map/ppermute | solution.py:37
  47.9 5.6 %collective-permute-start.12 = (bf16[2192,128]{1,0:T(8,128)(2,1)S(1)}, bf16[2192,128]{1,0:T(8,128)(2,1)S(1)}, u32[]{:S(2)}, u32[]{:S(2)}) collective-permute-start(bf16[2192,128]{1,0:T(8,128)(2,1)S(1)} %collective-permute-done.4.refs_9_), channel_id=1, source_target_pairs={{0,1},{1,0},{2,3},{3,2},{4,5},{5,4},{6,7},{7,6},{8,9},{9,8},{10,11... | collective-permute-start | bytes 1683464 | tf_op jit(solution)/shard_map/ppermute | solution.py:37
  51.7 3.3 %collective-permute-start.14 = (bf16[2192,128]{1,0:T(8,128)(2,1)S(1)}, bf16[2192,128]{1,0:T(8,128)(2,1)S(1)}, u32[]{:S(2)}, u32[]{:S(2)}) collective-permute-start(bf16[2192,128]{1,0:T(8,128)(2,1)S(1)} %collective-permute-done.6.refs_11_), channel_id=1, source_target_pairs={{0,1},{1,0},{2,3},{3,2},{4,5},{5,4},{6,7},{7,6},{8,9},{9,8},{10,11... | collective-permute-start | bytes 1683464 | tf_op jit(solution)/shard_map/ppermute | solution.py:37
  (7 other events, 101.0 us)

commit v7 on v5

--- a/solution.py
+++ b/solution.py
@@ -24,7 +24,7 @@
 A_BLOCK = A_ROWS + LABEL
 B_BLOCK = B_ROWS + LABEL
 LIST = 640
-LAST = (5, 6, 7, 13, 14, 15)
+LAST = (3, 5, 6, 7, 11, 13, 14, 15)
 GROUP = 32
 
 

time: 64.1 us -> 63.9 us (level)
  no operation moved by 1% of the time
where the time goes in v7:
time: 63.9 us; the launch traced here: 63.7 us
  starting transfers between devices  43.9 us (69%)
  Pallas kernels  10.1 us (16%)
  waiting for transfers between devices  9.18 us (14%)
    ppermute x15, starting transfers between devices, col_move(): return lax.ppermute(x, 'col', pairs)  31.3 us
    pallas_call x1, Pallas kernels, per_device(): pl.pallas_call(kernel, out_shape=jax.ShapeDtypeStruct((RL * CL, TILE, TIL...  8.85 us
    ppermute x5, starting transfers between devices, row_move(): return lax.ppermute(x, 'row', pairs)  8.19 us
    ppermute x15, waiting for transfers between devices, col_move(): return lax.ppermute(x, 'col', pairs)  5.36 us
    ppermute x2, starting transfers between devices, row_move_by_core(): return lax.ppermute(x, ('row', 'col'), pairs)  4.49 us
    ppermute x5, waiting for transfers between devices, row_move(): return lax.ppermute(x, 'row', pairs)  3.51 us
  transfers between devices with their start and end apart: 22, of which 8 were waited for; matrix products, arithmetic and copies ran while one was open for 0% of the time, Pallas kernels for 0%

profile of v7, /device:TPU:1, one launch (start us, length us, event | category | flops | bytes accessed | tf_op | source)
XLA Modules:
  0.0 63.7 jit_solution(14707415251192390412)
XLA Ops:
  0.0 1.2 %shard_map.73 = (bf16[2192,128]{1,0:T(8,128)(2,1)S(1)}, bf16[1296,128]{1,0:T(8,128)(2,1)S(1)}) custom-call(bf16[2176,128]{1,0:T(8,128)(2,1)} %bitcast.7, s32[2,17]{1,0:T(2,128)} %bitcast.9, bf16[1280,128]{1,0:T(8,128)(2,1)} %bitcast.8, s32[2,10]{1,0:T(2,128)} %bitcast.10), custom_call_target="tpu_custom_call" | custom-call | tf_op jit(solution)/shard_map/pallas_call | solution.py:68
  1.2 2.5 %collective-permute-start.18 = (bf16[1296,128]{1,0:T(8,128)(2,1)S(1)}, bf16[1296,128]{1,0:T(8,128)(2,1)S(1)}, u32[]{:S(2)}, u32[]{:S(2)}) collective-permute-start(bf16[1296,128]{1,0:T(8,128)(2,1)S(1)} %get-tuple-element.13.refs_20_), channel_id=1, source_target_pairs={{0,64},{16,80},{32,96},{48,112},{64,0},{80,16},{96,32},{112,48},{1... | collective-permute-start | bytes 995336 | tf_op jit(solution)/shard_map/ppermute | solution.py:45
  3.8 2.5 %collective-permute-start.16 = (bf16[1296,128]{1,0:T(8,128)(2,1)S(1)}, bf16[1296,128]{1,0:T(8,128)(2,1)S(1)}, u32[]{:S(2)}, u32[]{:S(2)}) collective-permute-start(bf16[1296,128]{1,0:T(8,128)(2,1)S(1)} %get-tuple-element.13.refs_20_), channel_id=1, source_target_pairs={{0,48},{16,0},{32,16},{48,32},{64,112},{80,64},{96,80},{112,96},{1... | collective-permute-start | bytes 995336 | tf_op jit(solution)/shard_map/ppermute | solution.py:45
  6.3 2.7 %collective-permute-start.1 = (bf16[2192,128]{1,0:T(8,128)(2,1)S(1)}, bf16[2192,128]{1,0:T(8,128)(2,1)S(1)}, u32[]{:S(2)}, u32[]{:S(2)}) collective-permute-start(bf16[2192,128]{1,0:T(8,128)(2,1)S(1)} %get-tuple-element.11.refs_4_), channel_id=1, source_target_pairs={{0,12},{1,13},{2,14},{3,15},{4,0},{5,1},{6,2},{7,3},{8,4},{9,5},{1... | collective-permute-start | bytes 1683464 | tf_op jit(solution)/shard_map/ppermute | solution.py:37
  9.0 2.3 %collective-permute-done.18.refs_24_ = bf16[1296,128]{1,0:T(8,128)(2,1)S(1)} collective-permute-done((bf16[1296,128]{1,0:T(8,128)(2,1)S(1)}, bf16[1296,128]{1,0:T(8,128)(2,1)S(1)}, u32[]{:S(2)}, u32[]{:S(2)}) %collective-permute-start.18) | collective-permute-done | bytes 331808 | tf_op jit(solution)/shard_map/ppermute | solution.py:45
  11.3 1.3 %collective-permute-start.7 = (bf16[2192,128]{1,0:T(8,128)(2,1)S(1)}, bf16[2192,128]{1,0:T(8,128)(2,1)S(1)}, u32[]{:S(2)}, u32[]{:S(2)}) collective-permute-start(bf16[2192,128]{1,0:T(8,128)(2,1)S(1)} %get-tuple-element.11.refs_4_), channel_id=1, source_target_pairs={{0,1},{1,0},{2,3},{3,2},{4,5},{5,4},{6,7},{7,6},{8,9},{9,8},{10,11... | collective-permute-start | bytes 1683464 | tf_op jit(solution)/shard_map/ppermute | solution.py:37
  12.5 3.4 %collective-permute-start.3 = (bf16[2192,128]{1,0:T(8,128)(2,1)S(1)}, bf16[2192,128]{1,0:T(8,128)(2,1)S(1)}, u32[]{:S(2)}, u32[]{:S(2)}) collective-permute-start(bf16[2192,128]{1,0:T(8,128)(2,1)S(1)} %get-tuple-element.11.refs_4_), channel_id=1, source_target_pairs={{0,2},{1,3},{2,0},{3,1},{4,6},{5,7},{6,4},{7,5},{8,10},{9,11},{10,... | collective-permute-start | bytes 1683464 | tf_op jit(solution)/shard_map/ppermute | solution.py:37
  16.0 3.2 %collective-permute-start.20 = (bf16[1296,128]{1,0:T(8,128)(2,1)S(1)}, bf16[1296,128]{1,0:T(8,128)(2,1)S(1)}, u32[]{:S(2)}, u32[]{:S(2)}) collective-permute-start(bf16[1296,128]{1,0:T(8,128)(2,1)S(1)} %collective-permute-done.18.refs_24_), channel_id=1, source_target_pairs={{0,48},{16,0},{32,16},{48,32},{64,112},{80,64},{96,80},{112,96},{1... | collective-permute-start | bytes 995336 | tf_op jit(solution)/shard_map/ppermute | solution.py:45
  19.2 0.6 collective-permute-done.1.refs_6_
  19.8 3.2 %collective-permute-done.refs_5_ = bf16[2192,128]{1,0:T(8,128)(2,1)} collective-permute-done((bf16[2192,128]{1,0:T(8,128)(2,1)S(1)}, bf16[2192,128]{1,0:T(8,128)(2,1)}, u32[]{:S(2)}, u32[]{:S(2)}) %collective-permute-start) | collective-permute-done | bytes 561184 | tf_op jit(solution)/shard_map/ppermute | solution.py:37
  23.0 0.1 broadcast_select_fusion
  23.1 0.3 collective-permute-start.2
  23.4 0.7 %collective-permute-done.20.refs_26_ = bf16[1296,128]{1,0:T(8,128)(2,1)S(1)} collective-permute-done((bf16[1296,128]{1,0:T(8,128)(2,1)S(1)}, bf16[1296,128]{1,0:T(8,128)(2,1)S(1)}, u32[]{:S(2)}, u32[]{:S(2)}) %collective-permute-start.20) | collective-permute-done | bytes 331808 | tf_op jit(solution)/shard_map/ppermute | solution.py:45
  24.1 3.5 %collective-permute-start.17 = (bf16[1296,128]{1,0:T(8,128)(2,1)S(1)}, bf16[1296,128]{1,0:T(8,128)(2,1)S(1)}, u32[]{:S(2)}, u32[]{:S(2)}) collective-permute-start(bf16[1296,128]{1,0:T(8,128)(2,1)S(1)} %broadcast_select_fusion.2), channel_id=1, source_target_pairs={{0,16},{1,49},{2,18},{3,51},{4,20},{5,53},{6,22},{7,55},{8,24},{9,... | collective-permute-start | bytes 995336 | tf_op jit(solution)/shard_map/ppermute | solution.py:54
  27.6 0.5 collective-permute-done.19.refs_25_
  28.2 1.0 %collective-permute-start.21 = (bf16[1296,128]{1,0:T(8,128)(2,1)S(1)}, bf16[1296,128]{1,0:T(8,128)(2,1)S(1)}, u32[]{:S(2)}, u32[]{:S(2)}) collective-permute-start(bf16[1296,128]{1,0:T(8,128)(2,1)S(1)} %broadcast_select_fusion.1), channel_id=1, source_target_pairs={{0,16},{1,49},{2,18},{3,51},{4,20},{5,53},{6,22},{7,55},{8,24},{9,... | collective-permute-start | bytes 995336 | tf_op jit(solution)/shard_map/ppermute | solution.py:54
  29.2 2.3 %collective-permute-start.11 = (bf16[2192,128]{1,0:T(8,128)(2,1)S(1)}, bf16[2192,128]{1,0:T(8,128)(2,1)S(1)}, u32[]{:S(2)}, u32[]{:S(2)}) collective-permute-start(bf16[2192,128]{1,0:T(8,128)(2,1)S(1)} %collective-permute-done.3.refs_8_), channel_id=1, source_target_pairs={{0,1},{1,0},{2,3},{3,2},{4,5},{5,4},{6,7},{7,6},{8,9},{9,8},{10,11... | collective-permute-start | bytes 1683464 | tf_op jit(solution)/shard_map/ppermute | solution.py:37
  31.5 0.1 collective-permute-start.9
  31.6 0.1 collective-permute-done.17.refs_23_
  31.7 3.3 %collective-permute-start.5 = (bf16[2192,128]{1,0:T(8,128)(2,1)S(1)}, bf16[2192,128]{1,0:T(8,128)(2,1)S(1)}, u32[]{:S(2)}, u32[]{:S(2)}) collective-permute-start(bf16[2192,128]{1,0:T(8,128)(2,1)S(1)} %collective-permute-done.3.refs_8_), channel_id=1, source_target_pairs={{0,12},{1,13},{2,14},{3,15},{4,0},{5,1},{6,2},{7,3},{8,4},{9,5},{1... | collective-permute-start | bytes 1683464 | tf_op jit(solution)/shard_map/ppermute | solution.py:37
  35.0 0.2 collective-permute-done.21.refs_27_
  35.2 1.2 %collective-permute-start.4 = (bf16[2192,128]{1,0:T(8,128)(2,1)S(1)}, bf16[2192,128]{1,0:T(8,128)(2,1)S(1)}, u32[]{:S(2)}, u32[]{:S(2)}) collective-permute-start(bf16[2192,128]{1,0:T(8,128)(2,1)S(1)} %collective-permute-done.3.refs_8_), channel_id=1, source_target_pairs={{0,4},{1,5},{2,6},{3,7},{4,8},{5,9},{6,10},{7,11},{8,12},{9,13},{1... | collective-permute-start | bytes 1683464 | tf_op jit(solution)/shard_map/ppermute | solution.py:37
  36.4 2.4 %collective-permute-start.6 = (bf16[2192,128]{1,0:T(8,128)(2,1)S(1)}, bf16[2192,128]{1,0:T(8,128)(2,1)S(1)}, u32[]{:S(2)}, u32[]{:S(2)}) collective-permute-start(bf16[2192,128]{1,0:T(8,128)(2,1)S(1)} %collective-permute-done.2.refs_7_), channel_id=1, source_target_pairs={{0,2},{1,3},{2,0},{3,1},{4,6},{5,7},{6,4},{7,5},{8,10},{9,11},{10,... | collective-permute-start | bytes 1683464 | tf_op jit(solution)/shard_map/ppermute | solution.py:37
  38.8 5.6 %collective-permute-start.8 = (bf16[2192,128]{1,0:T(8,128)(2,1)}, bf16[2192,128]{1,0:T(8,128)(2,1)}, u32[]{:S(2)}, u32[]{:S(2)}) collective-permute-start(bf16[2192,128]{1,0:T(8,128)(2,1)} %collective-permute-done.refs_5_), channel_id=1, source_target_pairs={{0,1},{1,0},{2,3},{3,2},{4,5},{5,4},{6,7},{7,6},{8,9},{9,8},{10,11... | collective-permute-start | bytes 1683464 | tf_op jit(solution)/shard_map/ppermute | solution.py:37
  44.4 0.1 collective-permute-start.10
  44.5 3.4 %collective-permute-start.13 = (bf16[2192,128]{1,0:T(8,128)(2,1)S(1)}, bf16[2192,128]{1,0:T(8,128)(2,1)S(1)}, u32[]{:S(2)}, u32[]{:S(2)}) collective-permute-start(bf16[2192,128]{1,0:T(8,128)(2,1)S(1)} %collective-permute-done.5.refs_10_), channel_id=1, source_target_pairs={{0,1},{1,0},{2,3},{3,2},{4,5},{5,4},{6,7},{7,6},{8,9},{9,8},{10,11... | collective-permute-start | bytes 1683464 | tf_op jit(solution)/shard_map/ppermute | solution.py:37
  47.9 3.7 %collective-permute-start.12 = (bf16[2192,128]{1,0:T(8,128)(2,1)S(1)}, bf16[2192,128]{1,0:T(8,128)(2,1)}, u32[]{:S(2)}, u32[]{:S(2)}) collective-permute-start(bf16[2192,128]{1,0:T(8,128)(2,1)S(1)} %collective-permute-done.4.refs_9_), channel_id=1, source_target_pairs={{0,1},{1,0},{2,3},{3,2},{4,5},{5,4},{6,7},{7,6},{8,9},{9,8},{10,11... | collective-permute-start | bytes 1683464 | tf_op jit(solution)/shard_map/ppermute | solution.py:37
  51.7 1.5 %collective-permute-start.14 = (bf16[2192,128]{1,0:T(8,128)(2,1)S(1)}, bf16[2192,128]{1,0:T(8,128)(2,1)}, u32[]{:S(2)}, u32[]{:S(2)}) collective-permute-start(bf16[2192,128]{1,0:T(8,128)(2,1)S(1)} %collective-permute-done.6.refs_11_), channel_id=1, source_target_pairs={{0,1},{1,0},{2,3},{3,2},{4,5},{5,4},{6,7},{7,6},{8,9},{9,8},{10,11... | collective-permute-start | bytes 1683464 | tf_op jit(solution)/shard_map/ppermute | solution.py:37
  53.2 0.1 copy.8.refs_3_
  53.3 0.1 pad_add_fusion.refs_0_
  53.4 1.5 %collective-permute-done.14.refs_19_ = bf16[2192,128]{1,0:T(8,128)(2,1)} collective-permute-done((bf16[2192,128]{1,0:T(8,128)(2,1)S(1)}, bf16[2192,128]{1,0:T(8,128)(2,1)}, u32[]{:S(2)}, u32[]{:S(2)}) %collective-permute-start.14) | collective-permute-done | bytes 561184 | tf_op jit(solution)/shard_map/ppermute | solution.py:37
  54.9 8.9 %shard_map.74 = bf16[48,128,128]{2,1,0:T(8,128)(2,1)} custom-call(s32[2]{0:T(128)S(1)} %pad_add_fusion.refs_0_, s32[64]{0:T(128)S(1)} %copy-done.2, s32[96]{0:T(128)S(1)} %copy-done.3, s32[24,2]{1,0:T(8,128)S(1)} %copy.8.refs_3_, bf16[2192,128]{1,0:T(8,128)(2,1)} %copy-done, bf16[2192,128]{1,0:T(8,128)(2,1)} %collective-permute-done.refs_5_, ...), custom_call_target="tpu_custom_call" | custom-call | flops 3000000000 | bytes 14000000 | tf_op jit(solution)/shard_map/pallas_call | solution.py:327
  (54 shorter events, 0.2 us)
Async XLA Ops:
  1.2 21.9 %copy-start.1 = (bf16[1296,128]{1,0:T(8,128)(2,1)}, bf16[1296,128]{1,0:T(8,128)(2,1)S(1)}, u32[]{:S(2)}) copy-start(bf16[1296,128]{1,0:T(8,128)(2,1)S(1)} %get-tuple-element.13.refs_20_) | copy-start | bytes 995332
  1.2 26.9 %copy-start = (bf16[2192,128]{1,0:T(8,128)(2,1)}, bf16[2192,128]{1,0:T(8,128)(2,1)S(1)}, u32[]{:S(2)}) copy-start(bf16[2192,128]{1,0:T(8,128)(2,1)S(1)} %get-tuple-element.11.refs_4_) | copy-start | bytes 1683460
  1.2 10.0 %collective-permute-start.18 = (bf16[1296,128]{1,0:T(8,128)(2,1)S(1)}, bf16[1296,128]{1,0:T(8,128)(2,1)S(1)}, u32[]{:S(2)}, u32[]{:S(2)}) collective-permute-start(bf16[1296,128]{1,0:T(8,128)(2,1)S(1)} %get-tuple-element.13.refs_20_), channel_id=1, source_target_pairs={{0,64},{16,80},{32,96},{48,112},{64,0},{80,16},{96,32},{112,48},{1... | collective-permute-start | bytes 995336 | tf_op jit(solution)/shard_map/ppermute | solution.py:45
  3.8 8.8 %collective-permute-start.16 = (bf16[1296,128]{1,0:T(8,128)(2,1)S(1)}, bf16[1296,128]{1,0:T(8,128)(2,1)S(1)}, u32[]{:S(2)}, u32[]{:S(2)}) collective-permute-start(bf16[1296,128]{1,0:T(8,128)(2,1)S(1)} %get-tuple-element.13.refs_20_), channel_id=1, source_target_pairs={{0,48},{16,0},{32,16},{48,32},{64,112},{80,64},{96,80},{112,96},{1... | collective-permute-start | bytes 995336 | tf_op jit(solution)/shard_map/ppermute | solution.py:45
  6.3 9.7 %collective-permute-start.15 = (bf16[1296,128]{1,0:T(8,128)(2,1)S(1)}, bf16[1296,128]{1,0:T(8,128)(2,1)S(1)}, u32[]{:S(2)}, u32[]{:S(2)}) collective-permute-start(bf16[1296,128]{1,0:T(8,128)(2,1)S(1)} %get-tuple-element.13.refs_20_), channel_id=1, source_target_pairs={{0,16},{16,32},{32,48},{48,0},{64,80},{80,96},{96,112},{112,64},{1... | collective-permute-start | bytes 995336 | tf_op jit(solution)/shard_map/ppermute | solution.py:45
  6.3 13.5 %collective-permute-start.1 = (bf16[2192,128]{1,0:T(8,128)(2,1)S(1)}, bf16[2192,128]{1,0:T(8,128)(2,1)S(1)}, u32[]{:S(2)}, u32[]{:S(2)}) collective-permute-start(bf16[2192,128]{1,0:T(8,128)(2,1)S(1)} %get-tuple-element.11.refs_4_), channel_id=1, source_target_pairs={{0,12},{1,13},{2,14},{3,15},{4,0},{5,1},{6,2},{7,3},{8,4},{9,5},{1... | collective-permute-start | bytes 1683464 | tf_op jit(solution)/shard_map/ppermute | solution.py:37
  9.0 14.0 %collective-permute-start = (bf16[2192,128]{1,0:T(8,128)(2,1)S(1)}, bf16[2192,128]{1,0:T(8,128)(2,1)}, u32[]{:S(2)}, u32[]{:S(2)}) collective-permute-start(bf16[2192,128]{1,0:T(8,128)(2,1)S(1)} %get-tuple-element.11.refs_4_), channel_id=1, source_target_pairs={{0,4},{1,5},{2,6},{3,7},{4,8},{5,9},{6,10},{7,11},{8,12},{9,13},{1... | collective-permute-start | bytes 1683464 | tf_op jit(solution)/shard_map/ppermute | solution.py:37
  11.3 20.2 %collective-permute-start.7 = (bf16[2192,128]{1,0:T(8,128)(2,1)S(1)}, bf16[2192,128]{1,0:T(8,128)(2,1)S(1)}, u32[]{:S(2)}, u32[]{:S(2)}) collective-permute-start(bf16[2192,128]{1,0:T(8,128)(2,1)S(1)} %get-tuple-element.11.refs_4_), channel_id=1, source_target_pairs={{0,1},{1,0},{2,3},{3,2},{4,5},{5,4},{6,7},{7,6},{8,9},{9,8},{10,11... | collective-permute-start | bytes 1683464 | tf_op jit(solution)/shard_map/ppermute | solution.py:37
  12.5 16.6 %collective-permute-start.3 = (bf16[2192,128]{1,0:T(8,128)(2,1)S(1)}, bf16[2192,128]{1,0:T(8,128)(2,1)S(1)}, u32[]{:S(2)}, u32[]{:S(2)}) collective-permute-start(bf16[2192,128]{1,0:T(8,128)(2,1)S(1)} %get-tuple-element.11.refs_4_), channel_id=1, source_target_pairs={{0,2},{1,3},{2,0},{3,1},{4,6},{5,7},{6,4},{7,5},{8,10},{9,11},{10,... | collective-permute-start | bytes 1683464 | tf_op jit(solution)/shard_map/ppermute | solution.py:37
  16.0 8.1 %collective-permute-start.20 = (bf16[1296,128]{1,0:T(8,128)(2,1)S(1)}, bf16[1296,128]{1,0:T(8,128)(2,1)S(1)}, u32[]{:S(2)}, u32[]{:S(2)}) collective-permute-start(bf16[1296,128]{1,0:T(8,128)(2,1)S(1)} %collective-permute-done.18.refs_24_), channel_id=1, source_target_pairs={{0,48},{16,0},{32,16},{48,32},{64,112},{80,64},{96,80},{112,96},{1... | collective-permute-start | bytes 995336 | tf_op jit(solution)/shard_map/ppermute | solution.py:45
  19.2 34.0 %copy-start.16 = (s32[24,2]{0,1:T(2,128)S(1)}, s32[24,2]{0,1:T(2,128)}, u32[]{:S(2)}) copy-start(s32[24,2]{0,1:T(2,128)} %param.13) | copy-start | bytes 580
  19.2 35.7 %copy-start.2 = (s32[64]{0:T(128)S(1)}, s32[64]{0:T(128)}, u32[]{:S(2)}) copy-start(s32[64]{0:T(128)} %refs_1_.1) | copy-start | bytes 772
  19.2 35.7 %copy-start.3 = (s32[96]{0:T(128)S(1)}, s32[96]{0:T(128)}, u32[]{:S(2)}) copy-start(s32[96]{0:T(128)} %refs_2_.1) | copy-start | bytes 1156
  19.8 24.7 %copy-start.4 = (bf16[2192,128]{1,0:T(8,128)(2,1)}, bf16[2192,128]{1,0:T(8,128)(2,1)S(1)}, u32[]{:S(2)}) copy-start(bf16[2192,128]{1,0:T(8,128)(2,1)S(1)} %collective-permute-done.1.refs_6_) | copy-start | bytes 1683460
  19.8 8.3 %collective-permute-start.19 = (bf16[1296,128]{1,0:T(8,128)(2,1)S(1)}, bf16[1296,128]{1,0:T(8,128)(2,1)S(1)}, u32[]{:S(2)}, u32[]{:S(2)}) collective-permute-start(bf16[1296,128]{1,0:T(8,128)(2,1)S(1)} %collective-permute-done.18.refs_24_), channel_id=1, source_target_pairs={{0,16},{16,32},{32,48},{48,0},{64,80},{80,96},{96,112},{112,64},{1... | collective-permute-start | bytes 995336 | tf_op jit(solution)/shard_map/ppermute | solution.py:45
  23.1 13.3 %collective-permute-start.2 = (bf16[2192,128]{1,0:T(8,128)(2,1)S(1)}, bf16[2192,128]{1,0:T(8,128)(2,1)S(1)}, u32[]{:S(2)}, u32[]{:S(2)}) collective-permute-start(bf16[2192,128]{1,0:T(8,128)(2,1)S(1)} %broadcast_select_fusion), channel_id=1, source_target_pairs={{0,4},{1,13},{2,6},{3,15},{4,8},{5,1},{6,10},{7,3},{8,12},{9,5},{1... | collective-permute-start | bytes 1683464 | tf_op jit(solution)/shard_map/ppermute | solution.py:37
  24.1 20.5 %copy-start.7 = (bf16[1296,128]{1,0:T(8,128)(2,1)}, bf16[1296,128]{1,0:T(8,128)(2,1)S(1)}, u32[]{:S(2)}) copy-start(bf16[1296,128]{1,0:T(8,128)(2,1)S(1)} %collective-permute-done.20.refs_26_) | copy-start | bytes 995332
  24.1 7.6 %collective-permute-start.17 = (bf16[1296,128]{1,0:T(8,128)(2,1)S(1)}, bf16[1296,128]{1,0:T(8,128)(2,1)S(1)}, u32[]{:S(2)}, u32[]{:S(2)}) collective-permute-start(bf16[1296,128]{1,0:T(8,128)(2,1)S(1)} %broadcast_select_fusion.2), channel_id=1, source_target_pairs={{0,16},{1,49},{2,18},{3,51},{4,20},{5,53},{6,22},{7,55},{8,24},{9,... | collective-permute-start | bytes 995336 | tf_op jit(solution)/shard_map/ppermute | solution.py:54
  28.2 7.0 %collective-permute-start.21 = (bf16[1296,128]{1,0:T(8,128)(2,1)S(1)}, bf16[1296,128]{1,0:T(8,128)(2,1)S(1)}, u32[]{:S(2)}, u32[]{:S(2)}) collective-permute-start(bf16[1296,128]{1,0:T(8,128)(2,1)S(1)} %broadcast_select_fusion.1), channel_id=1, source_target_pairs={{0,16},{1,49},{2,18},{3,51},{4,20},{5,53},{6,22},{7,55},{8,24},{9,... | collective-permute-start | bytes 995336 | tf_op jit(solution)/shard_map/ppermute | solution.py:54
  29.2 22.4 %copy-start.10 = (bf16[2192,128]{1,0:T(8,128)(2,1)}, bf16[2192,128]{1,0:T(8,128)(2,1)S(1)}, u32[]{:S(2)}) copy-start(bf16[2192,128]{1,0:T(8,128)(2,1)S(1)} %collective-permute-done.3.refs_8_) | copy-start | bytes 1683460
  29.2 9.6 %collective-permute-start.11 = (bf16[2192,128]{1,0:T(8,128)(2,1)S(1)}, bf16[2192,128]{1,0:T(8,128)(2,1)S(1)}, u32[]{:S(2)}, u32[]{:S(2)}) collective-permute-start(bf16[2192,128]{1,0:T(8,128)(2,1)S(1)} %collective-permute-done.3.refs_8_), channel_id=1, source_target_pairs={{0,1},{1,0},{2,3},{3,2},{4,5},{5,4},{6,7},{7,6},{8,9},{9,8},{10,11... | collective-permute-start | bytes 1683464 | tf_op jit(solution)/shard_map/ppermute | solution.py:37
  31.5 20.2 %copy-start.9 = (bf16[2192,128]{1,0:T(8,128)(2,1)}, bf16[2192,128]{1,0:T(8,128)(2,1)S(1)}, u32[]{:S(2)}) copy-start(bf16[2192,128]{1,0:T(8,128)(2,1)S(1)} %collective-permute-done.7.refs_12_) | copy-start | bytes 1683460
  31.5 13.0 %collective-permute-start.9 = (bf16[2192,128]{1,0:T(8,128)(2,1)S(1)}, bf16[2192,128]{1,0:T(8,128)(2,1)S(1)}, u32[]{:S(2)}, u32[]{:S(2)}) collective-permute-start(bf16[2192,128]{1,0:T(8,128)(2,1)S(1)} %collective-permute-done.1.refs_6_), channel_id=1, source_target_pairs={{0,1},{1,0},{2,3},{3,2},{4,5},{5,4},{6,7},{7,6},{8,9},{9,8},{10,11... | collective-permute-start | bytes 1683464 | tf_op jit(solution)/shard_map/ppermute | solution.py:37
  31.7 20.0 %copy-start.14 = (bf16[1296,128]{1,0:T(8,128)(2,1)}, bf16[1296,128]{1,0:T(8,128)(2,1)S(1)}, u32[]{:S(2)}) copy-start(bf16[1296,128]{1,0:T(8,128)(2,1)S(1)} %collective-permute-done.17.refs_23_) | copy-start | bytes 995332
  31.7 12.9 %collective-permute-start.5 = (bf16[2192,128]{1,0:T(8,128)(2,1)S(1)}, bf16[2192,128]{1,0:T(8,128)(2,1)S(1)}, u32[]{:S(2)}, u32[]{:S(2)}) collective-permute-start(bf16[2192,128]{1,0:T(8,128)(2,1)S(1)} %collective-permute-done.3.refs_8_), channel_id=1, source_target_pairs={{0,12},{1,13},{2,14},{3,15},{4,0},{5,1},{6,2},{7,3},{8,4},{9,5},{1... | collective-permute-start | bytes 1683464 | tf_op jit(solution)/shard_map/ppermute | solution.py:37
  35.2 12.7 %collective-permute-start.4 = (bf16[2192,128]{1,0:T(8,128)(2,1)S(1)}, bf16[2192,128]{1,0:T(8,128)(2,1)S(1)}, u32[]{:S(2)}, u32[]{:S(2)}) collective-permute-start(bf16[2192,128]{1,0:T(8,128)(2,1)S(1)} %collective-permute-done.3.refs_8_), channel_id=1, source_target_pairs={{0,4},{1,5},{2,6},{3,7},{4,8},{5,9},{6,10},{7,11},{8,12},{9,13},{1... | collective-permute-start | bytes 1683464 | tf_op jit(solution)/shard_map/ppermute | solution.py:37
  36.4 15.2 %collective-permute-start.6 = (bf16[2192,128]{1,0:T(8,128)(2,1)S(1)}, bf16[2192,128]{1,0:T(8,128)(2,1)S(1)}, u32[]{:S(2)}, u32[]{:S(2)}) collective-permute-start(bf16[2192,128]{1,0:T(8,128)(2,1)S(1)} %collective-permute-done.2.refs_7_), channel_id=1, source_target_pairs={{0,2},{1,3},{2,0},{3,1},{4,6},{5,7},{6,4},{7,5},{8,10},{9,11},{10,... | collective-permute-start | bytes 1683464 | tf_op jit(solution)/shard_map/ppermute | solution.py:37
  38.8 14.5 %collective-permute-start.8 = (bf16[2192,128]{1,0:T(8,128)(2,1)}, bf16[2192,128]{1,0:T(8,128)(2,1)}, u32[]{:S(2)}, u32[]{:S(2)}) collective-permute-start(bf16[2192,128]{1,0:T(8,128)(2,1)} %collective-permute-done.refs_5_), channel_id=1, source_target_pairs={{0,1},{1,0},{2,3},{3,2},{4,5},{5,4},{6,7},{7,6},{8,9},{9,8},{10,11... | collective-permute-start | bytes 1683464 | tf_op jit(solution)/shard_map/ppermute | solution.py:37
  44.4 8.9 %collective-permute-start.10 = (bf16[2192,128]{1,0:T(8,128)(2,1)S(1)}, bf16[2192,128]{1,0:T(8,128)(2,1)S(1)}, u32[]{:S(2)}, u32[]{:S(2)}) collective-permute-start(bf16[2192,128]{1,0:T(8,128)(2,1)S(1)} %collective-permute-done.2.refs_7_), channel_id=1, source_target_pairs={{0,1},{1,0},{2,3},{3,2},{4,5},{5,4},{6,7},{7,6},{8,9},{9,8},{10,11... | collective-permute-start | bytes 1683464 | tf_op jit(solution)/shard_map/ppermute | solution.py:37
  44.5 8.8 %collective-permute-start.13 = (bf16[2192,128]{1,0:T(8,128)(2,1)S(1)}, bf16[2192,128]{1,0:T(8,128)(2,1)S(1)}, u32[]{:S(2)}, u32[]{:S(2)}) collective-permute-start(bf16[2192,128]{1,0:T(8,128)(2,1)S(1)} %collective-permute-done.5.refs_10_), channel_id=1, source_target_pairs={{0,1},{1,0},{2,3},{3,2},{4,5},{5,4},{6,7},{7,6},{8,9},{9,8},{10,11... | collective-permute-start | bytes 1683464 | tf_op jit(solution)/shard_map/ppermute | solution.py:37
  47.9 5.4 %collective-permute-start.12 = (bf16[2192,128]{1,0:T(8,128)(2,1)S(1)}, bf16[2192,128]{1,0:T(8,128)(2,1)}, u32[]{:S(2)}, u32[]{:S(2)}) collective-permute-start(bf16[2192,128]{1,0:T(8,128)(2,1)S(1)} %collective-permute-done.4.refs_9_), channel_id=1, source_target_pairs={{0,1},{1,0},{2,3},{3,2},{4,5},{5,4},{6,7},{7,6},{8,9},{9,8},{10,11... | collective-permute-start | bytes 1683464 | tf_op jit(solution)/shard_map/ppermute | solution.py:37
  51.7 3.2 %collective-permute-start.14 = (bf16[2192,128]{1,0:T(8,128)(2,1)S(1)}, bf16[2192,128]{1,0:T(8,128)(2,1)}, u32[]{:S(2)}, u32[]{:S(2)}) collective-permute-start(bf16[2192,128]{1,0:T(8,128)(2,1)S(1)} %collective-permute-done.6.refs_11_), channel_id=1, source_target_pairs={{0,1},{1,0},{2,3},{3,2},{4,5},{5,4},{6,7},{7,6},{8,9},{9,8},{10,11... | collective-permute-start | bytes 1683464 | tf_op jit(solution)/shard_map/ppermute | solution.py:37
  (7 other events, 83.0 us)
